TPU v7x, 32 devices: a whole 2x2x4 slice. The times are simulated.
32 devices in a mesh: clip: 4 (over y, x), frame: 8 (over z, core).
Axes of the slice: x: 2, y: 2, z: 4, core: 2. Of those that a mesh axis runs over, the one named last changes fastest.
Arguments:
- hidden_in: bfloat16 [8, 1024, 1024], P('clip', 'frame'), may hold values from -6 to 6
- text_states: bfloat16 [8, 128, 1024], P('clip'), may hold values from -6 to 6
- out_grad: bfloat16 [8, 1024, 1024], P('clip', 'frame'), may hold values from -6 to 6
- self_qkv: bfloat16 [1024, 3, 1024], P(('clip', 'frame')), may hold values from -0.1875 to 0.1875
- self_out: bfloat16 [1024, 1024], P(('clip', 'frame')), may hold values from -1 to 1
- cross_qkv: bfloat16 [1024, 3, 1024], P(('clip', 'frame')), may hold values from -0.1875 to 0.1875
- cross_out: bfloat16 [1024, 1024], P(('clip', 'frame')), may hold values from -0.5 to 0.5
- ffn_in: bfloat16 [1024, 4096], P(('clip', 'frame')), may hold values from -0.1875 to 0.1875
- ffn_out: bfloat16 [4096, 1024], P(('clip', 'frame')), may hold values from -0.09375 to 0.09375
- ln_gain: bfloat16 [3, 1024], P(None, ('clip', 'frame')), may hold values from 0.5 to 1.5
- ln_bias: bfloat16 [3, 1024], P(None, ('clip', 'frame')), may hold values from -3 to 3
- clip_len: int32 [8], P('clip'), may hold values from 170 to 1024, as said below
- frame_mask: int32 [8, 1024], P('clip'), may hold values 0 or 1
- text_len: int32 [8], P('clip'), may hold values from 5 to 120
- text_mask: int32 [8, 128], P('clip'), may hold values 0 or 1
Outputs:
- output: bfloat16 [8, 1024, 1024], P('clip', 'frame')
- grad_hidden: bfloat16 [8, 1024, 1024], P('clip', 'frame')
- grad_text: bfloat16 [8, 128, 1024], P('clip', 'frame')
- grad_self_qkv: float32 [1024, 3, 1024], P(('clip', 'frame'))
- grad_self_out: float32 [1024, 1024], P(('clip', 'frame'))
- grad_cross_qkv: float32 [1024, 3, 1024], P(('clip', 'frame'))
- grad_cross_out: float32 [1024, 1024], P(('clip', 'frame'))
- grad_ffn_in: float32 [1024, 4096], P(('clip', 'frame'))
- grad_ffn_out: float32 [4096, 1024], P(('clip', 'frame'))
- grad_ln_gain: float32 [3, 1024], P(None, ('clip', 'frame'))
- grad_ln_bias: float32 [3, 1024], P(None, ('clip', 'frame'))
Inputs may be any that keep to these rules, and one draw needn't show every extreme that they name: `clip_len`: in every aligned group of 2 clips at least one has the full length 1024.
All inputs are finite; a program needn't handle non-finite values. No bound on the sum of `frame_mask` or of `text_mask` on one device may be relied on, other than what follows from the above.
Results may differ from a plain program's by a relative error of at most 0.019.
Values may be sent and summed in bfloat16 or wider, within the bound.
A program may use at most 320 MiB of HBM per device.

v0:
```python
import jax
import jax.numpy as jnp
from jax import lax
from jax.sharding import PartitionSpec as P

HD = 64


MASKED = -1000000000.0
EPSILON = 1e-05


def layer_norm(value, gain, shift):
    average = jnp.mean(value, axis=-1, keepdims=True)
    centered = value - average
    variance = jnp.mean(centered * centered, axis=-1, keepdims=True)
    return centered * lax.rsqrt(variance + EPSILON) * gain + shift


def activate(value):
    return jax.nn.gelu(value, approximate=False)


def project(left, right):
    return jnp.einsum("cnd,de->cne", left, right, preferred_element_type=jnp.float32)


def project_back(grad_rows, weight):
    return jnp.einsum("cne,de->cnd", grad_rows, weight, preferred_element_type=jnp.float32)


def weight_grad(left, right):
    return jnp.einsum("cnd,cne->de", left, right, preferred_element_type=jnp.float32)


def fetch_attention(self_qkv, self_out, cross_qkv, cross_out, ln_gain, ln_bias):
    return (
        lax.all_gather(self_qkv, ("clip", "frame"), axis=0, tiled=True),
        lax.all_gather(self_out, ("clip", "frame"), axis=0, tiled=True),
        lax.all_gather(cross_qkv, ("clip", "frame"), axis=0, tiled=True),
        lax.all_gather(cross_out, ("clip", "frame"), axis=0, tiled=True),
        lax.all_gather(ln_gain, ("clip", "frame"), axis=1, tiled=True),
        lax.all_gather(ln_bias, ("clip", "frame"), axis=1, tiled=True),
    )


def fetch_ffn(ffn_in, ffn_out):
    return (
        lax.all_gather(ffn_in, ("clip", "frame"), axis=0, tiled=True),
        lax.all_gather(ffn_out, ("clip", "frame"), axis=0, tiled=True),
    )


def self_masks(first_row, block_rows, clip_len, key_valid):
    columns = jnp.arange(key_valid.shape[1], dtype=jnp.int32)
    row_ids = first_row + jnp.arange(block_rows, dtype=jnp.int32)
    diagonal = columns[None, :] == row_ids[:, None]
    allowed = (columns[None, :] <= row_ids[:, None])[None] & (
        key_valid[:, None, :] | diagonal[None]
    )
    live_rows = (row_ids[None, :] < clip_len[:, None]).astype(jnp.float32)
    return (allowed[:, None], live_rows[:, None, :, None])


def self_forward(query_rows, key_rows, value_rows, clip_len, key_valid):
    length = query_rows.shape[1]
    block_rows = min(512, length)
    score_scale = query_rows.shape[3] ** (-0.5)

    def one_block(block_index):
        first_row = block_index * block_rows
        query_block = lax.dynamic_slice_in_dim(query_rows, first_row, block_rows, 1)
        raw_scores = jnp.einsum(
            "cqhd,ckhd->chqk", query_block, key_rows, preferred_element_type=jnp.float32
        )
        allowed, live_rows = self_masks(first_row, block_rows, clip_len, key_valid)
        logits = jnp.where(allowed, raw_scores * score_scale, MASKED)
        row_max = jnp.max(logits, axis=-1, keepdims=True)
        exponent = jnp.exp(logits - row_max)
        row_sum = jnp.sum(exponent, axis=-1, keepdims=True)
        weights = (exponent / row_sum * live_rows).astype(jnp.bfloat16)
        attended = jnp.einsum(
            "chqk,ckhd->cqhd", weights, value_rows, preferred_element_type=jnp.float32
        )
        return (attended.astype(jnp.bfloat16), row_max + jnp.log(row_sum))

    blocks, log_sums = lax.map(one_block, jnp.arange(length // block_rows, dtype=jnp.int32))
    return (jnp.moveaxis(blocks, 0, 1).reshape(query_rows.shape), log_sums)


def self_backward(query_rows, key_rows, value_rows, grad_rows, log_sums, clip_len, key_valid):
    length = query_rows.shape[1]
    block_rows = min(512, length)
    score_scale = query_rows.shape[3] ** (-0.5)

    def one_block(totals, block_index):
        grad_keys, grad_values = totals
        first_row = block_index * block_rows
        query_block = lax.dynamic_slice_in_dim(query_rows, first_row, block_rows, 1)
        grad_block = lax.dynamic_slice_in_dim(grad_rows, first_row, block_rows, 1)
        raw_scores = jnp.einsum(
            "cqhd,ckhd->chqk", query_block, key_rows, preferred_element_type=jnp.float32
        )
        allowed, live_rows = self_masks(first_row, block_rows, clip_len, key_valid)
        logits = jnp.where(allowed, raw_scores * score_scale, MASKED)
        probs = jnp.exp(logits - log_sums[block_index])
        weights = (probs * live_rows).astype(jnp.bfloat16)
        grad_probs = (
            jnp.einsum(
                "cqhd,ckhd->chqk", grad_block, value_rows, preferred_element_type=jnp.float32
            )
            * live_rows
        )
        row_dot = jnp.sum(probs * grad_probs, axis=-1, keepdims=True)
        grad_scores = (probs * (grad_probs - row_dot)).astype(jnp.bfloat16)
        grad_query = (
            jnp.einsum("chqk,ckhd->cqhd", grad_scores, key_rows, preferred_element_type=jnp.float32)
            * score_scale
        )
        grad_keys = (
            grad_keys
            + jnp.einsum(
                "chqk,cqhd->ckhd", grad_scores, query_block, preferred_element_type=jnp.float32
            )
            * score_scale
        )
        grad_values = grad_values + jnp.einsum(
            "chqk,cqhd->ckhd", weights, grad_block, preferred_element_type=jnp.float32
        )
        return ((grad_keys, grad_values), grad_query)

    zeros = jnp.zeros(key_rows.shape, jnp.float32)
    (grad_keys, grad_values), grad_blocks = lax.scan(
        one_block, (zeros, zeros), jnp.arange(length // block_rows, dtype=jnp.int32)
    )
    grad_query = jnp.moveaxis(grad_blocks, 0, 1).reshape(query_rows.shape)
    return (grad_query, grad_keys, grad_values)


def text_allowed(text_len, text_mask):
    slots = jnp.arange(text_mask.shape[1], dtype=jnp.int32)
    allowed = (slots[None, :] < text_len[:, None]) & ((text_mask > 0) | (slots[None, :] == 0))
    return allowed[:, None, None, :]


def cross_forward(query_rows, key_rows, value_rows, allowed):
    score_scale = query_rows.shape[3] ** (-0.5)
    raw_scores = jnp.einsum(
        "cqhd,ckhd->chqk", query_rows, key_rows, preferred_element_type=jnp.float32
    )
    logits = jnp.where(allowed, raw_scores * score_scale, MASKED)
    row_max = jnp.max(logits, axis=-1, keepdims=True)
    exponent = jnp.exp(logits - row_max)
    row_sum = jnp.sum(exponent, axis=-1, keepdims=True)
    weights = (exponent / row_sum).astype(jnp.bfloat16)
    crossed = jnp.einsum("chqk,ckhd->cqhd", weights, value_rows, preferred_element_type=jnp.float32)
    return (crossed.astype(jnp.bfloat16), row_max + jnp.log(row_sum))


def cross_backward(query_rows, key_rows, value_rows, grad_rows, log_sums, allowed):
    score_scale = query_rows.shape[3] ** (-0.5)
    raw_scores = jnp.einsum(
        "cqhd,ckhd->chqk", query_rows, key_rows, preferred_element_type=jnp.float32
    )
    logits = jnp.where(allowed, raw_scores * score_scale, MASKED)
    probs = jnp.exp(logits - log_sums)
    weights = probs.astype(jnp.bfloat16)
    grad_probs = jnp.einsum(
        "cqhd,ckhd->chqk", grad_rows, value_rows, preferred_element_type=jnp.float32
    )
    row_dot = jnp.sum(probs * grad_probs, axis=-1, keepdims=True)
    grad_scores = (probs * (grad_probs - row_dot)).astype(jnp.bfloat16)
    grad_query = (
        jnp.einsum("chqk,ckhd->cqhd", grad_scores, key_rows, preferred_element_type=jnp.float32)
        * score_scale
    )
    grad_keys = (
        jnp.einsum("chqk,cqhd->ckhd", grad_scores, query_rows, preferred_element_type=jnp.float32)
        * score_scale
    )
    grad_values = jnp.einsum(
        "chqk,cqhd->ckhd", weights, grad_rows, preferred_element_type=jnp.float32
    )
    return (grad_query, grad_keys, grad_values)


def sum_ffn(grad_ffn_in, grad_ffn_out):
    return (
        lax.psum_scatter(grad_ffn_in, ("clip", "frame"), scatter_dimension=0, tiled=True),
        lax.psum_scatter(grad_ffn_out, ("clip", "frame"), scatter_dimension=0, tiled=True),
    )


def sum_attention(
    grad_self_qkv, grad_self_out, grad_cross_qkv, grad_cross_out, grad_gains, grad_shifts
):
    return (
        lax.psum_scatter(grad_self_qkv, ("clip", "frame"), scatter_dimension=0, tiled=True),
        lax.psum_scatter(grad_self_out, ("clip", "frame"), scatter_dimension=0, tiled=True),
        lax.psum_scatter(grad_cross_qkv, ("clip", "frame"), scatter_dimension=0, tiled=True),
        lax.psum_scatter(grad_cross_out, ("clip", "frame"), scatter_dimension=0, tiled=True),
        lax.psum_scatter(grad_gains, ("clip", "frame"), scatter_dimension=1, tiled=True),
        lax.psum_scatter(grad_shifts, ("clip", "frame"), scatter_dimension=1, tiled=True),
    )


def on_device(
    hidden_in,
    text_states,
    out_grad,
    self_qkv,
    self_out,
    cross_qkv,
    cross_out,
    ffn_in,
    ffn_out,
    ln_gain,
    ln_bias,
    clip_len,
    frame_mask,
    text_len,
    text_mask,
):
    clip_count, frames, model_width = hidden_in.shape
    text_slots = text_states.shape[1]
    group_count = lax.axis_size("frame")
    columns_here = model_width // group_count
    heads_here = columns_here // HD
    length = frames * group_count
    frame_index = lax.axis_index("frame")
    full_qkv, full_out, full_cross, full_cross_out, gains_low, shifts_low = fetch_attention(
        self_qkv, self_out, cross_qkv, cross_out, ln_gain, ln_bias
    )
    gains = gains_low.astype(jnp.float32)
    shifts = shifts_low.astype(jnp.float32)
    hidden = hidden_in.astype(jnp.float32)
    first_norm, first_pull = jax.vjp(layer_norm, hidden, gains[0], shifts[0])
    first_low = first_norm.astype(jnp.bfloat16)
    query_low = project(first_low, full_qkv[:, 0]).astype(jnp.bfloat16)
    key_low = project(first_low, full_qkv[:, 1]).astype(jnp.bfloat16)
    value_low = project(first_low, full_qkv[:, 2]).astype(jnp.bfloat16)
    query_heads, key_heads, value_heads = (
        lax.all_to_all(query_low, "frame", split_axis=2, concat_axis=1, tiled=True),
        lax.all_to_all(key_low, "frame", split_axis=2, concat_axis=1, tiled=True),
        lax.all_to_all(value_low, "frame", split_axis=2, concat_axis=1, tiled=True),
    )
    head_shape = (clip_count, length, heads_here, HD)
    query_heads = query_heads.reshape(head_shape)
    key_heads = key_heads.reshape(head_shape)
    value_heads = value_heads.reshape(head_shape)
    columns = jnp.arange(length, dtype=jnp.int32)
    key_valid = (columns[None, :] < clip_len[:, None]) & (frame_mask > 0)
    attended_heads, self_sums = self_forward(
        query_heads, key_heads, value_heads, clip_len, key_valid
    )
    attended = lax.all_to_all(
        attended_heads.reshape(clip_count, length, columns_here),
        "frame",
        split_axis=1,
        concat_axis=2,
        tiled=True,
    )
    after_self = hidden + project(attended, full_out)
    second_norm, second_pull = jax.vjp(layer_norm, after_self, gains[1], shifts[1])
    second_low = second_norm.astype(jnp.bfloat16)
    cross_query = project(second_low, full_cross[:, 0]).astype(jnp.bfloat16)
    cross_query_heads = lax.all_to_all(
        cross_query, "frame", split_axis=2, concat_axis=1, tiled=True
    ).reshape(head_shape)
    key_columns = lax.dynamic_slice_in_dim(
        full_cross[:, 1], frame_index * columns_here, columns_here, 1
    )
    value_columns = lax.dynamic_slice_in_dim(
        full_cross[:, 2], frame_index * columns_here, columns_here, 1
    )
    text_shape = (clip_count, text_slots, heads_here, HD)
    text_keys = project(text_states, key_columns).astype(jnp.bfloat16).reshape(text_shape)
    text_values = project(text_states, value_columns).astype(jnp.bfloat16).reshape(text_shape)
    allowed_text = text_allowed(text_len, text_mask)
    crossed_heads, cross_sums = cross_forward(
        cross_query_heads, text_keys, text_values, allowed_text
    )
    crossed = lax.all_to_all(
        crossed_heads.reshape(clip_count, length, columns_here),
        "frame",
        split_axis=1,
        concat_axis=2,
        tiled=True,
    )
    after_cross = after_self + project(crossed, full_cross_out)
    ffn_weight_in, ffn_weight_out = fetch_ffn(ffn_in, ffn_out)
    third_norm, third_pull = jax.vjp(layer_norm, after_cross, gains[2], shifts[2])
    third_low = third_norm.astype(jnp.bfloat16)
    pre_act = project(third_low, ffn_weight_in)
    activated, gelu_pull = jax.vjp(activate, pre_act)
    inner_low = activated.astype(jnp.bfloat16)
    output = (after_cross + project(inner_low, ffn_weight_out)).astype(jnp.bfloat16)
    ffn_weight_in, ffn_weight_out = fetch_ffn(ffn_in, ffn_out)
    grad_ffn_out = weight_grad(inner_low, out_grad)
    (grad_pre,) = gelu_pull(project_back(out_grad, ffn_weight_out))
    grad_pre_low = grad_pre.astype(jnp.bfloat16)
    grad_ffn_in = weight_grad(third_low, grad_pre_low)
    ffn_sums = sum_ffn(grad_ffn_in, grad_ffn_out)
    grad_third, gain_third, shift_third = third_pull(project_back(grad_pre_low, ffn_weight_in))
    grad_after_cross = out_grad.astype(jnp.float32) + grad_third
    full_qkv, full_out, full_cross, full_cross_out, gains_low, shifts_low = fetch_attention(
        self_qkv, self_out, cross_qkv, cross_out, ln_gain, ln_bias
    )
    key_columns = lax.dynamic_slice_in_dim(
        full_cross[:, 1], frame_index * columns_here, columns_here, 1
    )
    value_columns = lax.dynamic_slice_in_dim(
        full_cross[:, 2], frame_index * columns_here, columns_here, 1
    )
    cross_branch = grad_after_cross.astype(jnp.bfloat16)
    grad_cross_out = weight_grad(crossed, cross_branch)
    grad_crossed = project_back(cross_branch, full_cross_out).astype(jnp.bfloat16)
    grad_crossed_heads = lax.all_to_all(
        grad_crossed, "frame", split_axis=2, concat_axis=1, tiled=True
    ).reshape(head_shape)
    grad_cq, grad_tk, grad_tv = cross_backward(
        cross_query_heads, text_keys, text_values, grad_crossed_heads, cross_sums, allowed_text
    )
    grad_tk_low = grad_tk.astype(jnp.bfloat16).reshape(clip_count, text_slots, columns_here)
    grad_tv_low = grad_tv.astype(jnp.bfloat16).reshape(clip_count, text_slots, columns_here)
    text_terms = project_back(grad_tk_low, key_columns) + project_back(grad_tv_low, value_columns)
    grad_text = lax.psum_scatter(
        text_terms.astype(jnp.bfloat16), "frame", scatter_dimension=1, tiled=True
    )
    empty_square = jnp.zeros((model_width, model_width), jnp.float32)
    grad_cross_key = lax.dynamic_update_slice_in_dim(
        empty_square, weight_grad(text_states, grad_tk_low), frame_index * columns_here, 1
    )
    grad_cross_value = lax.dynamic_update_slice_in_dim(
        empty_square, weight_grad(text_states, grad_tv_low), frame_index * columns_here, 1
    )
    grad_cq_low = grad_cq.astype(jnp.bfloat16).reshape(clip_count, length, columns_here)
    grad_cross_query = lax.all_to_all(grad_cq_low, "frame", split_axis=1, concat_axis=2, tiled=True)
    grad_cross_qw = weight_grad(second_low, grad_cross_query)
    grad_second, gain_second, shift_second = second_pull(
        project_back(grad_cross_query, full_cross[:, 0])
    )
    grad_after_self = grad_after_cross + grad_second
    self_branch = grad_after_self.astype(jnp.bfloat16)
    grad_self_out = weight_grad(attended, self_branch)
    grad_attended = project_back(self_branch, full_out).astype(jnp.bfloat16)
    grad_attended_heads = lax.all_to_all(
        grad_attended, "frame", split_axis=2, concat_axis=1, tiled=True
    ).reshape(head_shape)
    grad_query, grad_keys, grad_values = self_backward(
        query_heads, key_heads, value_heads, grad_attended_heads, self_sums, clip_len, key_valid
    )
    flat_shape = (clip_count, length, columns_here)
    grad_query, grad_keys, grad_values = (
        lax.all_to_all(
            grad_query.astype(jnp.bfloat16).reshape(flat_shape),
            "frame",
            split_axis=1,
            concat_axis=2,
            tiled=True,
        ),
        lax.all_to_all(
            grad_keys.astype(jnp.bfloat16).reshape(flat_shape),
            "frame",
            split_axis=1,
            concat_axis=2,
            tiled=True,
        ),
        lax.all_to_all(
            grad_values.astype(jnp.bfloat16).reshape(flat_shape),
            "frame",
            split_axis=1,
            concat_axis=2,
            tiled=True,
        ),
    )
    grad_self_qkv = jnp.stack(
        [
            weight_grad(first_low, grad_query),
            weight_grad(first_low, grad_keys),
            weight_grad(first_low, grad_values),
        ],
        axis=1,
    )
    grad_first_norm = (
        project_back(grad_query, full_qkv[:, 0])
        + project_back(grad_keys, full_qkv[:, 1])
        + project_back(grad_values, full_qkv[:, 2])
    )
    grad_first, gain_first, shift_first = first_pull(grad_first_norm)
    grad_hidden = (grad_after_self + grad_first).astype(jnp.bfloat16)
    grad_cross_qkv = jnp.stack([grad_cross_qw, grad_cross_key, grad_cross_value], axis=1)
    grad_gains = jnp.stack([gain_first, gain_second, gain_third])
    grad_shifts = jnp.stack([shift_first, shift_second, shift_third])
    attn_sums = sum_attention(
        grad_self_qkv, grad_self_out, grad_cross_qkv, grad_cross_out, grad_gains, grad_shifts
    )
    return (
        output,
        grad_hidden,
        grad_text,
        attn_sums[0],
        attn_sums[1],
        attn_sums[2],
        attn_sums[3],
        ffn_sums[0],
        ffn_sums[1],
        attn_sums[4],
        attn_sums[5],
    )


def solution(mesh):
    return jax.shard_map(
        on_device,
        mesh=mesh,
        in_specs=(
            P("clip", "frame", None),
            P("clip", None, None),
            P("clip", "frame", None),
            P(("clip", "frame"), None, None),
            P(("clip", "frame"), None),
            P(("clip", "frame"), None, None),
            P(("clip", "frame"), None),
            P(("clip", "frame"), None),
            P(("clip", "frame"), None),
            P(None, ("clip", "frame")),
            P(None, ("clip", "frame")),
            P("clip"),
            P("clip", None),
            P("clip"),
            P("clip", None),
        ),
        out_specs=(
            P("clip", "frame", None),
            P("clip", "frame", None),
            P("clip", "frame", None),
            P(("clip", "frame"), None, None),
            P(("clip", "frame"), None),
            P(("clip", "frame"), None, None),
            P(("clip", "frame"), None),
            P(("clip", "frame"), None),
            P(("clip", "frame"), None),
            P(None, ("clip", "frame")),
            P(None, ("clip", "frame")),
        ),
        check_vma=False,
    )
```

profile of v0, /device:TPU:0, one launch (start us, length us, event | category | flops | bytes accessed | tf_op | source)
XLA Modules:
  0.0 1968.1 jit_solution(16983453111743358615)
XLA Ops:
  10.6 43.7 %all-gather.1 = bf16[32,32,3]{1,2,0:T(4,128)(2,1)S(1)} all-gather(bf16[1,32,3]{1,2,0:T(4,128)(2,1)} %bitcast.452), channel_id=1, replica_groups=mesh['clip'=4,'frame'=8] {'clip','frame'}, dimensions={0}, use_global_device_ids=true | all-gather | bytes 6336 | tf_op jit(solution)/shard_map/all_gather | solution.py:43
  54.4 37.2 %all-gather = bf16[32,32,3]{1,2,0:T(4,128)(2,1)S(1)} all-gather(bf16[1,32,3]{1,2,0:T(4,128)(2,1)} %bitcast.453), channel_id=1, replica_groups=mesh['clip'=4,'frame'=8] {'clip','frame'}, dimensions={0}, use_global_device_ids=true | all-gather | bytes 6336 | tf_op jit(solution)/shard_map/all_gather | solution.py:42
  98.6 3.5 all-to-all-start
  105.6 13.2 all-to-all-done
  118.8 3.5 all-to-all-start.1
  125.8 17.6 all-to-all-done.1
  143.4 3.5 all-to-all-start.2
  152.4 11.3 all-to-all-done.2
  165.0 22.4 %while.27 = (s32[]{:T(128)}, bf16[2,2,512,2,64]{2,4,3,1,0:T(8,128)(2,1)}, f32[2,2,2,512,1]{3,2,1,4,0:T(2,128)S(1)}, s32[2]{0:T(128)S(1)}, pred[2,1024]{1,0:T(4,1...) while((s32[]{:T(128)}, ...), condition=%wide.region_5.6_spmd, body=%wide.region_2.5_spmd.sunk | while | flops 567411200 | bytes 39403816 | solution.py:87
  172.0 3.4 fusion.219
  183.2 3.4 fusion.219
  191.2 3.5 all-to-all-start.3
  194.7 28.9 %all-to-all-done.3 = bf16[2,1024,128]{2,0,1:T(2,128)(2,1)S(1)} async-done(((bf16[2,1024,128]{2,0,1:T(2,128)(2,1)}), bf16[2,1024,128]{2,0,1:T(2,128)(2,1)S(1)}, u32[]{:S(2)}, u32[]{:S(2)}) %all-to-all-start.3) | async-done | bytes 524320 | tf_op jit(solution)/shard_map/all_to_all | solution.py:256
  224.5 2.7 fusion.158
  231.1 4.0 all-to-all-start.4
  240.2 11.5 all-to-all-done.4
  258.3 21.2 %all_to_all.198 = bf16[2,1024,128]{2,0,1:T(2,128)(2,1)S(1)} all-to-all(bf16[2,1024,128]{2,0,1:T(2,128)(2,1)} %copy.199), channel_id=1, replica_groups=mesh['clip'=4,'frame'=8] {'frame'}, dimensions={1} | all-to-all | bytes 1048576 | tf_op jit(solution)/shard_map/all_to_all | solution.py:283
  282.7 5.0 all-gather.15.cloned.1.call-done
  287.7 2.8 fusion.160
  291.8 75.0 %all-gather.17.cloned.1.call-done = bf16[1024,4096]{1,0:T(8,128)(2,1)} async-done(((bf16[32,4096]{1,0:T(8,128)(2,1)}), bf16[1024,4096]{1,0:T(8,128)(2,1)}) %all-gather.17.cloned.1.call-update) | async-done | bytes 8388624 | tf_op jit(solution)/shard_map/all_gather | solution.py:49
  366.7 7.4 fusion.107
  376.2 10.8 multiply_convert_fusion.15
  387.0 58.6 %all-gather.19.cloned.1.call-done = bf16[4096,1024]{1,0:T(8,128)(2,1)} async-done(((bf16[128,1024]{1,0:T(8,128)(2,1)}), bf16[4096,1024]{1,0:T(8,128)(2,1)}) %all-gather.19.cloned.1.call-update) | async-done | bytes 8388624 | tf_op jit(solution)/shard_map/all_gather | solution.py:50
  445.6 9.5 add_convert_fusion
  455.2 6.8 multiply_reduce_fusion.2
  468.1 4.1 all-to-all-start.6
  472.2 15.3 all-to-all-done.6
  495.8 17.8 all_to_all.199
  516.8 2.7 fusion.152
  523.5 3.7 all-to-all-start.8
  527.2 15.2 all-to-all-done.8
  543.8 62.8 %while.28 = (s32[]{:T(128)}, f32[2,1024,2,64]{1,3,2,0:T(8,128)S(1)}, f32[2,1024,2,64]{1,3,2,0:T(8,128)}, bf16[2,2,512,2,64]{2,4,3,1,0:T(8,128)(2,1)}, s32[2]{0:T...) while((s32[]{:T(128)}, ...), condition=%wide.region_19.20_spmd.clone, body=%wide.region_17.19_spmd.clone.sunk | while | flops 1384514048 | bytes 133251608 | solution.py:133
  545.2 5.5 fusion.228
  554.2 6.1 multiply_reduce_fusion.9
  560.4 4.0 multiply_convert_fusion.22
  564.4 3.3 fusion.229
  567.8 5.2 fusion.230
  576.6 5.5 fusion.228
  585.6 6.1 multiply_reduce_fusion.9
  591.8 4.0 multiply_convert_fusion.22
  595.8 3.3 fusion.229
  599.2 5.2 fusion.230
  610.3 4.1 all-to-all-start.9
  617.5 12.3 all-to-all-done.9
  629.8 4.2 all-to-all-start.10
  638.0 11.3 all-to-all-done.10
  649.3 4.2 all-to-all-start.11
  663.4 5.4 all-to-all-done.11
  681.3 3.9 convolution_bitcast_fusion.2
  686.2 2.7 convolution_bitcast_fusion.4
  691.8 4.9 pad_maximum_fusion.1
  701.1 4.9 pad_maximum_fusion
  707.2 9.9 convolution_bitcast_fusion.1
  717.1 9.8 convolution_bitcast_fusion
  727.0 7.3 fusion.79
  735.5 74.2 %reduce-scatter.28.cloned.1.call-done = f32[32,3]{1,0:T(8,128)} async-done(((f32[1024,3]{1,0:T(8,128)}), f32[32,3]{1,0:T(8,128)}) %reduce-scatter.28.cloned.1.call-update) | async-done | bytes 400
  811.0 131.1 %reduce-scatter.30.cloned.1.call-done = f32[32,3]{1,0:T(8,128)} async-done(((f32[1024,3]{1,0:T(8,128)}), f32[32,3]{1,0:T(8,128)}) %reduce-scatter.30.cloned.1.call-update) | async-done | bytes 400
  943.5 29.1 %reduce-scatter.14.cloned.1.call-done = bf16[2,16,1024]{2,1,0:T(8,128)(2,1)} async-done(((bf16[2,128,1024]{2,1,0:T(8,128)(2,1)}), bf16[2,16,1024]{2,1,0:T(8,128)(2,1)}) %reduce-scatter.14.cloned.1.call-update) | async-done | bytes 65552 | tf_op jit(solution)/shard_map/reduce_scatter | solution.py:327
  972.6 143.6 %reduce-scatter.22.cloned.1.call-done = f32[32,1024]{1,0:T(8,128)} async-done(((f32[1024,1024]{1,0:T(8,128)}), f32[32,1024]{1,0:T(8,128)}) %reduce-scatter.22.cloned.1.call-update) | async-done | bytes 131088 | tf_op jit(solution)/shard_map/reduce_scatter | solution.py:201
  1116.1 142.5 %reduce-scatter.18.cloned.1.call-done = f32[32,1024]{1,0:T(8,128)} async-done(((f32[1024,1024]{1,0:T(8,128)}), f32[32,1024]{1,0:T(8,128)}) %reduce-scatter.18.cloned.1.call-update) | async-done | bytes 131088 | tf_op jit(solution)/shard_map/reduce_scatter | solution.py:199
  1258.7 163.1 %reduce-scatter.20.cloned.1.call-done = f32[32,3,1024]{2,0,1:T(8,128)} async-done(((f32[1024,3,1024]{2,0,1:T(8,128)}), f32[32,3,1024]{2,0,1:T(8,128)}) %reduce-scatter.20.cloned.1.call-update) | async-done | bytes 393232 | tf_op jit(solution)/shard_map/reduce_scatter | solution.py:200
  1421.8 164.9 %reduce-scatter.16.cloned.1.call-done = f32[32,3,1024]{2,0,1:T(8,128)} async-done(((f32[1024,3,1024]{2,0,1:T(8,128)}), f32[32,3,1024]{2,0,1:T(8,128)}) %reduce-scatter.16.cloned.1.call-update) | async-done | bytes 393232 | tf_op jit(solution)/shard_map/reduce_scatter | solution.py:198
  1586.6 187.6 %reduce-scatter.24.cloned.1.call-done = f32[32,4096]{1,0:T(8,128)} async-done(((f32[1024,4096]{1,0:T(8,128)}), f32[32,4096]{1,0:T(8,128)}) %reduce-scatter.24.cloned.1.call-update) | async-done | bytes 524304 | tf_op jit(solution)/shard_map/reduce_scatter | solution.py:189
  1774.2 187.2 %reduce-scatter.26.cloned.1.call-done = f32[128,1024]{1,0:T(8,128)} async-done(((f32[4096,1024]{1,0:T(8,128)}), f32[128,1024]{1,0:T(8,128)}) %reduce-scatter.26.cloned.1.call-update) | async-done | bytes 524304 | tf_op jit(solution)/shard_map/reduce_scatter | solution.py:190
  (340 shorter events, 142.4 us)
Async XLA Ops:
  7.2 232.1 %copy-start = (bf16[2,128,1024]{2,1,0:T(8,128)(2,1)S(1)}, bf16[2,128,1024]{2,1,0:T(8,128)(2,1)}, u32[]{:S(2)}) copy-start(bf16[2,128,1024]{2,1,0:T(8,128)(2,1)} %param.20) | copy-start | bytes 1572868
  7.2 87.7 %all-gather.9.cloned.1.call-start = ((), (), s32[]{:S(2)}) async-start(), calls=%async_computation.21 | async-start | bytes 6488064 | tf_op jit(solution)/shard_map/all_gather | solution.py:38
  7.9 216.5 %all-gather.11.cloned.1.call-start = ((), (), s32[]{:S(2)}) async-start(), calls=%async_computation.22 | async-start | bytes 2162688 | tf_op jit(solution)/shard_map/all_gather | solution.py:39
  8.7 218.9 %all-gather.13.cloned.1.call-start = ((), (), s32[]{:S(2)}) async-start(), calls=%async_computation.23 | async-start | bytes 6488064 | tf_op jit(solution)/shard_map/all_gather | solution.py:40
  9.4 278.3 %all-gather.15.cloned.1.call-start = ((), (), s32[]{:S(2)}) async-start(), calls=%async_computation.24 | async-start | bytes 2162688 | tf_op jit(solution)/shard_map/all_gather | solution.py:41
  10.0 356.7 %all-gather.17.cloned.1.call-start = ((), (), s32[]{:S(2)}) async-start(), calls=%async_computation.25 | async-start | bytes 8650752 | tf_op jit(solution)/shard_map/all_gather | solution.py:49
  91.7 10.4 copy-start.7
  93.0 29.3 %copy-start.54 = (f32[2,128]{1,0:T(2,128)}, f32[2,128]{1,0:T(2,128)S(1)}, u32[]{:S(2)}) copy-start(f32[2,128]{1,0:T(2,128)S(1)} %broadcast_multiply_fusion.2) | copy-start | bytes 3076
  94.3 28.0 %copy-start.56 = (f32[2,128]{1,0:T(2,128)}, f32[2,128]{1,0:T(2,128)S(1)}, u32[]{:S(2)}) copy-start(f32[2,128]{1,0:T(2,128)S(1)} %fusion.142) | copy-start | bytes 3076
  94.9 27.4 %copy-start.51 = (f32[1,1024]{1,0:T(1,128)}, f32[1,1024]{1,0:T(1,128)S(1)}, u32[]{:S(2)}) copy-start(f32[1,1024]{1,0:T(1,128)S(1)} %get-tuple-element.241) | copy-start | bytes 12292
  94.9 132.7 %copy-start.62 = (f32[1,1024]{1,0:T(1,128)}, f32[1,1024]{1,0:T(1,128)S(1)}, u32[]{:S(2)}) copy-start(f32[1,1024]{1,0:T(1,128)S(1)} %get-tuple-element.240) | copy-start | bytes 12292
  94.9 271.8 %copy-start.47 = (f32[1,1024]{1,0:T(1,128)}, f32[1,1024]{1,0:T(1,128)S(1)}, u32[]{:S(2)}) copy-start(f32[1,1024]{1,0:T(1,128)S(1)} %get-tuple-element.239) | copy-start | bytes 12292
  94.9 27.4 %copy-start.49 = (f32[1,1024]{1,0:T(1,128)}, f32[1,1024]{1,0:T(1,128)S(1)}, u32[]{:S(2)}) copy-start(f32[1,1024]{1,0:T(1,128)S(1)} %get-tuple-element.238) | copy-start | bytes 12292
  94.9 367.1 %copy-start.45 = (f32[1,1024]{1,0:T(1,128)}, f32[1,1024]{1,0:T(1,128)S(1)}, u32[]{:S(2)}) copy-start(f32[1,1024]{1,0:T(1,128)S(1)} %get-tuple-element.236) | copy-start | bytes 12292
  98.6 20.2 %all-to-all-start = ((bf16[2,128,1024]{1,0,2:T(2,128)(2,1)}), bf16[2,128,1024]{1,0,2:T(2,128)(2,1)S(1)}, u32[]{:S(2)}, u32[]{:S(2)}) async-start(bf16[2,128,1024]{1,0,2:T(2,128)(2,1)} %copy.184), calls=%async_computation | async-start | bytes 1048576 | tf_op jit(solution)/shard_map/all_to_all | solution.py:243
  105.5 41.9 %copy-start.53 = (s32[2]{0:T(128)S(1)}, s32[2]{0:T(128)}, u32[]{:S(2)}) copy-start(s32[2]{0:T(128)} %param.30) | copy-start | bytes 28
  105.6 41.9 %copy-start.66 = (s32[2,1024]{1,0:T(2,128)S(1)}, s32[2,1024]{1,0:T(2,128)}, u32[]{:S(2)}) copy-start(s32[2,1024]{1,0:T(2,128)} %param.31) | copy-start | bytes 24580
  118.8 24.6 %all-to-all-start.1 = ((bf16[2,128,1024]{1,0,2:T(2,128)(2,1)}), bf16[2,128,1024]{1,0,2:T(2,128)(2,1)S(1)}, u32[]{:S(2)}, u32[]{:S(2)}) async-start(bf16[2,128,1024]{1,0,2:T(2,128)(2,1)} %copy.186), calls=%async_computation.1 | async-start | bytes 1048576 | tf_op jit(solution)/shard_map/all_to_all | solution.py:244
  143.4 20.3 %all-to-all-start.2 = ((bf16[2,128,1024]{1,0,2:T(2,128)(2,1)}), bf16[2,128,1024]{1,0,2:T(2,128)(2,1)S(1)}, u32[]{:S(2)}, u32[]{:S(2)}) async-start(bf16[2,128,1024]{1,0,2:T(2,128)(2,1)} %copy.188), calls=%async_computation.2 | async-start | bytes 1048576 | tf_op jit(solution)/shard_map/all_to_all | solution.py:245
  146.9 298.7 %all-gather.19.cloned.1.call-start = ((), (), s32[]{:S(2)}) async-start(), calls=%async_computation.26 | async-start | bytes 8650752 | tf_op jit(solution)/shard_map/all_gather | solution.py:50
  187.4 39.8 %copy-start.9 = (bf16[2,1024,2,64]{1,3,2,0:T(8,128)(2,1)}, bf16[2,1024,2,64]{1,3,2,0:T(8,128)(2,1)S(1)}, u32[]{:S(2)}) copy-start(bf16[2,1024,2,64]{1,3,2,0:T(8,128)(2,1)S(1)} %get-tuple-element.512) | copy-start | bytes 1572868
  191.2 32.4 %all-to-all-start.3 = ((bf16[2,1024,128]{2,0,1:T(2,128)(2,1)}), bf16[2,1024,128]{2,0,1:T(2,128)(2,1)S(1)}, u32[]{:S(2)}, u32[]{:S(2)}) async-start(bf16[2,1024,128]{2,0,1:T(2,128)(2,1)} %reshape.421), calls=%async_computation.3 | async-start | bytes 1048576 | tf_op jit(solution)/shard_map/all_to_all | solution.py:256
  227.2 10.7 copy-start.4
  227.2 7.9 copy-start.67
  227.2 7.9 copy-start.68
  231.1 20.7 %all-to-all-start.4 = ((bf16[2,128,1024]{1,0,2:T(2,128)(2,1)}), bf16[2,128,1024]{1,0,2:T(2,128)(2,1)S(1)}, u32[]{:S(2)}, u32[]{:S(2)}) async-start(bf16[2,128,1024]{1,0,2:T(2,128)(2,1)} %copy.195), calls=%async_computation.4 | async-start | bytes 1048576 | tf_op jit(solution)/shard_map/all_to_all | solution.py:267
  254.6 238.8 %copy-start.2 = (f32[2,2,1024,128]{2,3,1,0:T(8,128)}, f32[2,2,1024,128]{2,3,1,0:T(8,128)S(1)}, u32[]{:S(2)}) copy-start(f32[2,2,1024,128]{2,3,1,0:T(8,128)S(1)} %get-tuple-element.245) | copy-start | bytes 6291460
  290.5 171.5 %copy-start.58 = (f32[2,128]{1,0:T(2,128)}, f32[2,128]{1,0:T(2,128)S(1)}, u32[]{:S(2)}) copy-start(f32[2,128]{1,0:T(2,128)S(1)} %broadcast_multiply_fusion) | copy-start | bytes 3076
  291.7 170.3 %copy-start.60 = (f32[2,128]{1,0:T(2,128)}, f32[2,128]{1,0:T(2,128)S(1)}, u32[]{:S(2)}) copy-start(f32[2,128]{1,0:T(2,128)S(1)} %fusion.144) | copy-start | bytes 3076
  445.6 9.6 copy-start.12
  455.1 6.8 copy-start.32
  455.2 8.4 copy-start.24
  468.1 19.5 all-to-all-start.6
  495.0 21.8 %copy-start.5 = (f32[2,128,1024]{2,1,0:T(8,128)S(1)}, f32[2,128,1024]{2,1,0:T(8,128)}, u32[]{:S(2)}) copy-start(f32[2,128,1024]{2,1,0:T(8,128)} %copy-done.4) | copy-start | bytes 3145732
  514.7 5.4 copy-start.18
  523.5 19.0 all-to-all-start.8
  554.2 6.2 slice-start
  554.2 6.2 slice-start.1
  567.7 5.3 copy-start.1
  567.8 5.3 copy-start.43
  585.6 6.2 slice-start
  585.6 6.2 slice-start.1
  610.3 19.5 all-to-all-start.9
  615.3 42.7 %copy-start.3 = (f32[2,2,1024,128]{2,3,1,0:T(8,128)S(1)}, f32[2,2,1024,128]{2,3,1,0:T(8,128)}, u32[]{:S(2)}) copy-start(f32[2,2,1024,128]{2,3,1,0:T(8,128)} %copy-done.2) | copy-start | bytes 6291460
  615.3 42.7 %copy-start.22 = (bf16[2,1024,2,64]{1,3,2,0:T(8,128)(2,1)S(1)}, bf16[2,1024,2,64]{1,3,2,0:T(8,128)(2,1)}, u32[]{:S(2)}) copy-start(bf16[2,1024,2,64]{1,3,2,0:T(8,128)(2,1)} %reshape.386) | copy-start | bytes 1572868
  629.8 19.5 all-to-all-start.10
  649.3 19.5 all-to-all-start.11
  653.5 156.2 %reduce-scatter.28.cloned.1.call-start = ((), (), s32[]{:S(2)}) async-start(), calls=%async_computation.34 | async-start | bytes 540672
  659.7 12.8 copy-start.34
  661.0 11.5 copy-start.8
  661.0 11.5 copy-start.50
  661.0 11.5 copy-start.55
  669.9 5.3 copy-start.36
  672.5 6.5 copy-start.28
  675.2 6.0 copy-start.20
  677.9 264.3 %reduce-scatter.30.cloned.1.call-start = ((), (), s32[]{:S(2)}) async-start(), calls=%async_computation.35 | async-start | bytes 540672
  679.0 293.5 %reduce-scatter.14.cloned.1.call-start = ((), (), s32[]{:S(2)}) async-start(), calls=%async_computation.27 | async-start | bytes 589824 | tf_op jit(solution)/shard_map/reduce_scatter | solution.py:327
  681.2 434.9 %reduce-scatter.22.cloned.1.call-start = ((), (), s32[]{:S(2)}) async-start(), calls=%async_computation.31 | async-start | bytes 4325376 | tf_op jit(solution)/shard_map/reduce_scatter | solution.py:201
  685.2 573.5 %reduce-scatter.18.cloned.1.call-start = ((), (), s32[]{:S(2)}) async-start(), calls=%async_computation.29 | async-start | bytes 4325376 | tf_op jit(solution)/shard_map/reduce_scatter | solution.py:199
  688.9 732.8 %reduce-scatter.20.cloned.1.call-start = ((), (), s32[]{:S(2)}) async-start(), calls=%async_computation.30 | async-start | bytes 12976128 | tf_op jit(solution)/shard_map/reduce_scatter | solution.py:200
  696.7 889.9 %reduce-scatter.16.cloned.1.call-start = ((), (), s32[]{:S(2)}) async-start(), calls=%async_computation.28 | async-start | bytes 12976128 | tf_op jit(solution)/shard_map/reduce_scatter | solution.py:198
  706.0 1068.2 %reduce-scatter.24.cloned.1.call-start = ((), (), s32[]{:S(2)}) async-start(), calls=%async_computation.32 | async-start | bytes 17301504 | tf_op jit(solution)/shard_map/reduce_scatter | solution.py:189
  717.1 1244.3 %reduce-scatter.26.cloned.1.call-start = ((), (), s32[]{:S(2)}) async-start(), calls=%async_computation.33 | async-start | bytes 17301504 | tf_op jit(solution)/shard_map/reduce_scatter | solution.py:190
  727.0 7.3 copy-start.27
  (43 other events, 84.9 us)
Sparse Core Ops, SparseCore 0:
  11.1 71.8 all-gather.8
  86.0 58.7 all-gather.10
  147.9 79.0 all-gather.12
  229.9 57.7 all-gather.14
  290.5 76.1 all-gather.16
  369.5 75.9 all-gather.18
  678.0 131.6 reduce-scatter.27
  812.0 130.0 reduce-scatter.29
  945.0 27.5 reduce-scatter.13
  975.4 140.7 reduce-scatter.21
  1119.1 139.5 reduce-scatter.17
  1261.5 160.2 reduce-scatter.19
  1424.8 161.8 reduce-scatter.15
  1589.5 184.6 reduce-scatter.23
  1777.0 184.3 reduce-scatter.25
where the time goes:
time: 1970 us
  waiting for transfers between devices  1510 us (77%)
  matrix products  156 us (8%)
  blocking collectives  120 us (6%)
  local copies, waits for them, and re-layouts  72.8 us (4%)
  other arithmetic  49.5 us (3%)
  starting transfers between devices  39.8 us (2%)
    unnamed x17, waiting for transfers between devices  209 us
    reduce_scatter x1, waiting for transfers between devices, sum_ffn(): lax.psum_scatter(grad_ffn_in, ('clip', 'frame'), scatter_dimension=0, til...  188 us
    reduce_scatter x1, waiting for transfers between devices, sum_ffn(): lax.psum_scatter(grad_ffn_out, ('clip', 'frame'), scatter_dimension=0, ti...  187 us
    reduce_scatter x1, waiting for transfers between devices, sum_attention(): lax.psum_scatter(grad_self_qkv, ('clip', 'frame'), scatter_dimension=0, t...  165 us
    reduce_scatter x1, waiting for transfers between devices, sum_attention(): lax.psum_scatter(grad_cross_qkv, ('clip', 'frame'), scatter_dimension=0,...  163 us
    reduce_scatter x1, waiting for transfers between devices, sum_attention(): lax.psum_scatter(grad_cross_out, ('clip', 'frame'), scatter_dimension=0,...  144 us
    reduce_scatter x1, waiting for transfers between devices, sum_attention(): lax.psum_scatter(grad_self_out, ('clip', 'frame'), scatter_dimension=0, t...  143 us
    all_gather x1, waiting for transfers between devices, fetch_ffn(): lax.all_gather(ffn_in, ('clip', 'frame'), axis=0, tiled=True)  75 us
  transfers between devices with their start and end apart: 25, of which 22 were waited for; matrix products, arithmetic and copies ran while one was open for 8% of the time, Pallas kernels for 0%

commit v1 on v0

--- a/solution.py
+++ b/solution.py
@@ -1,6 +1,10 @@
+import functools
+
 import jax
 import jax.numpy as jnp
 from jax import lax
+from jax.experimental import pallas as pl
+from jax.experimental.pallas import tpu as pltpu
 from jax.sharding import PartitionSpec as P
 
 HD = 64
@@ -204,7 +208,7 @@
     )
 
 
-def on_device(
+def on_device_any(
     hidden_in,
     text_states,
     out_grad,
@@ -410,9 +414,1010 @@
     )
 
 
+MESH = pl.DeviceIdType.MESH
+HBM = pl.BlockSpec(memory_space=pl.ANY)
+VMEM = pl.BlockSpec(memory_space=pltpu.VMEM)
+SMEM = pl.BlockSpec(memory_space=pltpu.SMEM)
+NEG = -1e30
+F32 = jnp.float32
+BF16 = jnp.bfloat16
+
+
+def fits(mesh):
+    return mesh.shape["clip"] == 4 and mesh.shape["frame"] == 8
+
+
+class Here:
+    def __init__(self):
+        self.c = lax.axis_index("clip")
+        self.f = lax.axis_index("frame")
+        self.core = lax.rem(self.f, 2)
+        self.z = lax.div(self.f, 2)
+        self.pair = lax.div(self.z, 2)
+        self.role = lax.rem(self.z, 2)
+        self.group = lax.rem(self.f, 4)
+        self.cx = self.c + 1 - 2 * lax.rem(self.c, 2)
+        self.cy = lax.rem(self.c + 2, 4)
+        self.cd = 3 - self.c
+        self.sib = self.f + 1 - 2 * self.core
+        self.partner = self.f + 2 - 4 * self.role
+        self.far_gate = 2 * (2 - self.pair) + self.core
+        self.is_gate = self.role + self.pair == 1
+        self.far = [2 * (2 * (1 - self.pair) + j) + self.core for j in range(2)]
+
+    def step(self, d):
+        return lax.rem(self.f + d, 8)
+
+    def zstep(self, d):
+        return lax.rem(self.f + 2 * d, 8)
+
+
+class Wire:
+    def __init__(self, here, send_sem, recv_sem):
+        self.here, self.send_sem, self.recv_sem = here, send_sem, recv_sem
+        self.used = 0
+        self.open = []
+
+    def copy(self, src, dst, tag, c, f):
+        self.used += 1
+        return pltpu.make_async_remote_copy(
+            src_ref=src,
+            dst_ref=dst,
+            send_sem=self.send_sem.at[self.used - 1],
+            recv_sem=self.recv_sem.at[tag],
+            device_id=(c, f),
+            device_id_type=MESH,
+        )
+
+    def send(self, src, dst, tag, c, f):
+        copy = self.copy(src, dst, tag, c, f)
+        copy.start()
+        self.open.append(copy)
+
+    def arrived(self, dst, tag):
+        pltpu.make_async_remote_copy(
+            src_ref=dst,
+            dst_ref=dst,
+            send_sem=self.send_sem.at[0],
+            recv_sem=self.recv_sem.at[tag],
+            device_id=(self.here.c, self.here.sib),
+            device_id_type=MESH,
+        ).wait_recv()
+
+    def drain(self):
+        for copy in self.open:
+            copy.wait_send()
+        self.open = []
+
+
+def greet(devices):
+    barrier = pltpu.get_barrier_semaphore()
+    for device in devices:
+        pl.semaphore_signal(barrier, inc=1, device_id=device, device_id_type=MESH)
+    pl.semaphore_wait(barrier, len(devices))
+
+
+def frame_others(here):
+    return [(here.c, here.step(d)) for d in range(1, 8)]
+
+
+def clip_others(here):
+    return [(here.cx, here.f), (here.cy, here.f), (here.cd, here.f)]
+
+
+class ClipGather:
+    def __init__(self, wire, block, tag):
+        self.wire, self.block, self.tag = wire, block, tag
+
+    def begin(self):
+        h, w, b, t = self.wire.here, self.wire, self.block, self.tag
+        w.send(b(h.c, 0), b(h.c, 0), t, h.cx, h.f)
+        w.send(b(h.c, 1), b(h.c, 1), t + 2, h.cy, h.f)
+        w.send(b(h.c, 1), b(h.c, 1), t + 1, h.cx, h.f)
+        w.send(b(h.c, 0), b(h.c, 0), t + 3, h.cy, h.f)
+
+    def middle(self):
+        h, w, b, t = self.wire.here, self.wire, self.block, self.tag
+        w.arrived(b(h.cx, 0), t)
+        w.send(b(h.cx, 0), b(h.cx, 0), t + 4, h.cy, h.f)
+        w.arrived(b(h.cy, 1), t + 2)
+        w.send(b(h.cy, 1), b(h.cy, 1), t + 5, h.cx, h.f)
+
+    def near(self):
+        h, w, b, t = self.wire.here, self.wire, self.block, self.tag
+        w.arrived(b(h.cx, 1), t + 1)
+        w.arrived(b(h.cy, 0), t + 3)
+
+    def end(self):
+        h, w, b, t = self.wire.here, self.wire, self.block, self.tag
+        w.arrived(b(h.cd, 0), t + 4)
+        w.arrived(b(h.cd, 1), t + 5)
+
+
+class ClipScatter:
+    def __init__(self, wire, parts, slots, tag):
+        self.wire, self.parts, self.slots, self.tag = wire, parts, slots, tag
+
+    def begin(self):
+        h, w, p, s, t = self.wire.here, self.wire, self.parts, self.slots, self.tag
+        w.send(p(h.cd, 0), s[0], t, h.cx, h.f)
+        w.send(p(h.cd, 1), s[1], t + 1, h.cy, h.f)
+        w.send(p(h.cx, 0), s[2], t + 2, h.cx, h.f)
+        w.send(p(h.cy, 1), s[3], t + 3, h.cy, h.f)
+
+    def middle(self):
+        h, w, p, s, t = self.wire.here, self.wire, self.parts, self.slots, self.tag
+        w.arrived(s[0], t)
+        add_into(s[0], p(h.cy, 0))
+        w.send(s[0], s[4], t + 4, h.cy, h.f)
+        w.arrived(s[1], t + 1)
+        add_into(s[1], p(h.cx, 1))
+        w.send(s[1], s[5], t + 5, h.cx, h.f)
+
+    def end(self):
+        w, s, t = self.wire, self.slots, self.tag
+        for i in range(2, 6):
+            w.arrived(s[i], t + i)
+
+    def total(self, half):
+        s = self.slots
+        first, second = (s[2], s[4]) if half == 0 else (s[5], s[3])
+        own = self.parts(self.wire.here.c, half)
+        return own[...].astype(F32) + first[...].astype(F32) + second[...].astype(F32)
+
+
+def add_into(into, other):
+    into[...] = (into[...].astype(F32) + other[...].astype(F32)).astype(BF16)
+
+
+def comm_call(body, out_shape, in_specs, out_specs, scratch, copies, tags, collective_id, cost=None):
+    return pl.pallas_call(
+        body,
+        out_shape=out_shape,
+        in_specs=in_specs,
+        out_specs=out_specs,
+        scratch_shapes=list(scratch)
+        + [pltpu.SemaphoreType.DMA((copies,)), pltpu.SemaphoreType.DMA((tags,))],
+        compiler_params=pltpu.CompilerParams(
+            collective_id=collective_id, has_side_effects=True, vmem_limit_bytes=60 * 2**20
+        ),
+    )
+
+
+def shape(dims, dtype=BF16):
+    return jax.ShapeDtypeStruct(dims, dtype)
+
+
+def fetch_body(hid, w5, square, grad, fin, o_hid, o_w5, o_square, o_grad, o_fin, local, send_sem, recv_sem):
+    h = Here()
+    w = Wire(h, send_sem, recv_sem)
+    greet(frame_others(h) + clip_others(h))
+    T_HID, T_W, T_FIN, T_ZL, T_ZR = 0, 7, 14, 17, 20
+    T_WXY, T_GXY, T_SXY, T_SIB = 23, 29, 35, 59
+
+    def my_columns(f):
+        return pl.ds(pl.multiple_of(lax.rem(f, 4) * 256, 256), 256)
+
+    def my_rows(f):
+        return pl.ds(pl.multiple_of(f * 32, 32), 32)
+
+    here_copies = [
+        pltpu.make_async_copy(hid.at[h.pair], o_hid.at[h.f], local.at[0]),
+        pltpu.make_async_copy(
+            w5.at[:, :, my_columns(h.f)], o_w5.at[:, h.c, my_rows(h.f), :], local.at[1]
+        ),
+        pltpu.make_async_copy(square, o_square.at[h.c, h.f], local.at[2]),
+        pltpu.make_async_copy(grad, o_grad.at[h.c], local.at[3]),
+        pltpu.make_async_copy(
+            fin.at[:, pl.ds(pl.multiple_of(h.c * 1024, 1024), 1024)], o_fin.at[h.c], local.at[4]
+        ),
+    ]
+    w.send(hid.at[h.pair], o_hid.at[h.f], T_HID + 1, h.c, h.partner)
+    far_tag = T_HID + 2 + h.role
+    w.send(hid.at[1 - h.pair], o_hid.at[h.f], far_tag, h.c, h.far_gate)
+    w.send(hid.at[h.pair], o_hid.at[h.f], T_HID, h.c, h.sib)
+    for d in range(1, 8):
+        f = h.step(d)
+        w.send(w5.at[:, :, my_columns(f)], o_w5.at[:, h.c, my_rows(h.f), :], T_W + d - 1, h.c, f)
+    for copy in here_copies:
+        copy.start()
+    for i, (c, f) in enumerate(clip_others(h)):
+        w.send(
+            fin.at[:, pl.ds(pl.multiple_of(c * 1024, 1024), 1024)], o_fin.at[h.c], T_FIN + i, c, f
+        )
+    for copy in here_copies:
+        copy.wait()
+    def square_slot(c, f):
+        return o_square.at[c, f]
+
+    z_copies = []
+
+    def z_step(s):
+        if s > 1:
+            @pl.when(h.z - (s - 1) >= 0)
+            def _():
+                w.arrived(square_slot(h.c, h.f - 2 * (s - 1)), T_ZL + s - 2)
+
+            @pl.when(h.z + (s - 1) <= 3)
+            def _():
+                w.arrived(square_slot(h.c, h.f + 2 * (s - 1)), T_ZR + s - 2)
+
+        if s > 3:
+            return
+        right_block = h.f - 2 * (s - 1)
+        left_block = h.f + 2 * (s - 1)
+        go_right = (right_block >= 0) & (h.z <= 2)
+        go_left = (left_block <= 7) & (h.z >= 1)
+        right = w.copy(
+            square_slot(h.c, right_block), square_slot(h.c, right_block), T_ZL + s - 1, h.c, h.f + 2
+        )
+        left = w.copy(
+            square_slot(h.c, left_block), square_slot(h.c, left_block), T_ZR + s - 1, h.c, h.f - 2
+        )
+        for go, copy in ((go_right, right), (go_left, left)):
+            pl.when(go)(copy.start)
+            z_copies.append((go, copy))
+
+    z_step(1)
+    for d in range(1, 8):
+        f = lax.rem(h.f + 8 - d, 8)
+        w.arrived(o_w5.at[:, h.c, my_rows(f), :], T_W + d - 1)
+    w5_gather = ClipGather(w, lambda c, half: o_w5.at[:, c, pl.ds(128 * half, 128), :], T_WXY)
+    w5_gather.begin()
+    w.arrived(o_hid.at[h.partner], T_HID + 1)
+    w.send(o_hid.at[h.partner], o_hid.at[h.partner], T_HID + 4, h.c, h.sib)
+    forwards = []
+    for j in range(2):
+        block = o_hid.at[h.far[j]]
+        w.arrived(block, T_HID + 2 + j)
+        forward = w.copy(block, block, T_HID + 2 + j, h.c, h.partner)
+        pl.when(h.is_gate)(forward.start)
+        forwards.append(forward)
+        w.send(block, block, T_HID + 5 + j, h.c, h.sib)
+    w5_gather.middle()
+    z_step(2)
+
+    def square_gather(d):
+        f = h.zstep(d)
+        return ClipGather(
+            w,
+            lambda c, half: o_square.at[c, f, pl.ds(64 * half, 64 - 16 * half), :],
+            T_SXY + 6 * d,
+        )
+
+    gathers = [square_gather(d) for d in range(4)]
+    gathers[0].begin()
+    grad_gather = ClipGather(w, lambda c, half: o_grad.at[c, pl.ds(128 * half, 128), :], T_GXY)
+    grad_gather.begin()
+    z_step(3)
+    z_step(4)
+    for d in range(1, 4):
+        gathers[d].begin()
+    grad_gather.middle()
+    for d in range(4):
+        f = h.zstep(d)
+        w.send(square_slot(h.c, f), square_slot(h.c, f), T_SIB + 4 * d, h.c, h.sib)
+        gathers[d].middle()
+        gathers[d].near()
+        w.send(square_slot(h.cx, f), square_slot(h.cx, f), T_SIB + 4 * d + 1, h.c, h.sib)
+        w.send(square_slot(h.cy, f), square_slot(h.cy, f), T_SIB + 4 * d + 2, h.c, h.sib)
+    for d in range(4):
+        f = h.zstep(d)
+        gathers[d].end()
+        w.send(square_slot(h.cd, f), square_slot(h.cd, f), T_SIB + 4 * d + 3, h.c, h.sib)
+    w5_gather.near()
+    w5_gather.end()
+    grad_gather.near()
+    grad_gather.end()
+    for i, (c, f) in enumerate(clip_others(h)):
+        w.arrived(o_fin.at[c], T_FIN + i)
+    w.arrived(o_hid.at[h.sib], T_HID)
+    w.arrived(o_hid.at[h.partner + h.sib - h.f], T_HID + 4)
+    for j in range(2):
+        w.arrived(o_hid.at[h.far[j] + h.sib - h.f], T_HID + 5 + j)
+    for d in range(4):
+        f = h.zstep(d) + h.sib - h.f
+        for i, c in enumerate((h.c, h.cx, h.cy, h.cd)):
+            w.arrived(square_slot(c, f), T_SIB + 4 * d + i)
+    w.drain()
+    for go, copy in z_copies:
+        pl.when(go)(copy.wait_send)
+    for copy in forwards:
+        pl.when(h.is_gate)(copy.wait_send)
+
+
+def fetch(hid, w5, square, grad, fin):
+    return comm_call(
+        fetch_body,
+        (
+            shape((8, 128, 1024)),
+            shape((5, 4, 256, 256)),
+            shape((4, 8, 112, 1024)),
+            shape((4, 256, 1024)),
+            shape((4, 32, 1024)),
+        ),
+        [HBM] * 5,
+        (HBM,) * 5,
+        [pltpu.SemaphoreType.DMA((5,))],
+        96,
+        80,
+        1,
+    )(hid, w5, square, grad, fin)
+
+
+ROWS = 256
+
+
+def dot(left, right, contract):
+    return lax.dot_general(left, right, ((contract[:1], contract[1:]), ((), ())), preferred_element_type=F32)
+
+
+def mask_scores(scores, bias_ref, first, rows):
+    low = scores[first:] + bias_ref[first : first + rows, 0:1]
+    key = lax.broadcasted_iota(jnp.int32, (rows, rows), 0)
+    query = lax.broadcasted_iota(jnp.int32, (rows, rows), 1)
+    low = jnp.where(key < query, low, jnp.where(key == query, scores[first:], NEG))
+    if first == 0:
+        return low
+    return jnp.concatenate([scores[:first] + bias_ref[0:first, 0:1], low], axis=0)
+
+
+def attend_body(length, bias, q_ref, k_ref, v_ref, o_ref, lse_ref, out_t, v_t):
+    v_t[...] = v_ref[...].T
+    lane_head = lax.broadcasted_iota(jnp.int32, (ROWS, 256), 1) // HD
+    for i in range(1024 // ROWS):
+        first, n = i * ROWS, (i + 1) * ROWS
+        q = q_ref[first:n, :]
+
+        def head(j, _):
+            q_head = jnp.where(lane_head == j, q, 0) * jnp.asarray(HD**-0.5, BF16)
+            scores = mask_scores(dot(k_ref[0:n, :], q_head, (1, 1)), bias, first, ROWS)
+            top = jnp.max(scores, axis=0, keepdims=True)
+            weight = jnp.exp(scores - top)
+            total = jnp.sum(weight, axis=0, keepdims=True)
+            at = pl.ds(pl.multiple_of(j * HD, HD), HD)
+            part = dot(v_t[at, 0:n], weight.astype(BF16), (1, 0))
+            out_t[at, :] = part / total
+            lse_ref[pl.ds(j, 1), first:n] = top + jnp.log(total)
+            return 0
+
+        lax.fori_loop(0, 4, head, 0)
+        live = first + lax.broadcasted_iota(jnp.int32, (ROWS, 256), 0) < length[0]
+        o_ref[first:n, :] = jnp.where(live, out_t[...].T, 0).astype(BF16)
+
+
+def attend(length, bias, q, k, v):
+    return pl.pallas_call(
+        attend_body,
+        out_shape=(shape((1024, 256)), shape((8, 1024), F32)),
+        in_specs=[SMEM] + [VMEM] * 4,
+        out_specs=(VMEM, VMEM),
+        scratch_shapes=[pltpu.VMEM((256, ROWS), F32), pltpu.VMEM((256, 1024), BF16)],
+        compiler_params=pltpu.CompilerParams(vmem_limit_bytes=56 * 2**20),
+    )(length, bias, q, k, v)
+
+
+def attend_back_body(
+    length, bias, q_ref, k_ref, v_ref, o_ref, lse_ref, g_ref, dq_ref, dk_ref, dv_ref, dq_t, k_t, dk, dv
+):
+    k_t[...] = k_ref[...].T
+    lane_head = lax.broadcasted_iota(jnp.int32, (ROWS, 256), 1) // HD
+    dk[...] = jnp.zeros_like(dk)
+    dv[...] = jnp.zeros_like(dv)
+    for i in range(1024 // ROWS):
+        first, n = i * ROWS, (i + 1) * ROWS
+        q = q_ref[first:n, :] * jnp.asarray(HD**-0.5, BF16)
+        live = first + lax.broadcasted_iota(jnp.int32, (ROWS, 256), 0) < length[0]
+        g = jnp.where(live, g_ref[first:n, :], 0)
+        both = (g.astype(F32) * o_ref[first:n, :].astype(F32)).T
+        row_dots = jnp.concatenate(
+            [jnp.sum(both[HD * j : HD * j + HD], axis=0, keepdims=True) for j in range(4)], axis=0
+        )
+        lse = lse_ref[0:4, first:n]
+
+        def pick(rows, j):
+            at = lax.broadcasted_iota(jnp.int32, rows.shape, 0) == j
+            return jnp.sum(jnp.where(at, rows, 0), axis=0, keepdims=True)
+
+        def head(j, _):
+            q_head = jnp.where(lane_head == j, q, 0)
+            g_head = jnp.where(lane_head == j, g, 0)
+            scores = mask_scores(dot(k_ref[0:n, :], q_head, (1, 1)), bias, first, ROWS)
+            probs = jnp.exp(scores - pick(lse, j))
+            grads = dot(v_ref[0:n, :], g_head, (1, 1))
+            dlogits = (probs * (grads - pick(row_dots, j))).astype(BF16)
+            dv[0:n, :] += dot(probs.astype(BF16), g_head, (1, 0))
+            dk[0:n, :] += dot(dlogits, q_head, (1, 0))
+            at = pl.ds(pl.multiple_of(j * HD, HD), HD)
+            dq_t[at, :] = dot(k_t[at, 0:n], dlogits, (1, 0))
+            return 0
+
+        lax.fori_loop(0, 4, head, 0)
+        dq_ref[first:n, :] = (dq_t[...].T * (HD**-0.5)).astype(BF16)
+    dk_ref[...] = dk[...].astype(BF16)
+    dv_ref[...] = dv[...].astype(BF16)
+
+
+def attend_back(length, bias, q, k, v, o, lse, g):
+    return pl.pallas_call(
+        attend_back_body,
+        out_shape=(shape((1024, 256)),) * 3,
+        in_specs=[SMEM] + [VMEM] * 7,
+        out_specs=(VMEM,) * 3,
+        scratch_shapes=[
+            pltpu.VMEM((256, ROWS), F32),
+            pltpu.VMEM((256, 1024), BF16),
+            pltpu.VMEM((1024, 256), F32),
+            pltpu.VMEM((1024, 256), F32),
+        ],
+        compiler_params=pltpu.CompilerParams(vmem_limit_bytes=56 * 2**20),
+    )(length, bias, q, k, v, o, lse, g)
+
+
+def return_body(att, tkv, o_att, o_tkv, local, send_sem, recv_sem):
+    h = Here()
+    w = Wire(h, send_sem, recv_sem)
+    greet(frame_others(h))
+
+    def slot(f):
+        return o_att.at[lax.div(f, 4), :, pl.ds(pl.multiple_of(lax.rem(f, 4) * 256, 256), 256)]
+
+    def text_slot(f):
+        return o_tkv.at[lax.div(f, 4), :, :, pl.ds(pl.multiple_of(lax.rem(f, 4) * 256, 256), 256)]
+
+    for d in range(1, 8):
+        f = h.step(d)
+        w.send(att.at[f], slot(h.f), d - 1, h.c, f)
+    copies = [
+        pltpu.make_async_copy(att.at[h.f], slot(h.f), local.at[0]),
+        pltpu.make_async_copy(tkv, text_slot(h.f), local.at[1]),
+    ]
+    for copy in copies:
+        copy.start()
+    for d in range(1, 4):
+        w.send(tkv, text_slot(h.f), 7 + d, h.c, h.zstep(d))
+    w.send(tkv, text_slot(h.f), 11, h.c, h.sib)
+    for d in range(1, 4):
+        f = lax.rem(h.f + 8 - 2 * d, 8)
+        w.arrived(text_slot(f), 7 + d)
+        w.send(text_slot(f), text_slot(f), 11 + d, h.c, h.sib)
+    for d in range(1, 8):
+        w.arrived(slot(lax.rem(h.f + 8 - d, 8)), d - 1)
+    w.arrived(text_slot(h.sib), 11)
+    for d in range(1, 4):
+        w.arrived(text_slot(lax.rem(h.sib + 8 - 2 * d, 8)), 11 + d)
+    for copy in copies:
+        copy.wait()
+    w.drain()
+
+
+def give_back(att, tkv):
+    return comm_call(
+        return_body,
+        (shape((2, 128, 1024)), shape((2, 2, 128, 1024))),
+        [HBM] * 2,
+        (HBM,) * 2,
+        [pltpu.SemaphoreType.DMA((2,))],
+        16,
+        16,
+        2,
+    )(att, tkv)
+
+
+def norm_parts(value):
+    centered = value - jnp.mean(value, axis=-1, keepdims=True)
+    scale = lax.rsqrt(jnp.mean(centered * centered, axis=-1, keepdims=True) + EPSILON)
+    return centered * scale, scale
+
+
+def square_of(square, which):
+    return square[:, 32 * which : 32 * which + 32, :].reshape(1024, 1024)
+
+
+def text_probs(query, keys, bias, lane_head):
+    heads = [jnp.where(lane_head == j, query, 0) for j in range(4)]
+    stacked = jnp.concatenate(heads, axis=0)
+    scores = dot(stacked, keys, (1, 1)) + bias
+    weight = jnp.exp(scores - jnp.max(scores, axis=1, keepdims=True))
+    return weight / jnp.sum(weight, axis=1, keepdims=True), stacked
+
+
+def pick_heads(stacked, lane_head):
+    return sum(jnp.where(lane_head == j, stacked[128 * j : 128 * j + 128], 0) for j in range(4))
+
+
+def middle_body(
+    hid, att, square, tkv, text_bias, params, o_self, second_ref, query_ref, crossed_ref, o_cross, third_ref
+):
+    att_value = att[...].reshape(256, 1024)
+    after_self = hid[...].reshape(256, 1024).astype(F32) + dot(att_value, square_of(square, 0), (1, 0))
+    o_self[...] = after_self
+    xhat, _ = norm_parts(after_self)
+    second_ref[...] = (xhat * params[1:2, :] + params[4:5, :]).astype(BF16)
+    query_ref[...] = dot(second_ref[...], square_of(square, 1), (1, 0)).astype(BF16)
+    lane_head = lax.broadcasted_iota(jnp.int32, (128, 256), 1) // HD
+    for clip in range(2):
+        for group in range(4):
+            rows, columns = pl.ds(128 * clip, 128), pl.ds(256 * group, 256)
+            query = query_ref[rows, columns] * jnp.asarray(HD**-0.5, BF16)
+            probs, _ = text_probs(query, tkv[clip, 0, :, columns], text_bias[clip : clip + 1, :], lane_head)
+            part = dot(probs.astype(BF16), tkv[clip, 1, :, columns], (1, 0))
+            crossed_ref[rows, columns] = pick_heads(part, lane_head).astype(BF16)
+    after_cross = after_self + dot(crossed_ref[...], square_of(square, 2), (1, 0))
+    o_cross[...] = after_cross
+    xhat, _ = norm_parts(after_cross)
+    third_ref[...] = (xhat * params[2:3, :] + params[5:6, :]).astype(BF16)
+
+
+def middle(hid, att, square, tkv, text_bias, params):
+    rows = (256, 1024)
+    return pl.pallas_call(
+        middle_body,
+        out_shape=(shape(rows, F32), shape(rows), shape(rows), shape(rows), shape(rows, F32), shape(rows)),
+        in_specs=[VMEM] * 6,
+        out_specs=(VMEM,) * 6,
+        compiler_params=pltpu.CompilerParams(vmem_limit_bytes=56 * 2**20),
+    )(hid, att, square, tkv, text_bias, params)
+
+
+def norm_back(xhat, scale, grad, gain):
+    h = grad * gain
+    return scale * (
+        h
+        - jnp.mean(h, axis=-1, keepdims=True)
+        - xhat * jnp.mean(h * xhat, axis=-1, keepdims=True)
+    )
+
+
+def middle_back_body(
+    g_third, g_out, after_cross, after_self, second, query_ref, crossed, att, square, tkv, text_bias, params,
+    o_after_self, o_square, o_att, o_text, o_norm, g_crossed, g_query,
+):
+    def put(which, value):
+        o_square[:, 32 * which : 32 * which + 32, :] = value.astype(BF16).reshape(32, 32, 1024)
+
+    xhat, scale = norm_parts(after_cross[...])
+    grad = g_third[...]
+    o_norm[0:1, :] = jnp.sum(grad * xhat, axis=0, keepdims=True)
+    o_norm[1:2, :] = jnp.sum(grad, axis=0, keepdims=True)
+    g_after_cross = g_out[...].reshape(256, 1024).astype(F32) + norm_back(xhat, scale, grad, params[2:3, :])
+    branch = g_after_cross.astype(BF16)
+    put(2, dot(crossed[...], branch, (0, 0)))
+    g_crossed[...] = dot(branch, square_of(square, 2), (1, 1)).astype(BF16)
+    lane_head = lax.broadcasted_iota(jnp.int32, (128, 256), 1) // HD
+    for clip in range(2):
+        for group in range(4):
+            rows, columns = pl.ds(128 * clip, 128), pl.ds(256 * group, 256)
+            keys, values = tkv[clip, 0, :, columns], tkv[clip, 1, :, columns]
+            query = query_ref[rows, columns] * jnp.asarray(HD**-0.5, BF16)
+            probs, stacked = text_probs(query, keys, text_bias[clip : clip + 1, :], lane_head)
+            grads = g_crossed[rows, columns]
+            g_stacked = jnp.concatenate([jnp.where(lane_head == j, grads, 0) for j in range(4)], axis=0)
+            g_probs = dot(g_stacked, values, (1, 1))
+            row_dot = jnp.sum(probs * g_probs, axis=1, keepdims=True)
+            g_logits = (probs * (g_probs - row_dot)).astype(BF16)
+            part = dot(g_logits, keys, (1, 0))
+            g_query[rows, columns] = (pick_heads(part, lane_head) * (HD**-0.5)).astype(BF16)
+            o_text[clip, 0, :, columns] = dot(g_logits, stacked, (0, 0)).astype(BF16)
+            o_text[clip, 1, :, columns] = dot(probs.astype(BF16), g_stacked, (0, 0)).astype(BF16)
+    put(1, dot(second[...], g_query[...], (0, 0)))
+    grad = dot(g_query[...], square_of(square, 1), (1, 1))
+    xhat, scale = norm_parts(after_self[...])
+    o_norm[2:3, :] = jnp.sum(grad * xhat, axis=0, keepdims=True)
+    o_norm[3:4, :] = jnp.sum(grad, axis=0, keepdims=True)
+    g_after_self = g_after_cross + norm_back(xhat, scale, grad, params[1:2, :])
+    o_after_self[...] = g_after_self
+    branch = g_after_self.astype(BF16)
+    put(0, dot(att[...].reshape(256, 1024), branch, (0, 0)))
+    o_att[...] = dot(branch, square_of(square, 0), (1, 1)).astype(BF16).reshape(2, 128, 1024)
+
+
+def middle_back(*args):
+    return pl.pallas_call(
+        middle_back_body,
+        out_shape=(
+            shape((256, 1024), F32),
+            shape((32, 96, 1024)),
+            shape((2, 128, 1024)),
+            shape((2, 2, 128, 1024)),
+            shape((8, 1024), F32),
+        ),
+        in_specs=[VMEM] * 12,
+        out_specs=(VMEM,) * 5,
+        scratch_shapes=[pltpu.VMEM((256, 1024), BF16)] * 2,
+        compiler_params=pltpu.CompilerParams(vmem_limit_bytes=60 * 2**20),
+    )(*args)
+
+
+def clip_gather_body(block, out, local, send_sem, recv_sem):
+    h = Here()
+    w = Wire(h, send_sem, recv_sem)
+    greet(clip_others(h)[:2])
+    copy = pltpu.make_async_copy(block, out.at[h.c], local.at[0])
+    copy.start()
+    copy.wait()
+    gather = ClipGather(w, lambda c, half: out.at[c, pl.ds(128 * half, 128), :], 0)
+    gather.begin()
+    gather.middle()
+    gather.near()
+    gather.end()
+    w.drain()
+
+
+def clip_gather(block):
+    return comm_call(
+        clip_gather_body,
+        shape((4, 256, 1024)),
+        [HBM],
+        HBM,
+        [pltpu.SemaphoreType.DMA((1,))],
+        6,
+        6,
+        3,
+    )(block)
+
+
+def clip_scatter_body(first, second, o_first, o_second, slots, send_sem, recv_sem):
+    h = Here()
+    w = Wire(h, send_sem, recv_sem)
+    greet(clip_others(h)[:2])
+    scatters = []
+    for i, terms in enumerate((first, second)):
+        scatters.append(
+            ClipScatter(
+                w,
+                lambda c, half, terms=terms: terms.at[c, pl.ds(128 * half, 128), :],
+                [slots.at[i, j] for j in range(6)],
+                6 * i,
+            )
+        )
+    for one in scatters:
+        one.begin()
+    for one in scatters:
+        one.middle()
+    for one, out in zip(scatters, (o_first, o_second)):
+        one.end()
+        for half in range(2):
+            out[128 * half : 128 * half + 128, :] = one.total(half)
+    w.drain()
+
+
+def clip_scatter(first, second):
+    return comm_call(
+        clip_scatter_body,
+        (shape((256, 1024), F32),) * 2,
+        [VMEM] * 2,
+        (VMEM,) * 2,
+        [pltpu.VMEM((2, 6, 128, 1024), BF16)],
+        12,
+        12,
+        4,
+    )(first, second)
+
+
+def forth_body(g_att, text, o_att, o_text, sums, from_sib, from_z, local, send_sem, recv_sem):
+    h = Here()
+    w = Wire(h, send_sem, recv_sem)
+    greet(frame_others(h))
+
+    def columns(f):
+        return pl.ds(pl.multiple_of(lax.rem(f, 4) * 256, 256), 256)
+
+    def part(f):
+        return g_att.at[lax.div(f, 4), :, columns(f)]
+
+    def text_part(f):
+        return text.at[lax.div(f, 4), :, :, columns(f)]
+
+    for z in range(4):
+        w.send(text_part(2 * z + 1 - h.core), from_sib.at[z], 8 + z, h.c, h.sib)
+    for d in range(1, 8):
+        f = h.step(d)
+        w.send(part(f), o_att.at[h.f], d - 1, h.c, f)
+    copy = pltpu.make_async_copy(part(h.f), o_att.at[h.f], local.at[0])
+    copy.start()
+    for z in range(4):
+        w.arrived(from_sib.at[z], 8 + z)
+        mine = text_part(2 * z + h.core)
+        sums[z] = (mine[...].astype(F32) + from_sib[z].astype(F32)).astype(BF16)
+    for d in range(1, 4):
+        w.send(sums.at[lax.rem(h.z + d, 4)], from_z.at[d - 1], 11 + d, h.c, h.zstep(d))
+    for d in range(1, 4):
+        w.arrived(from_z.at[d - 1], 11 + d)
+    total = sums[h.z].astype(F32)
+    for d in range(3):
+        total = total + from_z[d].astype(F32)
+    o_text[...] = total.astype(BF16)
+    for d in range(1, 8):
+        w.arrived(o_att.at[lax.rem(h.f + 8 - d, 8)], d - 1)
+    copy.wait()
+    w.drain()
+
+
+def give_forth(g_att, text):
+    block = (2, 128, 256)
+    return comm_call(
+        forth_body,
+        (shape((8, 128, 256)), shape(block)),
+        [VMEM] * 2,
+        (VMEM,) * 2,
+        [
+            pltpu.VMEM((4,) + block, BF16),
+            pltpu.VMEM((4,) + block, BF16),
+            pltpu.VMEM((3,) + block, BF16),
+            pltpu.SemaphoreType.DMA((1,)),
+        ],
+        16,
+        16,
+        5,
+    )(g_att, text)
+
+
+def last_body(
+    first, square, cols, text, o_first, o_square, o_cols, o_norm, o_text,
+    f_sib, f_sum, f_in, s_sib, s_sum, s_slots, s_z, s_zin, c_slots, c_sum, c_in, t_in,
+    send_sem, recv_sem,
+):
+    h = Here()
+    w = Wire(h, send_sem, recv_sem)
+    greet(frame_others(h) + clip_others(h)[:2])
+    T_F, T_S, T_C, T_T = 0, 12, 24, 40
+    for z in range(4):
+        w.send(first.at[2 * z + 1 - h.core], f_sib.at[z], T_F + z, h.c, h.sib)
+    for z in range(4):
+        w.send(square.at[:, 2 * z + 1 - h.core], s_sib.at[:, z], T_S + z, h.c, h.sib)
+    cols_scatter = ClipScatter(
+        w,
+        lambda c, half: cols.at[c, pl.ds(4 * half, 4)],
+        [c_slots.at[i] for i in range(6)],
+        T_C,
+    )
+    cols_scatter.begin()
+    for d in range(1, 8):
+        f = h.step(d)
+        w.send(text.at[pl.ds(pl.multiple_of(f * 16, 16), 16), :], t_in.at[h.f], T_T + d - 1, h.c, f)
+    t_in[h.f] = text[pl.ds(pl.multiple_of(h.f * 16, 16), 16), :]
+    for z in range(4):
+        w.arrived(f_sib.at[z], T_F + z)
+        f_sum[z] = (first[2 * z + h.core].astype(F32) + f_sib[z].astype(F32)).astype(BF16)
+    other = 2 * (1 - h.pair)
+    is_end = jnp.logical_not(h.is_gate)
+    w.send(f_sum.at[lax.div(h.partner, 2)], f_in.at[0], T_F + 4, h.c, h.partner)
+    to_gate, to_far = [], []
+    for j in range(2):
+        to_gate.append(w.copy(f_sum.at[other + j], f_in.at[1 + j], T_F + 5 + j, h.c, h.partner))
+        pl.when(is_end)(to_gate[j].start)
+    for z in range(4):
+        w.arrived(s_sib.at[:, z], T_S + z)
+
+    def add_square(i, _):
+        c, z = lax.div(i, 4), lax.rem(i, 4)
+        s_sum[c, z] = (square[c, 2 * z + h.core].astype(F32) + s_sib[c, z].astype(F32)).astype(BF16)
+        return 0
+
+    lax.fori_loop(0, 16, add_square, 0)
+    square_scatter = ClipScatter(
+        w,
+        lambda c, half: s_sum.at[c, :, pl.ds(48 * half, 48), :],
+        [s_slots.at[i] for i in range(6)],
+        T_S + 4,
+    )
+    square_scatter.begin()
+    for j in range(2):
+        @pl.when(h.is_gate)
+        def _():
+            w.arrived(f_in.at[1 + j], T_F + 5 + j)
+            f_sum[other + j] = (f_sum[other + j].astype(F32) + f_in[1 + j].astype(F32)).astype(BF16)
+
+        to_far.append(w.copy(f_sum.at[other + j], f_in.at[3], T_F + 7, h.c, h.far[j]))
+        pl.when(h.is_gate)(to_far[j].start)
+    cols_scatter.middle()
+    square_scatter.middle()
+    cols_scatter.end()
+    for half in range(2):
+        c_sum[4 * half : 4 * half + 4] = cols_scatter.total(half).astype(BF16)
+    for d in range(1, 8):
+        f = h.step(d)
+        w.send(c_sum.at[f], c_in.at[h.f], T_C + 6 + d - 1, h.c, f)
+    c_in[h.f] = c_sum[h.f]
+    square_scatter.end()
+    for half in range(2):
+        s_z[:, 48 * half : 48 * half + 48, :] = square_scatter.total(half).astype(BF16)
+    for d in range(1, 4):
+        w.send(s_z.at[lax.rem(h.z + d, 4)], s_zin.at[d - 1], T_S + 10 + d - 1 if d < 3 else 47, h.c, h.zstep(d))
+    w.arrived(f_in.at[0], T_F + 4)
+    w.arrived(f_in.at[3], T_F + 7)
+    o_first[h.pair] = f_sum[h.z].astype(F32) + f_in[0].astype(F32)
+    o_first[1 - h.pair] = f_in[3].astype(F32)
+    for d in range(1, 8):
+        w.arrived(t_in.at[lax.rem(h.f + 8 - d, 8)], T_T + d - 1)
+    for p in range(2):
+        o_text[p] = sum(t_in[4 * p + q].astype(F32) for q in range(4)).astype(BF16)
+    for d in range(1, 8):
+        w.arrived(c_in.at[lax.rem(h.f + 8 - d, 8)], T_C + 6 + d - 1)
+    for q in range(4):
+        o_cols[:, 256 * q : 256 * q + 256] = c_in[q, 0:160, :].astype(F32) + c_in[4 + q, 0:160, :].astype(F32)
+    o_norm[...] = sum(c_in[f, 160:176, 0:128].astype(F32) for f in range(8))
+    for d in range(1, 4):
+        w.arrived(s_zin.at[d - 1], T_S + 10 + d - 1 if d < 3 else 47)
+    o_square[...] = s_z[h.z].astype(F32) + sum(s_zin[d].astype(F32) for d in range(3))
+    w.drain()
+    for j in range(2):
+        pl.when(is_end)(to_gate[j].wait_send)
+        pl.when(h.is_gate)(to_far[j].wait_send)
+
+
+def last_sums(first, square, cols, text):
+    def buffer(*dims):
+        return pltpu.VMEM(dims, BF16)
+
+    return comm_call(
+        last_body,
+        (
+            shape((2, 128, 1024), F32),
+            shape((96, 1024), F32),
+            shape((160, 1024), F32),
+            shape((16, 128), F32),
+            shape((2, 16, 1024)),
+        ),
+        [VMEM] * 4,
+        (VMEM,) * 5,
+        [
+            buffer(4, 128, 1024),
+            buffer(4, 128, 1024),
+            buffer(4, 128, 1024),
+            buffer(4, 4, 96, 1024),
+            buffer(4, 4, 96, 1024),
+            buffer(6, 4, 48, 1024),
+            buffer(4, 96, 1024),
+            buffer(3, 96, 1024),
+            buffer(6, 4, 176, 256),
+            buffer(8, 176, 256),
+            buffer(8, 176, 256),
+            buffer(8, 16, 1024),
+        ],
+        64,
+        48,
+        6,
+    )(first, square, cols, text)
+
+
+def matmul(left, right):
+    return jnp.dot(left, right, preferred_element_type=F32)
+
+
+def on_device_fast(
+    hidden_in,
+    text_states,
+    out_grad,
+    self_qkv,
+    self_out,
+    cross_qkv,
+    cross_out,
+    ffn_in,
+    ffn_out,
+    ln_gain,
+    ln_bias,
+    clip_len,
+    frame_mask,
+    text_len,
+    text_mask,
+):
+    frame = lax.axis_index("frame")
+    pair = frame // 4
+    w5 = jnp.concatenate([jnp.moveaxis(self_qkv, 1, 0), jnp.moveaxis(cross_qkv, 1, 0)[1:]], axis=0)
+    norms = jnp.concatenate([ln_gain, ln_bias], axis=0).reshape(1, 192)
+    square_here = jnp.concatenate(
+        [self_out, cross_qkv[:, 0], cross_out, jnp.pad(norms, ((0, 15), (0, 832)))], axis=0
+    )
+    hid_all, w_all, square_all, grad_all, fin_all = fetch(
+        hidden_in, w5, square_here, out_grad.reshape(256, 1024), ffn_in
+    )
+    square = square_all.reshape(32, 112, 1024)
+    params = square[:, 96, :192].reshape(32, 6, 32).transpose(1, 0, 2).reshape(6, 1024).astype(F32)
+    params = jnp.pad(params, ((0, 2), (0, 0)))
+    weights = w_all.reshape(5, 1024, 256)
+    ffn_w_out = lax.all_gather(ffn_out, "frame", axis=0, tiled=True)
+    ffn_w_in = (
+        lax.all_gather(fin_all, "frame", axis=0).transpose(1, 0, 2, 3).reshape(1024, 1024)
+    )
+    clip_x = hid_all.reshape(1024, 1024).astype(F32)
+    first_hat, first_scale = norm_parts(clip_x)
+    first_low = (first_hat * params[0:1] + params[3:4]).astype(BF16)
+    query, key, value = (matmul(first_low, weights[i]).astype(BF16) for i in range(3))
+    columns = jnp.arange(1024, dtype=jnp.int32)
+    my_len = lax.dynamic_slice_in_dim(clip_len, pair, 1, 0)
+    my_mask = lax.dynamic_slice_in_dim(frame_mask, pair, 1, 0)[0]
+    bias = jnp.where((columns < my_len) & (my_mask > 0), 0.0, NEG).astype(F32)
+    bias = jnp.broadcast_to(bias[:, None], (1024, 128))
+    att_heads, lse = attend(my_len, bias, query, key, value)
+    my_text = lax.dynamic_slice_in_dim(text_states, pair, 1, 0)[0]
+    text_kv = jnp.stack([matmul(my_text, weights[3]), matmul(my_text, weights[4])]).astype(BF16)
+    att, tkv = give_back(att_heads.reshape(8, 128, 256), text_kv)
+    slots = jnp.arange(128, dtype=jnp.int32)
+    text_ok = (slots[None] < text_len[:, None]) & ((text_mask > 0) | (slots[None] == 0))
+    text_bias = jnp.where(text_ok, 0.0, NEG).astype(F32)
+    after_self, second, cross_query, crossed, after_cross, third = middle(
+        hidden_in, att, square, tkv, text_bias, params
+    )
+    third_all = clip_gather(third).reshape(1024, 1024)
+    grad_tokens = grad_all.reshape(1024, 1024)
+    pre_act = matmul(third_all, ffn_w_in)
+    activated, gelu_pull = jax.vjp(activate, pre_act)
+    inner = activated.astype(BF16)
+    out_terms = matmul(inner, ffn_w_out).astype(BF16)
+    (grad_pre,) = gelu_pull(lax.dot_general(grad_tokens, ffn_w_out, (((1,), (1,)), ((), ())), preferred_element_type=F32))
+    grad_pre = grad_pre.astype(BF16)
+    third_terms = lax.dot_general(grad_pre, ffn_w_in, (((1,), (1,)), ((), ())), preferred_element_type=F32).astype(BF16)
+    out_sum, third_sum = clip_scatter(out_terms.reshape(4, 256, 1024), third_terms.reshape(4, 256, 1024))
+    output = (after_cross + out_sum).astype(BF16).reshape(2, 128, 1024)
+    g_ffn_out = lax.dot_general(inner, grad_tokens, (((0,), (0,)), ((), ())), preferred_element_type=F32).astype(BF16)
+    g_ffn_in = lax.dot_general(third_all, grad_pre, (((0,), (0,)), ((), ())), preferred_element_type=F32).astype(BF16)
+    ffn_terms = jnp.concatenate(
+        [
+            g_ffn_out.reshape(8, 128, 1024),
+            g_ffn_in.reshape(4, 8, 32, 1024).transpose(1, 0, 2, 3).reshape(8, 128, 1024),
+        ],
+        axis=1,
+    )
+    ffn_sum = lax.psum_scatter(ffn_terms, "frame", scatter_dimension=0, tiled=True)[0]
+    grad_ffn_out = ffn_sum[:128].astype(F32)
+    grad_ffn_in = lax.all_to_all(
+        ffn_sum[128:].reshape(4, 32, 1024), "clip", split_axis=0, concat_axis=2, tiled=True
+    )[0].astype(F32)
+    g_after_self, g_square, g_att, g_text, g_norms = middle_back(
+        third_sum, out_grad, after_cross, after_self, second, cross_query, crossed, att, square, tkv,
+        text_bias, params,
+    )
+    g_heads, g_tkv = give_forth(g_att, g_text)
+    g_query, g_key, g_value = attend_back(
+        my_len, bias, query, key, value, att_heads, lse, g_heads.reshape(1024, 256)
+    )
+
+    def back(grad, weight):
+        return lax.dot_general(grad, weight, (((1,), (1,)), ((), ())), preferred_element_type=F32)
+
+    def weight_term(left, grad):
+        return lax.dot_general(left, grad, (((0,), (0,)), ((), ())), preferred_element_type=F32)
+
+    g_first = back(g_query, weights[0]) + back(g_key, weights[1]) + back(g_value, weights[2])
+    gain_first = jnp.sum(g_first * first_hat, axis=0)
+    shift_first = jnp.sum(g_first, axis=0)
+    text_terms = (back(g_tkv[0], weights[3]) + back(g_tkv[1], weights[4])).astype(BF16)
+    terms = jnp.stack(
+        [weight_term(first_low, g) for g in (g_query, g_key, g_value)]
+        + [weight_term(my_text, g_tkv[i]) for i in range(2)]
+    )
+    terms = terms.astype(BF16).reshape(5, 4, 8, 32, 256).transpose(1, 2, 0, 3, 4).reshape(4, 8, 160, 256)
+    norm_terms = jnp.stack([gain_first, g_norms[2], g_norms[0], shift_first, g_norms[3], g_norms[1]])
+    norm_terms = norm_terms.astype(BF16).reshape(6, 4, 8, 32).transpose(1, 2, 0, 3)
+    norm_terms = jnp.pad(norm_terms, ((0, 0), (0, 0), (0, 10), (0, 224)))
+    cols = jnp.concatenate([terms, norm_terms], axis=2)
+    first_sum, square_sum, cols_sum, norm_sum, grad_text = last_sums(
+        g_first.astype(BF16).reshape(8, 128, 1024), g_square.reshape(4, 8, 96, 1024), cols, text_terms
+    )
+    own_hat, own_scale = norm_parts(hidden_in.astype(F32))
+    grad_hidden = (
+        g_after_self.reshape(2, 128, 1024) + norm_back(own_hat, own_scale, first_sum, params[0])
+    ).astype(BF16)
+    cols_sum = cols_sum.reshape(5, 32, 1024)
+    return (
+        output,
+        grad_hidden,
+        grad_text,
+        jnp.stack([cols_sum[0], cols_sum[1], cols_sum[2]], axis=1),
+        square_sum[0:32],
+        jnp.stack([square_sum[32:64], cols_sum[3], cols_sum[4]], axis=1),
+        square_sum[64:96],
+        grad_ffn_in,
+        grad_ffn_out,
+        norm_sum[0:3, 0:32],
+        norm_sum[3:6, 0:32],
+    )
+
 def solution(mesh):
     return jax.shard_map(
-        on_device,
+        on_device_fast if fits(mesh) else on_device_any,
         mesh=mesh,
         in_specs=(
             P("clip", "frame", None),

time: 1970 us -> 538 us (0.27)
  waiting for transfers between devices: 1510 us -> 5.5 us
  Pallas kernels: 0 us -> 407 us
  blocking collectives: 120 us -> 0 us
  matrix products: 156 us -> 49.8 us
  local copies, waits for them, and re-layouts: 72.8 us -> 26.5 us
  starting transfers between devices: 39.8 us -> 3.52 us
  other arithmetic: 49.5 us -> 24 us
    reduce_scatter x7 -> x1, waiting for transfers between devices: 1020 us -> 0.01 us  [on_device_fast(): lax.psum_scatter(ffn_terms, 'frame', scatter_dimension=0, tiled=True)[0]]
    pallas_call x0 -> x10, Pallas kernels: none -> 407 us  [the longest x1 120 us: fetch(): comm_call(fetch_body, (shape((8, 128, 1024)), shape((5, 4, 256, 256)), sh...]
    unnamed x17 -> x3, waiting for transfers between devices: 209 us -> 0.73 us
    all_gather x6 -> x2, waiting for transfers between devices: 139 us -> 0.02 us  [the longest x1 0.02 us: on_device_fast(): lax.all_gather(fin_all, 'frame', axis=0).transpose(1, 0, 2, 3)]
    all_to_all x10 -> x1, waiting for transfers between devices: 142 us -> 4.74 us  [on_device_fast(): lax.all_to_all(ffn_sum[128:].reshape(4, 32, 1024), 'clip', split_axis=0,...]
    dot_general x50 -> x21, matrix products: 156 us -> 49.8 us  [the longest x1 14.1 us: on_device_fast(): lax.dot_general(grad_tokens, ffn_w_out, (((1,), (1,)), ((), ())), preferr...]
    all_gather x2 -> x0, blocking collectives: 80.9 us -> none  [the longest x1 43.7 us: fetch_attention(): lax.all_gather(ln_bias, ('clip', 'frame'), axis=1, tiled=True)]
    all_to_all x2 -> x0, blocking collectives: 38.9 us -> none  [the longest x1 21.2 us: on_device(): lax.all_to_all(crossed_heads.reshape(clip_count, length, columns_here), '...]
  transfers between devices with their start and end apart: 25 -> 4, of which waited for: 22 -> 1; matrix products, arithmetic and copies ran while one was open for 8% -> 12% of each run, Pallas kernels for 0% -> 54%
where the time goes in v1:
time: 538 us; the launch traced here: 531 us
  Pallas kernels  407 us (76%)
  matrix products  49.8 us (9%)
  local copies, waits for them, and re-layouts  26.5 us (5%)
  other arithmetic  24 us (4%)
  between operations  14.8 us (3%)
  waiting for transfers between devices  5.5 us (1%)
    pallas_call x1, Pallas kernels, fetch(): comm_call(fetch_body, (shape((8, 128, 1024)), shape((5, 4, 256, 256)), sh...  120 us
    pallas_call x1, Pallas kernels, last_sums(): comm_call(last_body, (shape((2, 128, 1024), F32), shape((96, 1024), F32),...  83.7 us
    pallas_call x1, Pallas kernels, give_back(): comm_call(return_body, (shape((2, 128, 1024)), shape((2, 2, 128, 1024))),...  42 us
    pallas_call x1, Pallas kernels, clip_scatter(): comm_call(clip_scatter_body, (shape((256, 1024), F32),) * 2, [VMEM] * 2,...  39.9 us
    pallas_call x1, Pallas kernels, clip_gather(): comm_call(clip_gather_body, shape((4, 256, 1024)), [HBM], HBM, [pltpu.Sem...  37.3 us
    pallas_call x1, Pallas kernels, give_forth(): comm_call(forth_body, (shape((8, 128, 256)), shape(block)), [VMEM] * 2, (...  29.1 us
    pallas_call x1, Pallas kernels, middle_back(): pl.pallas_call(middle_back_body, out_shape=(shape((256, 1024), F32), shap...  16.6 us
    pallas_call x1, Pallas kernels, attend_back(): pl.pallas_call(attend_back_body, out_shape=(shape((1024, 256)),) * 3, in_...  15.4 us
  transfers between devices with their start and end apart: 4, of which 1 were waited for; matrix products, arithmetic and copies ran while one was open for 12% of the time, Pallas kernels for 54%

profile of v1, /device:TPU:0, one launch (start us, length us, event | category | flops | bytes accessed | tf_op | source)
XLA Modules:
  0.0 531.0 jit_solution(10672279010340553611)
XLA Ops:
  7.2 0.9 slice_bitcast_fusion.7
  8.1 0.9 slice.140
  9.0 0.7 pad_maximum_fusion.5
  9.8 1.7 pad_maximum_fusion.3.w5
  11.5 1.6 fusion.39.square
  13.1 119.6 %shard_map.230 = (bf16[8,128,1024]{2,1,0:T(8,128)(2,1)}, bf16[5,4,256,256]{3,2,1,0:T(8,128)(2,1)}, bf16[4,8,112,1024]{3,2,1,0:T(8,128)(2,1)}, bf16[4,256,1024]{2,1,0:T(8,128)(2,1)}, bf16[4,32,1024]{2,1,0:T(8,128)(2,1)}) custom-call(bf16[2,128,1024]{2,1,0:T(8,128)(2,1)} %hid.3, bf16[5,32,1024]{2,1,0:T(8,128)(2,1)} %pad_maximum_fusion.3.w5, ...), custom_call_target="tpu_custom_call" | custom-call | tf_op jit(solution)/shard_map/pallas_call | solution.py:730
  132.8 0.7 all-gather.4.cloned.1.call-update
  133.6 0.7 compare_reduce_fusion
  134.3 1.2 dynamic_slice.9.length
  135.6 1.9 convert_reduce_fusion
  137.5 1.0 fusion.51
  138.6 0.7 fusion.53
  139.6 0.7 multiply_reduce_fusion.1
  140.3 1.9 fusion.60
  142.3 0.8 add_convert_fusion.2
  143.1 1.5 convolution_convert_fusion.7.v_ref
  144.6 1.5 convolution_convert_fusion.8.k_ref
  146.1 1.5 convolution_convert_fusion.9.q_ref
  147.6 1.0 broadcast_in_dim.20.bias
  148.6 13.6 %shard_map.231 = (bf16[1024,256]{1,0:T(8,128)(2,1)}, f32[8,1024]{1,0:T(8,128)}) custom-call(s32[1]{0:T(128)} %dynamic_slice.9.length, f32[1024,128]{1,0:T(8,128)} %broadcast_in_dim.20.bias, bf16[1024,256]{1,0:T(8,128)(2,1)} %convolution_convert_fusion.9.q_ref, bf16[1024,256]{1,0:T(8,128)(2,1)} %convolution_convert_fusion.8.k_ref, ...), custom_call_target="tpu_custom_call" | custom-call | tf_op jit(solution)/shard_map/pallas_call | solution.py:790
  162.7 0.7 pad_maximum_fusion.4.tkv
  163.4 42.0 %shard_map.232 = (bf16[2,128,1024]{2,1,0:T(8,128)(2,1)}, bf16[2,2,128,1024]{3,2,1,0:T(8,128)(2,1)}) custom-call(bf16[8,128,256]{2,1,0:T(8,128)(2,1)} %bitcast.211, bf16[2,128,256]{2,1,0:T(8,128)(2,1)} %pad_maximum_fusion.4.tkv), custom_call_target="tpu_custom_call" | custom-call | tf_op jit(solution)/shard_map/pallas_call | solution.py:895
  205.4 0.6 pad.13.params
  206.0 0.6 and_select_fusion.text_bias
  206.7 9.4 %shard_map.233 = (f32[256,1024]{1,0:T(8,128)}, bf16[256,1024]{1,0:T(8,128)(2,1)}, bf16[256,1024]{1,0:T(8,128)(2,1)}, bf16[256,1024]{1,0:T(8,128)(2,1)}, f32[256,1024]{1,0:T(8,128)}, /*index=5*/bf16[256,1024]{1,0:T(8,128)(2,1)}) custom-call(bf16[2,128,1024]{2,1,0:T(8,128)(2,1)} %hid.3, bf16[2,128,1024]{2,1,0:T(8,128)(2,1)} %get-tuple-element.47.att, ...), custom_call_target="tpu_custom_call" | custom-call | tf_op jit(solution)/shard_map/pallas_call | solution.py:954
  216.1 37.3 %shard_map.234 = bf16[4,256,1024]{2,1,0:T(8,128)(2,1)} custom-call(bf16[256,1024]{1,0:T(8,128)(2,1)} %get-tuple-element.50.block), custom_call_target="tpu_custom_call" | custom-call | tf_op jit(solution)/shard_map/pallas_call | solution.py:1048
  253.4 1.9 copy.59
  255.4 1.3 copy-done.20
  256.6 4.4 fusion.63
  261.0 14.1 %add_convert_fusion.1 = (bf16[1024,1024]{1,0:T(8,128)(2,1)S(1)}, f32[1024,1024]{1,0:T(8,128)S(1)}) fusion(f32[1024,1024]{1,0:T(8,128)} %fusion.63, bf16[1024,1024]{1,0:T(8,128)(2,1)} %bitcast.223, bf16[1024,1024]{1,0:T(8,128)(2,1)} %all-gather.4.cloned.1.call-done), kind=kOutput, calls=%fused_computation.10 | convolution fusion | flops 2222981120 | bytes 14680064 | tf_op jit(solution)/shard_map/dot_general | solution.py:1349
  275.1 2.4 convolution_convert_fusion
  277.8 2.0 copy-done.9
  279.8 1.1 multiply_convert_fusion
  281.4 2.4 convolution_convert_fusion.1
  283.8 2.4 pad_maximum_fusion
  286.2 0.7 dynamic-slice_bitcast_fusion
  286.9 1.1 copy.61
  288.5 6.2 %convolution_convert_fusion.2 = bf16[1024,1024]{1,0:T(8,128)(2,1)} fusion(bf16[1024,1024]{1,0:T(8,128)(2,1)} %copy-done.36, bf16[1024,1024]{1,0:T(8,128)(2,1)} %bitcast.201), kind=kOutput, calls=%fused_computation.31 | convolution fusion | flops 2148532224 | bytes 6291456 | tf_op jit(solution)/shard_map/dot_general | solution.py:1351
  294.7 3.7 convolution_convert_fusion.3
  298.3 39.9 %shard_map.235 = (f32[256,1024]{1,0:T(8,128)}, f32[256,1024]{1,0:T(8,128)}) custom-call(bf16[4,256,1024]{2,1,0:T(8,128)(2,1)} %bitcast.206, bf16[4,256,1024]{2,1,0:T(8,128)(2,1)} %bitcast.202), custom_call_target="tpu_custom_call" | custom-call | tf_op jit(solution)/shard_map/pallas_call | solution.py:1086
  338.3 16.6 %shard_map.236 = (f32[256,1024]{1,0:T(8,128)}, bf16[32,96,1024]{2,1,0:T(8,128)(2,1)}, bf16[2,128,1024]{2,1,0:T(8,128)(2,1)}, bf16[2,2,128,1024]{3,2,1,0:T(8,128)(2,1)}, f32[8,1024]{1,0:T(8,128)}) custom-call(f32[256,1024]{1,0:T(8,128)} %get-tuple-element.54.g_third, bf16[2,128,1024]{2,1,0:T(8,128)(2,1)} %g_out.1, f32[256,1024]{1,0:T(8,128)} %get-tuple-element.49.after_cross, ...), custom_call_target="tpu_custom_call" | custom-call | tf_op jit(solution)/shard_map/pallas_call | solution.py:1016
  354.9 29.1 %shard_map.237 = (bf16[8,128,256]{2,1,0:T(8,128)(2,1)}, bf16[2,128,256]{2,1,0:T(8,128)(2,1)}) custom-call(bf16[2,128,1024]{2,1,0:T(8,128)(2,1)} %get-tuple-element.61.g_att, bf16[2,2,128,1024]{3,2,1,0:T(8,128)(2,1)} %get-tuple-element.62.text), custom_call_target="tpu_custom_call" | custom-call | tf_op jit(solution)/shard_map/pallas_call | solution.py:1139
  384.1 15.4 %shard_map.238 = (bf16[1024,256]{1,0:T(8,128)(2,1)}, bf16[1024,256]{1,0:T(8,128)(2,1)}, bf16[1024,256]{1,0:T(8,128)(2,1)}) custom-call(s32[1]{0:T(128)} %dynamic_slice.9.length, f32[1024,128]{1,0:T(8,128)} %broadcast_in_dim.20.bias, bf16[1024,256]{1,0:T(8,128)(2,1)} %convolution_convert_fusion.9.q_ref, bf16[1024,256]{1,0:T(8,128)(2,1)} %convolution_convert_fusion.8.k_ref, ...), custom_call_target="tpu_custom_call" | custom-call | tf_op jit(solution)/shard_map/pallas_call | solution.py:842
  399.6 1.9 fusion.65
  401.5 0.7 fusion.64
  402.3 4.0 fusion.58
  406.3 2.9 copy.60
  409.2 1.8 fusion.16
  411.0 0.7 fusion.18
  412.0 0.7 fusion.20
  413.5 1.8 copy.62
  416.0 3.5 fusion.8.cols
  419.8 1.0 fusion.21.text
  420.9 83.7 %shard_map.239 = (f32[2,128,1024]{2,1,0:T(8,128)}, f32[96,1024]{1,0:T(8,128)}, f32[160,1024]{1,0:T(8,128)}, f32[16,128]{1,0:T(8,128)}, bf16[2,16,1024]{2,1,0:T(8,128)(2,1)}) custom-call(bf16[8,128,1024]{2,1,0:T(8,128)(2,1)} %bitcast.180, bf16[4,8,96,1024]{3,2,1,0:T(8,128)(2,1)} %bitcast.182, bf16[4,8,176,256]{3,2,1,0:T(8,128)(2,1)} %fusion.8.cols, ...), custom_call_target="tpu_custom_call" | custom-call | tf_op jit(solution)/shard_map/pallas_call | solution.py:1254
  504.6 1.9 fusion.61
  506.5 1.2 slice_bitcast_fusion.2
  507.7 0.9 pad_maximum_fusion.1
  509.0 0.9 add_convert_fusion.3
  509.9 1.2 fusion.30
  511.2 2.0 fusion.36
  513.1 3.4 all-to-all-start
  517.1 4.7 all-to-all-done
  522.3 1.1 copy.76
  523.4 0.6 copy.82
  (114 shorter events, 5.8 us)
Async XLA Ops:
  7.2 155.0 %copy-start = (bf16[2,128,1024]{2,1,0:T(8,128)(2,1)S(1)}, bf16[2,128,1024]{2,1,0:T(8,128)(2,1)}, u32[]{:S(2)}) copy-start(bf16[2,128,1024]{2,1,0:T(8,128)(2,1)} %param.16) | copy-start | bytes 1572868
  7.2 246.2 %all-gather.6.cloned.1.call-start = ((), (), s32[]{:S(2)}) async-start(), calls=%async_computation.4 | async-start | bytes 2359296 | tf_op jit(solution)/shard_map/all_gather | solution.py:1322
  132.7 6.9 %copy-start.1 = (bf16[8,128,1024]{2,1,0:T(8,128)(2,1)S(1)}, bf16[8,128,1024]{2,1,0:T(8,128)(2,1)}, u32[]{:S(2)}) copy-start(bf16[8,128,1024]{2,1,0:T(8,128)(2,1)} %get-tuple-element.43) | copy-start | bytes 6291460
  132.8 128.3 %all-gather.4.cloned.1.call-start = ((), (), s32[]{:S(2)}) async-start(), calls=%async_computation.2 | async-start | bytes 2359296 | tf_op jit(solution)/shard_map/all_gather | solution.py:1320
  133.5 377.6 %reduce-scatter.2.cloned.1.call-start = ((), (), s32[]{:S(2)}) async-start(), calls=%async_computation.3 | async-start | bytes 4718592 | tf_op jit(solution)/shard_map/reduce_scatter | solution.py:1363
  142.2 2.4 copy-start.12
  142.2 2.4 copy-start.16
  142.2 3.9 copy-start.14
  142.3 20.0 %copy-start.5 = (bf16[1,4,256,256]{3,2,1,0:T(8,128)(2,1)}, bf16[1,4,256,256]{3,2,1,0:T(8,128)(2,1)S(1)}, u32[]{:S(2)}) copy-start(bf16[1,4,256,256]{3,2,1,0:T(8,128)(2,1)S(1)} %get-tuple-element.88) | copy-start | bytes 1572868
  142.3 20.2 %copy-start.3 = (bf16[1,4,256,256]{3,2,1,0:T(8,128)(2,1)}, bf16[1,4,256,256]{3,2,1,0:T(8,128)(2,1)S(1)}, u32[]{:S(2)}) copy-start(bf16[1,4,256,256]{3,2,1,0:T(8,128)(2,1)S(1)} %get-tuple-element.89) | copy-start | bytes 1572868
  146.1 59.9 %copy-start.32 = (s32[2,128]{1,0:T(2,128)S(1)}, s32[2,128]{1,0:T(2,128)}, u32[]{:S(2)}) copy-start(s32[2,128]{1,0:T(2,128)} %param.29) | copy-start | bytes 3076
  146.1 59.9 %copy-start.33 = (s32[2]{0:T(128)S(1)}, s32[2]{0:T(128)}, u32[]{:S(2)}) copy-start(s32[2]{0:T(128)} %param.28) | copy-start | bytes 28
  253.4 3.2 copy-start.18
  255.3 1.3 copy-start.20
  261.0 14.1 %copy-start.19 = (bf16[4,256,1024]{2,1,0:T(8,128)(2,1)S(1)}, bf16[4,256,1024]{2,1,0:T(8,128)(2,1)}, u32[]{:S(2)}) copy-start(bf16[4,256,1024]{2,1,0:T(8,128)(2,1)} %shard_map.234) | copy-start | bytes 6291460
  275.1 2.5 copy-start.36
  277.6 2.2 copy-start.9
  279.8 1.6 copy-start.35
  281.4 2.4 copy-start.10
  286.2 1.9 copy-start.2
  288.5 6.2 %copy-start.11 = (bf16[1024,1024]{1,0:T(8,128)(2,1)S(1)}, bf16[1024,1024]{1,0:T(8,128)(2,1)}, u32[]{:S(2)}) copy-start(bf16[1024,1024]{1,0:T(8,128)(2,1)} %copy-done.10) | copy-start | bytes 6291460
  288.5 6.2 %copy-start.34 = (bf16[1024,1024]{1,0:T(8,128)(2,1)S(1)}, bf16[1024,1024]{1,0:T(8,128)(2,1)}, u32[]{:S(2)}) copy-start(bf16[1024,1024]{1,0:T(8,128)(2,1)} %all-gather.4.cloned.1.call-done) | copy-start | bytes 6291460
  354.9 44.6 %copy-start.17 = (bf16[1,4,256,256]{3,2,1,0:T(8,128)(2,1)S(1)}, bf16[1,4,256,256]{3,2,1,0:T(8,128)(2,1)}, u32[]{:S(2)}) copy-start(bf16[1,4,256,256]{3,2,1,0:T(8,128)(2,1)} %copy-done.16) | copy-start | bytes 1572868
  384.1 17.4 %copy-start.15 = (bf16[1,4,256,256]{3,2,1,0:T(8,128)(2,1)S(1)}, bf16[1,4,256,256]{3,2,1,0:T(8,128)(2,1)}, u32[]{:S(2)}) copy-start(bf16[1,4,256,256]{3,2,1,0:T(8,128)(2,1)} %copy-done.14) | copy-start | bytes 1572868
  399.6 1.9 copy-start.26
  399.6 2.7 copy-start.13
  399.6 2.7 copy-start.23
  409.1 1.8 copy-start.25
  411.0 1.0 copy-start.24
  412.0 0.9 copy-start.27
  412.7 2.6 copy-start.30
  412.7 2.7 copy-start.29
  415.3 4.2 copy-start.6
  415.3 4.5 copy-start.4
  504.5 4.1 copy-start.8
  504.5 4.5 copy-start.7
  504.6 4.5 copy-start.22
  504.6 5.4 %copy-start.21 = (f32[256,1024]{1,0:T(8,128)S(1)}, f32[256,1024]{1,0:T(8,128)}, u32[]{:S(2)}) copy-start(f32[256,1024]{1,0:T(8,128)} %get-tuple-element.59) | copy-start | bytes 3145732
  509.0 7.6 %copy-start.31 = (f32[16,128]{1,0:T(8,128)S(1)}, f32[16,128]{1,0:T(8,128)}, u32[]{:S(2)}) copy-start(f32[16,128]{1,0:T(8,128)} %get-tuple-element.74) | copy-start | bytes 24580
  509.9 13.4 %copy-start.28 = (bf16[2,16,1024]{2,1,0:T(8,128)(2,1)S(1)}, bf16[2,16,1024]{2,1,0:T(8,128)(2,1)}, u32[]{:S(2)}) copy-start(bf16[2,16,1024]{2,1,0:T(8,128)(2,1)} %get-tuple-element.128) | copy-start | bytes 196612
  513.1 8.8 %all-to-all-start = ((bf16[4,32,1024]{2,1,0:T(8,128)(2,1)}), bf16[4,32,1024]{2,1,0:T(8,128)(2,1)S(1)}, u32[]{:S(2)}, u32[]{:S(2)}) async-start(bf16[4,32,1024]{2,1,0:T(8,128)(2,1)} %bitcast.66), calls=%async_computation.1 | async-start | bytes 524288 | tf_op jit(solution)/shard_map/all_to_all | solution.py:1365
Sparse Core Ops, SparseCore 0:
  132.9 27.3 all-gather.5
  161.9 44.7 all-gather.3
  286.3 51.1 reduce-scatter.1

commit v2 on v1

--- a/solution.py
+++ b/solution.py
@@ -506,15 +506,16 @@
 
 
 class ClipGather:
-    def __init__(self, wire, block, tag):
+    def __init__(self, wire, block, tag, own=None):
         self.wire, self.block, self.tag = wire, block, tag
+        self.own = own or (lambda half: block(wire.here.c, half))
 
     def begin(self):
-        h, w, b, t = self.wire.here, self.wire, self.block, self.tag
-        w.send(b(h.c, 0), b(h.c, 0), t, h.cx, h.f)
-        w.send(b(h.c, 1), b(h.c, 1), t + 2, h.cy, h.f)
-        w.send(b(h.c, 1), b(h.c, 1), t + 1, h.cx, h.f)
-        w.send(b(h.c, 0), b(h.c, 0), t + 3, h.cy, h.f)
+        h, w, b, t, own = self.wire.here, self.wire, self.block, self.tag, self.own
+        w.send(own(0), b(h.c, 0), t, h.cx, h.f)
+        w.send(own(1), b(h.c, 1), t + 2, h.cy, h.f)
+        w.send(own(1), b(h.c, 1), t + 1, h.cx, h.f)
+        w.send(own(0), b(h.c, 0), t + 3, h.cy, h.f)
 
     def middle(self):
         h, w, b, t = self.wire.here, self.wire, self.block, self.tag
@@ -534,16 +535,61 @@
         w.arrived(b(h.cd, 1), t + 5)
 
 
+class ZGather:
+    def __init__(self, wire, slot, tag, own=None):
+        self.wire, self.slot, self.tag = wire, slot, tag
+        self.own = own if own is not None else slot(wire.here.f)
+        self.open = []
+
+    def step(self, s):
+        h, w = self.wire.here, self.wire
+        left, right = h.f - 2 * (s - 1), h.f + 2 * (s - 1)
+        if s > 1:
+
+            @pl.when(left >= 0)
+            def _():
+                w.arrived(self.slot(left), self.tag + s - 2)
+
+            @pl.when(right <= 7)
+            def _():
+                w.arrived(self.slot(right), self.tag + 3 + s - 2)
+
+        if s > 3:
+            return
+        for block, tag, go, to in (
+            (left, self.tag, (left >= 0) & (h.z <= 2), h.f + 2),
+            (right, self.tag + 3, (right <= 7) & (h.z >= 1), h.f - 2),
+        ):
+            src = self.own if s == 1 else self.slot(block)
+            copy = w.copy(src, self.slot(block), tag + s - 1, h.c, to)
+            pl.when(go)(copy.start)
+            self.open.append((go, copy))
+
+    def relay(self, d):
+        h, w = self.wire.here, self.wire
+        f = h.zstep(d)
+        w.send(self.own if d == 0 else self.slot(f), self.slot(f), self.tag + 6 + d, h.c, h.sib)
+
+    def end(self):
+        h, w = self.wire.here, self.wire
+        for d in range(4):
+            w.arrived(self.slot(h.zstep(d) + h.sib - h.f), self.tag + 6 + d)
+        for go, copy in self.open:
+            pl.when(go)(copy.wait_send)
+
+
 class ClipScatter:
     def __init__(self, wire, parts, slots, tag):
         self.wire, self.parts, self.slots, self.tag = wire, parts, slots, tag
 
-    def begin(self):
+    def begin(self, which=None):
         h, w, p, s, t = self.wire.here, self.wire, self.parts, self.slots, self.tag
-        w.send(p(h.cd, 0), s[0], t, h.cx, h.f)
-        w.send(p(h.cd, 1), s[1], t + 1, h.cy, h.f)
-        w.send(p(h.cx, 0), s[2], t + 2, h.cx, h.f)
-        w.send(p(h.cy, 1), s[3], t + 3, h.cy, h.f)
+        if which != 1:
+            w.send(p(h.cd, 0), s[0], t, h.cx, h.f)
+            w.send(p(h.cd, 1), s[1], t + 1, h.cy, h.f)
+        if which != 0:
+            w.send(p(h.cx, 0), s[2], t + 2, h.cx, h.f)
+            w.send(p(h.cy, 1), s[3], t + 3, h.cy, h.f)
 
     def middle(self):
         h, w, p, s, t = self.wire.here, self.wire, self.parts, self.slots, self.tag
@@ -568,6 +614,20 @@
 
 def add_into(into, other):
     into[...] = (into[...].astype(F32) + other[...].astype(F32)).astype(BF16)
+
+
+class LocalCopy:
+    def __init__(self, src, through, dst, sem):
+        self.a = pltpu.make_async_copy(src, through, sem)
+        self.b = pltpu.make_async_copy(through, dst, sem)
+        self.a.start()
+
+    def turn(self):
+        self.a.wait()
+        self.b.start()
+
+    def wait(self):
+        self.b.wait()
 
 
 def comm_call(body, out_shape, in_specs, out_specs, scratch, copies, tags, collective_id, cost=None):
@@ -588,163 +648,6 @@
     return jax.ShapeDtypeStruct(dims, dtype)
 
 
-def fetch_body(hid, w5, square, grad, fin, o_hid, o_w5, o_square, o_grad, o_fin, local, send_sem, recv_sem):
-    h = Here()
-    w = Wire(h, send_sem, recv_sem)
-    greet(frame_others(h) + clip_others(h))
-    T_HID, T_W, T_FIN, T_ZL, T_ZR = 0, 7, 14, 17, 20
-    T_WXY, T_GXY, T_SXY, T_SIB = 23, 29, 35, 59
-
-    def my_columns(f):
-        return pl.ds(pl.multiple_of(lax.rem(f, 4) * 256, 256), 256)
-
-    def my_rows(f):
-        return pl.ds(pl.multiple_of(f * 32, 32), 32)
-
-    here_copies = [
-        pltpu.make_async_copy(hid.at[h.pair], o_hid.at[h.f], local.at[0]),
-        pltpu.make_async_copy(
-            w5.at[:, :, my_columns(h.f)], o_w5.at[:, h.c, my_rows(h.f), :], local.at[1]
-        ),
-        pltpu.make_async_copy(square, o_square.at[h.c, h.f], local.at[2]),
-        pltpu.make_async_copy(grad, o_grad.at[h.c], local.at[3]),
-        pltpu.make_async_copy(
-            fin.at[:, pl.ds(pl.multiple_of(h.c * 1024, 1024), 1024)], o_fin.at[h.c], local.at[4]
-        ),
-    ]
-    w.send(hid.at[h.pair], o_hid.at[h.f], T_HID + 1, h.c, h.partner)
-    far_tag = T_HID + 2 + h.role
-    w.send(hid.at[1 - h.pair], o_hid.at[h.f], far_tag, h.c, h.far_gate)
-    w.send(hid.at[h.pair], o_hid.at[h.f], T_HID, h.c, h.sib)
-    for d in range(1, 8):
-        f = h.step(d)
-        w.send(w5.at[:, :, my_columns(f)], o_w5.at[:, h.c, my_rows(h.f), :], T_W + d - 1, h.c, f)
-    for copy in here_copies:
-        copy.start()
-    for i, (c, f) in enumerate(clip_others(h)):
-        w.send(
-            fin.at[:, pl.ds(pl.multiple_of(c * 1024, 1024), 1024)], o_fin.at[h.c], T_FIN + i, c, f
-        )
-    for copy in here_copies:
-        copy.wait()
-    def square_slot(c, f):
-        return o_square.at[c, f]
-
-    z_copies = []
-
-    def z_step(s):
-        if s > 1:
-            @pl.when(h.z - (s - 1) >= 0)
-            def _():
-                w.arrived(square_slot(h.c, h.f - 2 * (s - 1)), T_ZL + s - 2)
-
-            @pl.when(h.z + (s - 1) <= 3)
-            def _():
-                w.arrived(square_slot(h.c, h.f + 2 * (s - 1)), T_ZR + s - 2)
-
-        if s > 3:
-            return
-        right_block = h.f - 2 * (s - 1)
-        left_block = h.f + 2 * (s - 1)
-        go_right = (right_block >= 0) & (h.z <= 2)
-        go_left = (left_block <= 7) & (h.z >= 1)
-        right = w.copy(
-            square_slot(h.c, right_block), square_slot(h.c, right_block), T_ZL + s - 1, h.c, h.f + 2
-        )
-        left = w.copy(
-            square_slot(h.c, left_block), square_slot(h.c, left_block), T_ZR + s - 1, h.c, h.f - 2
-        )
-        for go, copy in ((go_right, right), (go_left, left)):
-            pl.when(go)(copy.start)
-            z_copies.append((go, copy))
-
-    z_step(1)
-    for d in range(1, 8):
-        f = lax.rem(h.f + 8 - d, 8)
-        w.arrived(o_w5.at[:, h.c, my_rows(f), :], T_W + d - 1)
-    w5_gather = ClipGather(w, lambda c, half: o_w5.at[:, c, pl.ds(128 * half, 128), :], T_WXY)
-    w5_gather.begin()
-    w.arrived(o_hid.at[h.partner], T_HID + 1)
-    w.send(o_hid.at[h.partner], o_hid.at[h.partner], T_HID + 4, h.c, h.sib)
-    forwards = []
-    for j in range(2):
-        block = o_hid.at[h.far[j]]
-        w.arrived(block, T_HID + 2 + j)
-        forward = w.copy(block, block, T_HID + 2 + j, h.c, h.partner)
-        pl.when(h.is_gate)(forward.start)
-        forwards.append(forward)
-        w.send(block, block, T_HID + 5 + j, h.c, h.sib)
-    w5_gather.middle()
-    z_step(2)
-
-    def square_gather(d):
-        f = h.zstep(d)
-        return ClipGather(
-            w,
-            lambda c, half: o_square.at[c, f, pl.ds(64 * half, 64 - 16 * half), :],
-            T_SXY + 6 * d,
-        )
-
-    gathers = [square_gather(d) for d in range(4)]
-    gathers[0].begin()
-    grad_gather = ClipGather(w, lambda c, half: o_grad.at[c, pl.ds(128 * half, 128), :], T_GXY)
-    grad_gather.begin()
-    z_step(3)
-    z_step(4)
-    for d in range(1, 4):
-        gathers[d].begin()
-    grad_gather.middle()
-    for d in range(4):
-        f = h.zstep(d)
-        w.send(square_slot(h.c, f), square_slot(h.c, f), T_SIB + 4 * d, h.c, h.sib)
-        gathers[d].middle()
-        gathers[d].near()
-        w.send(square_slot(h.cx, f), square_slot(h.cx, f), T_SIB + 4 * d + 1, h.c, h.sib)
-        w.send(square_slot(h.cy, f), square_slot(h.cy, f), T_SIB + 4 * d + 2, h.c, h.sib)
-    for d in range(4):
-        f = h.zstep(d)
-        gathers[d].end()
-        w.send(square_slot(h.cd, f), square_slot(h.cd, f), T_SIB + 4 * d + 3, h.c, h.sib)
-    w5_gather.near()
-    w5_gather.end()
-    grad_gather.near()
-    grad_gather.end()
-    for i, (c, f) in enumerate(clip_others(h)):
-        w.arrived(o_fin.at[c], T_FIN + i)
-    w.arrived(o_hid.at[h.sib], T_HID)
-    w.arrived(o_hid.at[h.partner + h.sib - h.f], T_HID + 4)
-    for j in range(2):
-        w.arrived(o_hid.at[h.far[j] + h.sib - h.f], T_HID + 5 + j)
-    for d in range(4):
-        f = h.zstep(d) + h.sib - h.f
-        for i, c in enumerate((h.c, h.cx, h.cy, h.cd)):
-            w.arrived(square_slot(c, f), T_SIB + 4 * d + i)
-    w.drain()
-    for go, copy in z_copies:
-        pl.when(go)(copy.wait_send)
-    for copy in forwards:
-        pl.when(h.is_gate)(copy.wait_send)
-
-
-def fetch(hid, w5, square, grad, fin):
-    return comm_call(
-        fetch_body,
-        (
-            shape((8, 128, 1024)),
-            shape((5, 4, 256, 256)),
-            shape((4, 8, 112, 1024)),
-            shape((4, 256, 1024)),
-            shape((4, 32, 1024)),
-        ),
-        [HBM] * 5,
-        (HBM,) * 5,
-        [pltpu.SemaphoreType.DMA((5,))],
-        96,
-        80,
-        1,
-    )(hid, w5, square, grad, fin)
-
-
 ROWS = 256
 
 
@@ -762,39 +665,284 @@
     return jnp.concatenate([scores[:first] + bias_ref[0:first, 0:1], low], axis=0)
 
 
-def attend_body(length, bias, q_ref, k_ref, v_ref, o_ref, lse_ref, out_t, v_t):
-    v_t[...] = v_ref[...].T
+def norm_parts(value):
+    centered = value - jnp.mean(value, axis=-1, keepdims=True)
+    scale = lax.rsqrt(jnp.mean(centered * centered, axis=-1, keepdims=True) + EPSILON)
+    return centered * scale, scale
+
+
+def column_weight(cols, j):
+    return cols[:, :, 32 * j : 32 * j + 32, :].reshape(1024, 256)
+
+
+def attend_rows(i, length, bias, q_ref, k_ref, v_t, o_ref, lse_ref, out_t):
     lane_head = lax.broadcasted_iota(jnp.int32, (ROWS, 256), 1) // HD
-    for i in range(1024 // ROWS):
-        first, n = i * ROWS, (i + 1) * ROWS
-        q = q_ref[first:n, :]
-
-        def head(j, _):
-            q_head = jnp.where(lane_head == j, q, 0) * jnp.asarray(HD**-0.5, BF16)
-            scores = mask_scores(dot(k_ref[0:n, :], q_head, (1, 1)), bias, first, ROWS)
-            top = jnp.max(scores, axis=0, keepdims=True)
-            weight = jnp.exp(scores - top)
-            total = jnp.sum(weight, axis=0, keepdims=True)
-            at = pl.ds(pl.multiple_of(j * HD, HD), HD)
-            part = dot(v_t[at, 0:n], weight.astype(BF16), (1, 0))
-            out_t[at, :] = part / total
-            lse_ref[pl.ds(j, 1), first:n] = top + jnp.log(total)
-            return 0
-
-        lax.fori_loop(0, 4, head, 0)
-        live = first + lax.broadcasted_iota(jnp.int32, (ROWS, 256), 0) < length[0]
-        o_ref[first:n, :] = jnp.where(live, out_t[...].T, 0).astype(BF16)
-
-
-def attend(length, bias, q, k, v):
-    return pl.pallas_call(
-        attend_body,
-        out_shape=(shape((1024, 256)), shape((8, 1024), F32)),
-        in_specs=[SMEM] + [VMEM] * 4,
-        out_specs=(VMEM, VMEM),
-        scratch_shapes=[pltpu.VMEM((256, ROWS), F32), pltpu.VMEM((256, 1024), BF16)],
-        compiler_params=pltpu.CompilerParams(vmem_limit_bytes=56 * 2**20),
-    )(length, bias, q, k, v)
+    first, n = i * ROWS, (i + 1) * ROWS
+    q = q_ref[first:n, :]
+
+    def head(j, _):
+        q_head = jnp.where(lane_head == j, q, 0) * jnp.asarray(HD**-0.5, BF16)
+        scores = mask_scores(dot(k_ref[0:n, :], q_head, (1, 1)), bias, first, ROWS)
+        top = jnp.max(scores, axis=0, keepdims=True)
+        weight = jnp.exp(scores - top)
+        total = jnp.sum(weight, axis=0, keepdims=True)
+        at = pl.ds(pl.multiple_of(j * HD, HD), HD)
+        out_t[at, :] = dot(v_t[at, 0:n], weight.astype(BF16), (1, 0)) / total
+        lse_ref[pl.ds(j, 1), first:n] = top + jnp.log(total)
+        return 0
+
+    lax.fori_loop(0, 4, head, 0)
+    live = first + lax.broadcasted_iota(jnp.int32, (ROWS, 256), 0) < length[0]
+    o_ref[first:n, :] = jnp.where(live, out_t[...].T, 0).astype(BF16)
+
+
+def front_body(
+    length, bias, text, hid, cols_a, cols_b, square, fin,
+    o_hid, o_first, o_q, o_k, o_v, o_heads, o_lse, o_cols_a, o_cols_b, o_params, o_att, o_tkv, o_square, o_fin,
+    out_t, v_t, tkv, v_square, v_fin, local, send_sem, recv_sem,
+):
+    h = Here()
+    w = Wire(h, send_sem, recv_sem)
+    T_HID, T_A, T_B, T_FIN, T_AXY, T_BXY = 0, 10, 17, 24, 27, 33
+    T_Z, T_SXY, T_SIB, T_ATT, T_TKV = 39, 49, 73, 85, 93
+
+    def my_columns(f):
+        return pl.ds(pl.multiple_of(lax.rem(f, 4) * 256, 256), 256)
+
+    def fin_part(c):
+        return fin.at[:, pl.ds(pl.multiple_of(c * 1024, 1024), 1024)]
+
+    plain = [
+        pltpu.make_async_copy(cols_a.at[:, my_columns(h.f)], o_cols_a.at[h.c, h.f], local.at[0]),
+        pltpu.make_async_copy(cols_b.at[:, my_columns(h.f)], o_cols_b.at[h.c, h.f], local.at[1]),
+        pltpu.make_async_copy(hid.at[h.pair], o_hid.at[h.f], local.at[2]),
+    ]
+    for copy in plain:
+        copy.start()
+    turned = [
+        LocalCopy(square, v_square, o_square.at[h.c, h.f], local.at[3]),
+        LocalCopy(fin_part(h.c), v_fin, o_fin.at[h.c], local.at[4]),
+    ]
+    greet(frame_others(h) + clip_others(h))
+
+    for d in (2, 6, 4, 3, 5, 1, 7):
+        f = h.step(d)
+        w.send(cols_a.at[:, my_columns(f)], o_cols_a.at[h.c, h.f], T_A + d - 1, h.c, f)
+
+    def half_of(ref, part):
+        return ref.at[pl.ds(64 * part, 64), :]
+
+    for part in range(2):
+        w.send(half_of(hid.at[h.pair], part), half_of(o_hid.at[h.f], part), T_HID + 1 + part, h.c, h.partner)
+        w.send(
+            half_of(hid.at[1 - h.pair], part),
+            half_of(o_hid.at[h.f], part),
+            T_HID + 3 + 2 * h.role + part,
+            h.c,
+            h.far_gate,
+        )
+    w.send(hid.at[h.pair], o_hid.at[h.f], T_HID, h.c, h.sib)
+
+    def square_slot(f):
+        return o_square.at[h.c, f]
+
+    z_gather = ZGather(w, square_slot, T_Z, square)
+
+    def square_gather(d):
+        f = h.zstep(d)
+        return ClipGather(
+            w,
+            lambda c, half: o_square.at[c, f, pl.ds(48 * half, 48), :],
+            T_SXY + 6 * d,
+            (lambda half: square.at[pl.ds(48 * half, 48), :]) if d == 0 else None,
+        )
+
+    gathers = [square_gather(d) for d in range(4)]
+    gathers[0].begin()
+    for i, (c, f) in enumerate(clip_others(h)):
+        w.send(fin_part(c), o_fin.at[h.c], T_FIN + i, c, f)
+    for copy in turned:
+        copy.turn()
+    plain[0].wait()
+    for d in range(1, 8):
+        w.arrived(o_cols_a.at[h.c, lax.rem(h.f + 8 - d, 8)], T_A + d - 1)
+    a_gather = ClipGather(w, lambda c, half: o_cols_a.at[c, pl.ds(4 * half, 4)], T_AXY)
+    a_gather.begin()
+    forwards = []
+    for part in range(2):
+        for j in range(2):
+            block = half_of(o_hid.at[h.far[j]], part)
+            w.arrived(block, T_HID + 3 + 2 * j + part)
+            forward = w.copy(block, block, T_HID + 3 + 2 * j + part, h.c, h.partner)
+            pl.when(h.is_gate)(forward.start)
+            forwards.append(forward)
+    for d in (2, 6, 4, 3, 5, 1, 7):
+        f = h.step(d)
+        w.send(cols_b.at[:, my_columns(f)], o_cols_b.at[h.c, h.f], T_B + d - 1, h.c, f)
+    for part in range(2):
+        w.arrived(half_of(o_hid.at[h.partner], part), T_HID + 1 + part)
+    w.send(o_hid.at[h.partner], o_hid.at[h.partner], T_HID + 7, h.c, h.sib)
+    for j in range(2):
+        w.send(o_hid.at[h.far[j]], o_hid.at[h.far[j]], T_HID + 8 + j, h.c, h.sib)
+    a_gather.middle()
+    z_gather.step(1)
+    z_gather.relay(0)
+    plain[1].wait()
+    for d in range(1, 8):
+        w.arrived(o_cols_b.at[h.c, lax.rem(h.f + 8 - d, 8)], T_B + d - 1)
+    b_gather = ClipGather(w, lambda c, half: o_cols_b.at[c, pl.ds(4 * half, 4)], T_BXY)
+    b_gather.begin()
+    gathers[0].middle()
+    a_gather.near()
+    a_gather.end()
+    for g in range(8):
+        group = sum(o_cols_a[g // 2, 4 * (g % 2) + i, 96:104, 0:128].astype(F32) for i in range(4))
+        o_params[:, 128 * g : 128 * g + 128] = group
+    plain[2].wait()
+    w.arrived(o_hid.at[h.sib], T_HID)
+    w.arrived(o_hid.at[h.partner + h.sib - h.f], T_HID + 7)
+    for j in range(2):
+        w.arrived(o_hid.at[h.far[j] + h.sib - h.f], T_HID + 8 + j)
+    z_gather.step(2)
+
+    def project_rows(i, _):
+        at = pl.ds(pl.multiple_of(i * 256, 256), 256)
+        rows = o_hid[pl.ds(2 * i, 2)].reshape(256, 1024).astype(F32)
+        xhat, _ = norm_parts(rows)
+        low = (xhat * o_params[0:1, :] + o_params[3:4, :]).astype(BF16)
+        o_first[at, :] = low
+        for j, out in enumerate((o_q, o_k, o_v)):
+            out[at, :] = dot(low, column_weight(o_cols_a, j), (1, 0)).astype(BF16)
+        return 0
+
+    lax.fori_loop(0, 2, project_rows, 0)
+    z_gather.step(3)
+    gathers[2].begin()
+    z_gather.relay(2)
+    b_gather.middle()
+    lax.fori_loop(2, 4, project_rows, 0)
+    v_t[...] = o_v[...].T
+    b_gather.near()
+    b_gather.end()
+    z_gather.step(4)
+    for d in (1, 3):
+        gathers[d].begin()
+        z_gather.relay(d)
+
+    def text_slot(f):
+        return o_tkv.at[lax.div(f, 4), :, :, my_columns(f)]
+
+    for j in range(2):
+        tkv[j] = dot(text[h.pair], column_weight(o_cols_b, j), (1, 0)).astype(BF16)
+    for d in range(1, 4):
+        w.send(tkv, text_slot(h.f), T_TKV + d, h.c, h.zstep(d))
+    w.send(tkv, text_slot(h.f), T_TKV, h.c, h.sib)
+    text_copy = pltpu.make_async_copy(tkv, text_slot(h.f), local.at[5])
+    text_copy.start()
+
+    def att_slot(f):
+        return o_att.at[lax.div(f, 4), :, my_columns(f)]
+
+    att_sends = []
+
+    def attend_and_send(i):
+        attend_rows(i, length, bias, o_q, o_k, v_t, o_heads, o_lse, out_t)
+        for f in (2 * i, 2 * i + 1):
+            block = o_heads.at[pl.ds(128 * f, 128), :]
+            away = h.f != f
+            copy = w.copy(block, att_slot(h.f), T_ATT + h.f, h.c, f)
+            stay = pltpu.make_async_copy(block, att_slot(h.f), local.at[6])
+            pl.when(away)(copy.start)
+            pl.when(jnp.logical_not(away))(stay.start)
+            att_sends.append((away, copy, stay))
+
+    def square_steps(d):
+        f = h.zstep(d)
+        if d > 0:
+            gathers[d].middle()
+        gathers[d].near()
+        for i, c in enumerate((h.cx, h.cy)):
+            w.send(o_square.at[c, f], o_square.at[c, f], T_SIB + 3 * d + i, h.c, h.sib)
+
+    def square_last(d):
+        f = h.zstep(d)
+        gathers[d].end()
+        w.send(o_square.at[h.cd, f], o_square.at[h.cd, f], T_SIB + 3 * d + 2, h.c, h.sib)
+
+    attend_and_send(3)
+    square_steps(0)
+    square_steps(2)
+    square_last(0)
+    attend_and_send(2)
+    square_steps(1)
+    square_last(2)
+    for d in range(1, 4):
+        f = lax.rem(h.f + 8 - 2 * d, 8)
+        w.arrived(text_slot(f), T_TKV + d)
+        w.send(text_slot(f), text_slot(f), T_TKV + 3 + d, h.c, h.sib)
+    attend_and_send(1)
+    square_steps(3)
+    attend_and_send(0)
+    square_last(1)
+    square_last(3)
+    z_gather.end()
+    for d in range(4):
+        f = h.zstep(d) + h.sib - h.f
+        for i, c in enumerate((h.cx, h.cy, h.cd)):
+            w.arrived(o_square.at[c, f], T_SIB + 3 * d + i)
+    for d in range(1, 8):
+        f = lax.rem(h.f + 8 - d, 8)
+        w.arrived(att_slot(f), T_ATT + f)
+    w.arrived(text_slot(h.sib), T_TKV)
+    for d in range(1, 4):
+        w.arrived(text_slot(lax.rem(h.sib + 8 - 2 * d, 8)), T_TKV + 3 + d)
+    for i, (c, f) in enumerate(clip_others(h)):
+        w.arrived(o_fin.at[c], T_FIN + i)
+    for copy in turned:
+        copy.wait()
+    text_copy.wait()
+    w.drain()
+    for copy in forwards:
+        pl.when(h.is_gate)(copy.wait_send)
+    for away, copy, stay in att_sends:
+        pl.when(away)(copy.wait_send)
+        pl.when(jnp.logical_not(away))(stay.wait)
+
+
+def front(length, bias, text, hid, cols_a, cols_b, square, fin):
+    column = (1024, 256)
+    return comm_call(
+        front_body,
+        (
+            shape((8, 128, 1024)),
+            shape((1024, 1024)),
+            shape(column),
+            shape(column),
+            shape(column),
+            shape(column),
+            shape((8, 1024), F32),
+            shape((4, 8, 112, 256)),
+            shape((4, 8, 64, 256)),
+            shape((8, 1024), F32),
+            shape((2, 128, 1024)),
+            shape((2, 2, 128, 1024)),
+            shape((4, 8, 96, 1024)),
+            shape((4, 32, 1024)),
+        ),
+        [SMEM, VMEM, VMEM] + [HBM] * 5,
+        (VMEM,) * 10 + (HBM,) * 4,
+        [
+            pltpu.VMEM((256, ROWS), F32),
+            pltpu.VMEM((256, 1024), BF16),
+            pltpu.VMEM((2, 128, 256), BF16),
+            pltpu.VMEM((96, 1024), BF16),
+            pltpu.VMEM((32, 1024), BF16),
+            pltpu.SemaphoreType.DMA((7,)),
+        ],
+        128,
+        100,
+        1,
+    )(length, bias, text, hid, cols_a, cols_b, square, fin)
 
 
 def attend_back_body(
@@ -854,62 +1002,6 @@
     )(length, bias, q, k, v, o, lse, g)
 
 
-def return_body(att, tkv, o_att, o_tkv, local, send_sem, recv_sem):
-    h = Here()
-    w = Wire(h, send_sem, recv_sem)
-    greet(frame_others(h))
-
-    def slot(f):
-        return o_att.at[lax.div(f, 4), :, pl.ds(pl.multiple_of(lax.rem(f, 4) * 256, 256), 256)]
-
-    def text_slot(f):
-        return o_tkv.at[lax.div(f, 4), :, :, pl.ds(pl.multiple_of(lax.rem(f, 4) * 256, 256), 256)]
-
-    for d in range(1, 8):
-        f = h.step(d)
-        w.send(att.at[f], slot(h.f), d - 1, h.c, f)
-    copies = [
-        pltpu.make_async_copy(att.at[h.f], slot(h.f), local.at[0]),
-        pltpu.make_async_copy(tkv, text_slot(h.f), local.at[1]),
-    ]
-    for copy in copies:
-        copy.start()
-    for d in range(1, 4):
-        w.send(tkv, text_slot(h.f), 7 + d, h.c, h.zstep(d))
-    w.send(tkv, text_slot(h.f), 11, h.c, h.sib)
-    for d in range(1, 4):
-        f = lax.rem(h.f + 8 - 2 * d, 8)
-        w.arrived(text_slot(f), 7 + d)
-        w.send(text_slot(f), text_slot(f), 11 + d, h.c, h.sib)
-    for d in range(1, 8):
-        w.arrived(slot(lax.rem(h.f + 8 - d, 8)), d - 1)
-    w.arrived(text_slot(h.sib), 11)
-    for d in range(1, 4):
-        w.arrived(text_slot(lax.rem(h.sib + 8 - 2 * d, 8)), 11 + d)
-    for copy in copies:
-        copy.wait()
-    w.drain()
-
-
-def give_back(att, tkv):
-    return comm_call(
-        return_body,
-        (shape((2, 128, 1024)), shape((2, 2, 128, 1024))),
-        [HBM] * 2,
-        (HBM,) * 2,
-        [pltpu.SemaphoreType.DMA((2,))],
-        16,
-        16,
-        2,
-    )(att, tkv)
-
-
-def norm_parts(value):
-    centered = value - jnp.mean(value, axis=-1, keepdims=True)
-    scale = lax.rsqrt(jnp.mean(centered * centered, axis=-1, keepdims=True) + EPSILON)
-    return centered * scale, scale
-
-
 def square_of(square, which):
     return square[:, 32 * which : 32 * which + 32, :].reshape(1024, 1024)
 
@@ -926,15 +1018,46 @@
     return sum(jnp.where(lane_head == j, stacked[128 * j : 128 * j + 128], 0) for j in range(4))
 
 
+def near_devices(here):
+    return [(here.c, here.sib)] + [(here.c, here.zstep(d)) for d in range(1, 4)] + clip_others(here)[:2]
+
+
 def middle_body(
-    hid, att, square, tkv, text_bias, params, o_self, second_ref, query_ref, crossed_ref, o_cross, third_ref
+    hid, att, square, tkv, text_bias, params, grad, fin,
+    o_self, second_ref, query_ref, crossed_ref, o_cross, third_ref, o_grad, o_win,
+    v_grad, v_fin, local, send_sem, recv_sem,
 ):
+    h = Here()
+    w = Wire(h, send_sem, recv_sem)
+
+    def win_slot(f):
+        return o_win.at[:, f]
+
+    own = [
+        LocalCopy(grad, v_grad, o_grad.at[h.c], local.at[0]),
+        LocalCopy(fin, v_fin, win_slot(h.f), local.at[1]),
+    ]
+    greet(near_devices(h))
+    z_gather = ZGather(w, win_slot, 0, fin)
+    grad_gather = ClipGather(
+        w,
+        lambda c, half: o_grad.at[c, pl.ds(128 * half, 128), :],
+        10,
+        lambda half: grad.at[pl.ds(128 * half, 128), :],
+    )
+    z_gather.step(1)
+    grad_gather.begin()
+    z_gather.relay(0)
+    for copy in own:
+        copy.turn()
     att_value = att[...].reshape(256, 1024)
     after_self = hid[...].reshape(256, 1024).astype(F32) + dot(att_value, square_of(square, 0), (1, 0))
     o_self[...] = after_self
     xhat, _ = norm_parts(after_self)
     second_ref[...] = (xhat * params[1:2, :] + params[4:5, :]).astype(BF16)
+    z_gather.step(2)
     query_ref[...] = dot(second_ref[...], square_of(square, 1), (1, 0)).astype(BF16)
+    grad_gather.middle()
     lane_head = lax.broadcasted_iota(jnp.int32, (128, 256), 1) // HD
     for clip in range(2):
         for group in range(4):
@@ -943,21 +1066,156 @@
             probs, _ = text_probs(query, tkv[clip, 0, :, columns], text_bias[clip : clip + 1, :], lane_head)
             part = dot(probs.astype(BF16), tkv[clip, 1, :, columns], (1, 0))
             crossed_ref[rows, columns] = pick_heads(part, lane_head).astype(BF16)
-    after_cross = after_self + dot(crossed_ref[...], square_of(square, 2), (1, 0))
+        z_gather.step(3 + clip)
+    for d in range(1, 4):
+        z_gather.relay(d)
+    after_cross = o_self[...] + dot(crossed_ref[...], square_of(square, 2), (1, 0))
     o_cross[...] = after_cross
     xhat, _ = norm_parts(after_cross)
     third_ref[...] = (xhat * params[2:3, :] + params[5:6, :]).astype(BF16)
-
-
-def middle(hid, att, square, tkv, text_bias, params):
+    grad_gather.near()
+    grad_gather.end()
+    z_gather.end()
+    for copy in own:
+        copy.wait()
+    w.drain()
+
+
+def middle(hid, att, square, tkv, text_bias, params, grad, fin):
     rows = (256, 1024)
-    return pl.pallas_call(
+    return comm_call(
         middle_body,
-        out_shape=(shape(rows, F32), shape(rows), shape(rows), shape(rows), shape(rows, F32), shape(rows)),
-        in_specs=[VMEM] * 6,
-        out_specs=(VMEM,) * 6,
-        compiler_params=pltpu.CompilerParams(vmem_limit_bytes=56 * 2**20),
-    )(hid, att, square, tkv, text_bias, params)
+        (
+            shape(rows, F32),
+            shape(rows),
+            shape(rows),
+            shape(rows),
+            shape(rows, F32),
+            shape(rows),
+            shape((4, 256, 1024)),
+            shape((4, 8, 32, 1024)),
+        ),
+        [VMEM] * 6 + [HBM] * 2,
+        (VMEM,) * 6 + (HBM,) * 2,
+        [
+            pltpu.VMEM((256, 1024), BF16),
+            pltpu.VMEM((4, 32, 1024), BF16),
+            pltpu.SemaphoreType.DMA((2,)),
+        ],
+        20,
+        16,
+        2,
+    )(hid, att, square, tkv, text_bias, params, grad, fin)
+
+
+def feed_body(
+    third, grad, win, fout, o_third, o_out, o_terms,
+    tokens, wout, inner, slope, g_pre, terms, slots, local, send_sem, recv_sem,
+):
+    h = Here()
+    w = Wire(h, send_sem, recv_sem)
+    own = [
+        pltpu.make_async_copy(third, tokens.at[h.c], local.at[0]),
+        pltpu.make_async_copy(fout, wout.at[h.f], local.at[1]),
+    ]
+    for copy in own:
+        copy.start()
+    greet(near_devices(h))
+    gather = ClipGather(
+        w,
+        lambda c, half: tokens.at[c, pl.ds(128 * half, 128), :],
+        0,
+        lambda half: third.at[pl.ds(128 * half, 128), :],
+    )
+    gather.begin()
+    z_gather = ZGather(w, lambda f: wout.at[f], 6, fout)
+    z_gather.step(1)
+    z_gather.relay(0)
+    for copy in own:
+        copy.wait()
+
+    def hidden(c):
+        for part in range(2):
+            rows = pl.ds(128 * part, 128)
+            pre = dot(tokens[c, rows, :], win[...].reshape(1024, 1024), (1, 0))
+            cdf = 0.5 * (1.0 + lax.erf(pre * (0.5**0.5)))
+            inner[c, rows, :] = (pre * cdf).astype(BF16)
+            slope[c, rows, :] = cdf + pre * jnp.exp(-0.5 * pre * pre) * 0.3989422804014327
+
+    def hidden_back(c):
+        g_inner = dot(grad[c], wout[...].reshape(1024, 1024), (1, 1))
+        g_pre[c] = (g_inner * slope[c]).astype(BF16)
+        terms[c] = dot(g_pre[c], win[...].reshape(1024, 1024), (1, 1)).astype(BF16)
+
+    def out_terms(c):
+        o_out[c] = dot(inner[c], wout[...].reshape(1024, 1024), (1, 0)).astype(BF16)
+
+    hidden(h.c)
+    z_gather.step(2)
+    gather.middle()
+    gather.near()
+    z_gather.step(3)
+    hidden(h.cx)
+    z_gather.step(4)
+    for d in range(1, 4):
+        z_gather.relay(d)
+    hidden(h.cy)
+    gather.end()
+    hidden(h.cd)
+    z_gather.end()
+    scatter = ClipScatter(
+        w,
+        lambda c, half: terms.at[c, pl.ds(128 * half, 128), :],
+        [slots.at[i] for i in range(6)],
+        16,
+    )
+    hidden_back(h.cd)
+    scatter.begin(0)
+    hidden_back(h.cx)
+    hidden_back(h.cy)
+    scatter.begin(1)
+    scatter.middle()
+    hidden_back(h.c)
+
+    def weight_terms(i, _):
+        columns = pl.ds(pl.multiple_of(i * 256, 256), 256)
+        tall = (1024, 1024)
+        out = dot(inner[:, :, columns].reshape(1024, 256), grad[...].reshape(tall), (0, 0))
+        o_terms[pl.ds(2 * i, 2), 0:128, :] = out.astype(BF16).reshape(2, 128, 1024)
+        out = dot(tokens[:, :, columns].reshape(1024, 256), g_pre[...].reshape(tall), (0, 0))
+        o_terms[:, pl.ds(pl.multiple_of(128 + 32 * i, 32), 32), :] = out.astype(BF16).reshape(8, 32, 1024)
+        return 0
+
+    lax.fori_loop(0, 4, weight_terms, 0)
+    for c in range(4):
+        out_terms(c)
+    scatter.end()
+    for half in range(2):
+        o_third[128 * half : 128 * half + 128, :] = scatter.total(half)
+    w.drain()
+
+
+def feed(third, grad, win, fout):
+    full = (4, 256, 1024)
+    return comm_call(
+        feed_body,
+        (shape((256, 1024), F32), shape(full), shape((8, 256, 1024))),
+        [HBM, VMEM, VMEM, HBM],
+        (VMEM,) * 3,
+        [
+            pltpu.VMEM(full, BF16),
+            pltpu.VMEM((8, 128, 1024), BF16),
+            pltpu.VMEM(full, BF16),
+            pltpu.VMEM(full, F32),
+            pltpu.VMEM(full, BF16),
+            pltpu.VMEM(full, BF16),
+            pltpu.VMEM((6, 128, 1024), BF16),
+            pltpu.SemaphoreType.DMA((2,)),
+        ],
+        32,
+        22,
+        3,
+    )(third, grad, win, fout)
 
 
 def norm_back(xhat, scale, grad, gain):
@@ -970,9 +1228,30 @@
 
 
 def middle_back_body(
-    g_third, g_out, after_cross, after_self, second, query_ref, crossed, att, square, tkv, text_bias, params,
-    o_after_self, o_square, o_att, o_text, o_norm, g_crossed, g_query,
+    g_third, g_out, after_cross, after_self, second, query_ref, crossed, att, square, tkv, text_bias, params, out_terms,
+    o_after_self, o_square, o_heads, o_text, o_norm, o_output,
+    g_crossed, g_query, g_att, g_text, slots, sums, from_sib, from_z, local, send_sem, recv_sem,
 ):
+    h = Here()
+    w = Wire(h, send_sem, recv_sem)
+    greet(frame_others(h) + clip_others(h)[:2])
+    scatter = ClipScatter(
+        w,
+        lambda c, half: out_terms.at[c, pl.ds(128 * half, 128), :],
+        [slots.at[i] for i in range(6)],
+        16,
+    )
+    scatter.begin()
+
+    def columns_of(f):
+        return pl.ds(pl.multiple_of(lax.rem(f, 4) * 256, 256), 256)
+
+    def part_of(f):
+        return g_att.at[lax.div(f, 4), :, columns_of(f)]
+
+    def text_part(f):
+        return g_text.at[lax.div(f, 4), :, :, columns_of(f)]
+
     def put(which, value):
         o_square[:, 32 * which : 32 * which + 32, :] = value.astype(BF16).reshape(32, 32, 1024)
 
@@ -998,8 +1277,12 @@
             g_logits = (probs * (g_probs - row_dot)).astype(BF16)
             part = dot(g_logits, keys, (1, 0))
             g_query[rows, columns] = (pick_heads(part, lane_head) * (HD**-0.5)).astype(BF16)
-            o_text[clip, 0, :, columns] = dot(g_logits, stacked, (0, 0)).astype(BF16)
-            o_text[clip, 1, :, columns] = dot(probs.astype(BF16), g_stacked, (0, 0)).astype(BF16)
+            g_text[clip, 0, :, columns] = dot(g_logits, stacked, (0, 0)).astype(BF16)
+            g_text[clip, 1, :, columns] = dot(probs.astype(BF16), g_stacked, (0, 0)).astype(BF16)
+        if clip == 0:
+            scatter.middle()
+    for z in range(4):
+        w.send(text_part(2 * z + 1 - h.core), from_sib.at[z], 8 + z, h.c, h.sib)
     put(1, dot(second[...], g_query[...], (0, 0)))
     grad = dot(g_query[...], square_of(square, 1), (1, 1))
     xhat, scale = norm_parts(after_self[...])
@@ -1008,113 +1291,11 @@
     g_after_self = g_after_cross + norm_back(xhat, scale, grad, params[1:2, :])
     o_after_self[...] = g_after_self
     branch = g_after_self.astype(BF16)
-    put(0, dot(att[...].reshape(256, 1024), branch, (0, 0)))
-    o_att[...] = dot(branch, square_of(square, 0), (1, 1)).astype(BF16).reshape(2, 128, 1024)
-
-
-def middle_back(*args):
-    return pl.pallas_call(
-        middle_back_body,
-        out_shape=(
-            shape((256, 1024), F32),
-            shape((32, 96, 1024)),
-            shape((2, 128, 1024)),
-            shape((2, 2, 128, 1024)),
-            shape((8, 1024), F32),
-        ),
-        in_specs=[VMEM] * 12,
-        out_specs=(VMEM,) * 5,
-        scratch_shapes=[pltpu.VMEM((256, 1024), BF16)] * 2,
-        compiler_params=pltpu.CompilerParams(vmem_limit_bytes=60 * 2**20),
-    )(*args)
-
-
-def clip_gather_body(block, out, local, send_sem, recv_sem):
-    h = Here()
-    w = Wire(h, send_sem, recv_sem)
-    greet(clip_others(h)[:2])
-    copy = pltpu.make_async_copy(block, out.at[h.c], local.at[0])
-    copy.start()
-    copy.wait()
-    gather = ClipGather(w, lambda c, half: out.at[c, pl.ds(128 * half, 128), :], 0)
-    gather.begin()
-    gather.middle()
-    gather.near()
-    gather.end()
-    w.drain()
-
-
-def clip_gather(block):
-    return comm_call(
-        clip_gather_body,
-        shape((4, 256, 1024)),
-        [HBM],
-        HBM,
-        [pltpu.SemaphoreType.DMA((1,))],
-        6,
-        6,
-        3,
-    )(block)
-
-
-def clip_scatter_body(first, second, o_first, o_second, slots, send_sem, recv_sem):
-    h = Here()
-    w = Wire(h, send_sem, recv_sem)
-    greet(clip_others(h)[:2])
-    scatters = []
-    for i, terms in enumerate((first, second)):
-        scatters.append(
-            ClipScatter(
-                w,
-                lambda c, half, terms=terms: terms.at[c, pl.ds(128 * half, 128), :],
-                [slots.at[i, j] for j in range(6)],
-                6 * i,
-            )
-        )
-    for one in scatters:
-        one.begin()
-    for one in scatters:
-        one.middle()
-    for one, out in zip(scatters, (o_first, o_second)):
-        one.end()
-        for half in range(2):
-            out[128 * half : 128 * half + 128, :] = one.total(half)
-    w.drain()
-
-
-def clip_scatter(first, second):
-    return comm_call(
-        clip_scatter_body,
-        (shape((256, 1024), F32),) * 2,
-        [VMEM] * 2,
-        (VMEM,) * 2,
-        [pltpu.VMEM((2, 6, 128, 1024), BF16)],
-        12,
-        12,
-        4,
-    )(first, second)
-
-
-def forth_body(g_att, text, o_att, o_text, sums, from_sib, from_z, local, send_sem, recv_sem):
-    h = Here()
-    w = Wire(h, send_sem, recv_sem)
-    greet(frame_others(h))
-
-    def columns(f):
-        return pl.ds(pl.multiple_of(lax.rem(f, 4) * 256, 256), 256)
-
-    def part(f):
-        return g_att.at[lax.div(f, 4), :, columns(f)]
-
-    def text_part(f):
-        return text.at[lax.div(f, 4), :, :, columns(f)]
-
-    for z in range(4):
-        w.send(text_part(2 * z + 1 - h.core), from_sib.at[z], 8 + z, h.c, h.sib)
+    g_att[...] = dot(branch, square_of(square, 0), (1, 1)).astype(BF16).reshape(2, 128, 1024)
     for d in range(1, 8):
         f = h.step(d)
-        w.send(part(f), o_att.at[h.f], d - 1, h.c, f)
-    copy = pltpu.make_async_copy(part(h.f), o_att.at[h.f], local.at[0])
+        w.send(part_of(f), o_heads.at[h.f], d - 1, h.c, f)
+    copy = pltpu.make_async_copy(part_of(h.f), o_heads.at[h.f], local.at[0])
     copy.start()
     for z in range(4):
         w.arrived(from_sib.at[z], 8 + z)
@@ -1122,6 +1303,11 @@
         sums[z] = (mine[...].astype(F32) + from_sib[z].astype(F32)).astype(BF16)
     for d in range(1, 4):
         w.send(sums.at[lax.rem(h.z + d, 4)], from_z.at[d - 1], 11 + d, h.c, h.zstep(d))
+    put(0, dot(att[...].reshape(256, 1024), branch, (0, 0)))
+    scatter.end()
+    for half in range(2):
+        rows = pl.ds(128 * half, 128)
+        o_output[rows, :] = (after_cross[rows, :] + scatter.total(half)).astype(BF16)
     for d in range(1, 4):
         w.arrived(from_z.at[d - 1], 11 + d)
     total = sums[h.z].astype(F32)
@@ -1129,28 +1315,40 @@
         total = total + from_z[d].astype(F32)
     o_text[...] = total.astype(BF16)
     for d in range(1, 8):
-        w.arrived(o_att.at[lax.rem(h.f + 8 - d, 8)], d - 1)
+        w.arrived(o_heads.at[lax.rem(h.f + 8 - d, 8)], d - 1)
     copy.wait()
     w.drain()
 
 
-def give_forth(g_att, text):
-    block = (2, 128, 256)
+def middle_back(*args):
+    rows, block = (256, 1024), (2, 128, 256)
     return comm_call(
-        forth_body,
-        (shape((8, 128, 256)), shape(block)),
-        [VMEM] * 2,
-        (VMEM,) * 2,
+        middle_back_body,
+        (
+            shape(rows, F32),
+            shape((32, 96, 1024)),
+            shape((8, 128, 256)),
+            shape(block),
+            shape((8, 1024), F32),
+            shape(rows),
+        ),
+        [VMEM] * 13,
+        (VMEM,) * 6,
         [
+            pltpu.VMEM(rows, BF16),
+            pltpu.VMEM(rows, BF16),
+            pltpu.VMEM((2, 128, 1024), BF16),
+            pltpu.VMEM((2, 2, 128, 1024), BF16),
+            pltpu.VMEM((6, 128, 1024), BF16),
             pltpu.VMEM((4,) + block, BF16),
             pltpu.VMEM((4,) + block, BF16),
             pltpu.VMEM((3,) + block, BF16),
             pltpu.SemaphoreType.DMA((1,)),
         ],
-        16,
-        16,
-        5,
-    )(g_att, text)
+        24,
+        24,
+        4,
+    )(*args)
 
 
 def last_body(
@@ -1278,7 +1476,7 @@
         ],
         64,
         48,
-        6,
+        5,
     )(first, square, cols, text)
 
 
@@ -1305,71 +1503,43 @@
 ):
     frame = lax.axis_index("frame")
     pair = frame // 4
-    w5 = jnp.concatenate([jnp.moveaxis(self_qkv, 1, 0), jnp.moveaxis(cross_qkv, 1, 0)[1:]], axis=0)
-    norms = jnp.concatenate([ln_gain, ln_bias], axis=0).reshape(1, 192)
-    square_here = jnp.concatenate(
-        [self_out, cross_qkv[:, 0], cross_out, jnp.pad(norms, ((0, 15), (0, 832)))], axis=0
-    )
-    hid_all, w_all, square_all, grad_all, fin_all = fetch(
-        hidden_in, w5, square_here, out_grad.reshape(256, 1024), ffn_in
-    )
-    square = square_all.reshape(32, 112, 1024)
-    params = square[:, 96, :192].reshape(32, 6, 32).transpose(1, 0, 2).reshape(6, 1024).astype(F32)
-    params = jnp.pad(params, ((0, 2), (0, 0)))
-    weights = w_all.reshape(5, 1024, 256)
-    ffn_w_out = lax.all_gather(ffn_out, "frame", axis=0, tiled=True)
-    ffn_w_in = (
-        lax.all_gather(fin_all, "frame", axis=0).transpose(1, 0, 2, 3).reshape(1024, 1024)
-    )
-    clip_x = hid_all.reshape(1024, 1024).astype(F32)
-    first_hat, first_scale = norm_parts(clip_x)
-    first_low = (first_hat * params[0:1] + params[3:4]).astype(BF16)
-    query, key, value = (matmul(first_low, weights[i]).astype(BF16) for i in range(3))
+    norms = jnp.concatenate([ln_gain, ln_bias], axis=0)
+    placed = lax.dynamic_update_slice(jnp.zeros((16, 256), BF16), norms, (0, 32 * (frame % 4)))
+    cols_a = jnp.concatenate(
+        [jnp.moveaxis(self_qkv, 1, 0).reshape(96, 1024), jnp.tile(placed, (1, 4))], axis=0
+    )
+    cols_b = jnp.moveaxis(cross_qkv, 1, 0)[1:].reshape(64, 1024)
+    square_here = jnp.concatenate([self_out, cross_qkv[:, 0], cross_out], axis=0)
     columns = jnp.arange(1024, dtype=jnp.int32)
     my_len = lax.dynamic_slice_in_dim(clip_len, pair, 1, 0)
     my_mask = lax.dynamic_slice_in_dim(frame_mask, pair, 1, 0)[0]
     bias = jnp.where((columns < my_len) & (my_mask > 0), 0.0, NEG).astype(F32)
     bias = jnp.broadcast_to(bias[:, None], (1024, 128))
-    att_heads, lse = attend(my_len, bias, query, key, value)
+    (
+        hid_all, first_low, query, key, value, att_heads, lse, w_a, w_b, params, att, tkv, square, fin_all
+    ) = front(my_len, bias, text_states, hidden_in, cols_a, cols_b, square_here, ffn_in)
+    square = square.reshape(32, 96, 1024)
+    weights = [w_a[:, :, 32 * j : 32 * j + 32].reshape(1024, 256) for j in range(3)]
+    weights += [w_b[:, :, 32 * j : 32 * j + 32].reshape(1024, 256) for j in range(2)]
+    first_hat, _ = norm_parts(hid_all.reshape(1024, 1024).astype(F32))
     my_text = lax.dynamic_slice_in_dim(text_states, pair, 1, 0)[0]
-    text_kv = jnp.stack([matmul(my_text, weights[3]), matmul(my_text, weights[4])]).astype(BF16)
-    att, tkv = give_back(att_heads.reshape(8, 128, 256), text_kv)
     slots = jnp.arange(128, dtype=jnp.int32)
     text_ok = (slots[None] < text_len[:, None]) & ((text_mask > 0) | (slots[None] == 0))
     text_bias = jnp.where(text_ok, 0.0, NEG).astype(F32)
-    after_self, second, cross_query, crossed, after_cross, third = middle(
-        hidden_in, att, square, tkv, text_bias, params
-    )
-    third_all = clip_gather(third).reshape(1024, 1024)
-    grad_tokens = grad_all.reshape(1024, 1024)
-    pre_act = matmul(third_all, ffn_w_in)
-    activated, gelu_pull = jax.vjp(activate, pre_act)
-    inner = activated.astype(BF16)
-    out_terms = matmul(inner, ffn_w_out).astype(BF16)
-    (grad_pre,) = gelu_pull(lax.dot_general(grad_tokens, ffn_w_out, (((1,), (1,)), ((), ())), preferred_element_type=F32))
-    grad_pre = grad_pre.astype(BF16)
-    third_terms = lax.dot_general(grad_pre, ffn_w_in, (((1,), (1,)), ((), ())), preferred_element_type=F32).astype(BF16)
-    out_sum, third_sum = clip_scatter(out_terms.reshape(4, 256, 1024), third_terms.reshape(4, 256, 1024))
-    output = (after_cross + out_sum).astype(BF16).reshape(2, 128, 1024)
-    g_ffn_out = lax.dot_general(inner, grad_tokens, (((0,), (0,)), ((), ())), preferred_element_type=F32).astype(BF16)
-    g_ffn_in = lax.dot_general(third_all, grad_pre, (((0,), (0,)), ((), ())), preferred_element_type=F32).astype(BF16)
-    ffn_terms = jnp.concatenate(
-        [
-            g_ffn_out.reshape(8, 128, 1024),
-            g_ffn_in.reshape(4, 8, 32, 1024).transpose(1, 0, 2, 3).reshape(8, 128, 1024),
-        ],
-        axis=1,
-    )
+    after_self, second, cross_query, crossed, after_cross, third, grad_all, ffn_w_in = middle(
+        hidden_in, att, square, tkv, text_bias, params, out_grad.reshape(256, 1024), fin_all
+    )
+    third_sum, out_terms, ffn_terms = feed(third, grad_all, ffn_w_in, ffn_out)
     ffn_sum = lax.psum_scatter(ffn_terms, "frame", scatter_dimension=0, tiled=True)[0]
     grad_ffn_out = ffn_sum[:128].astype(F32)
     grad_ffn_in = lax.all_to_all(
         ffn_sum[128:].reshape(4, 32, 1024), "clip", split_axis=0, concat_axis=2, tiled=True
     )[0].astype(F32)
-    g_after_self, g_square, g_att, g_text, g_norms = middle_back(
+    g_after_self, g_square, g_heads, g_tkv, g_norms, output = middle_back(
         third_sum, out_grad, after_cross, after_self, second, cross_query, crossed, att, square, tkv,
-        text_bias, params,
-    )
-    g_heads, g_tkv = give_forth(g_att, g_text)
+        text_bias, params, out_terms,
+    )
+    output = output.reshape(2, 128, 1024)
     g_query, g_key, g_value = attend_back(
         my_len, bias, query, key, value, att_heads, lse, g_heads.reshape(1024, 256)
     )

time: 538 us -> 415 us (0.77)
  Pallas kernels: 407 us -> 343 us
  matrix products: 49.8 us -> 9.68 us
  local copies, waits for them, and re-layouts: 26.5 us -> 16.8 us
  other arithmetic: 24 us -> 15.1 us
    pallas_call x8 -> x4, Pallas kernels: 308 us -> 240 us  [the longest x1 96.4 us: front(): comm_call(front_body, (shape((8, 128, 1024)), shape((1024, 1024)), shape(...]
    dot_general x11 -> x0, matrix products: 38.1 us -> none  [the longest x1 14.1 us: on_device_fast(): lax.dot_general(grad_tokens, ffn_w_out, (((1,), (1,)), ((), ())), preferr...]
  transfers between devices with their start and end apart: 4 -> 2, of which waited for: 1 -> 1; matrix products, arithmetic and copies ran while one was open for 12% -> 6% of each run, Pallas kernels for 54% -> 40%
where the time goes in v2:
time: 415 us; the launch traced here: 408 us
  Pallas kernels  343 us (83%)
  local copies, waits for them, and re-layouts  16.8 us (4%)
  other arithmetic  15.1 us (4%)
  between operations  14.7 us (4%)
  matrix products  9.68 us (2%)
  waiting for transfers between devices  4.94 us (1%)
    pallas_call x1, Pallas kernels, front(): comm_call(front_body, (shape((8, 128, 1024)), shape((1024, 1024)), shape(...  96.4 us
    pallas_call x1, Pallas kernels, last_sums(): comm_call(last_body, (shape((2, 128, 1024), F32), shape((96, 1024), F32),...  88.4 us
    pallas_call x1, Pallas kernels, middle_back(): comm_call(middle_back_body, (shape(rows, F32), shape((32, 96, 1024)), sha...  58.2 us
    pallas_call x1, Pallas kernels, feed(): comm_call(feed_body, (shape((256, 1024), F32), shape(full), shape((8, 256...  52.4 us
    pallas_call x1, Pallas kernels, middle(): comm_call(middle_body, (shape(rows, F32), shape(rows), shape(rows), shape...  32.7 us
    pallas_call x1, Pallas kernels, attend_back(): pl.pallas_call(attend_back_body, out_shape=(shape((1024, 256)),) * 3, in_...  15.3 us
  transfers between devices with their start and end apart: 2, of which 1 were waited for; matrix products, arithmetic and copies ran while one was open for 6% of the time, Pallas kernels for 40%

profile of v2, /device:TPU:0, one launch (start us, length us, event | category | flops | bytes accessed | tf_op | source)
XLA Modules:
  0.0 408.0 jit_solution(18309302638547884043)
XLA Ops:
  7.2 0.0 reduce-scatter.2.cloned.1.call-start
  7.3 0.7 compare_reduce_fusion
  8.0 1.2 dynamic_slice.9.length
  9.2 0.7 pad_maximum_fusion.4
  9.9 0.3 dynamic_update_slice.6
  10.3 0.8 slice_bitcast_fusion.7
  11.2 1.6 slice.117
  12.7 0.6 fusion.31
  13.4 1.6 pad_maximum_fusion.2.cols_a
  15.0 1.6 pad_maximum_fusion.3.square
  16.6 1.3 and_select_fusion.text_bias
  17.9 1.0 broadcast_in_dim.20.bias
  18.9 96.4 %shard_map.230 = (bf16[8,128,1024]{2,1,0:T(8,128)(2,1)}, bf16[1024,1024]{1,0:T(8,128)(2,1)}, bf16[1024,256]{1,0:T(8,128)(2,1)}, bf16[1024,256]{1,0:T(8,128)(2,1)...) custom-call(s32[1]{0:T(128)} %dynamic_slice.9.length, ...), custom_call_target="tpu_custom_call" | custom-call | tf_op jit(solution)/shard_map/pallas_call | solution.py:914
  115.3 32.7 %shard_map.231 = (f32[256,1024]{1,0:T(8,128)}, bf16[256,1024]{1,0:T(8,128)(2,1)}, bf16[256,1024]{1,0:T(8,128)(2,1)}, bf16[256,1024]{1,0:T(8,128)(2,1)}, f32[256,...) custom-call(bf16[2,128,1024]{2,1,0:T(8,128)(2,1)} %hid.3, ...), custom_call_target="tpu_custom_call" | custom-call | tf_op jit(solution)/shard_map/pallas_call | solution.py:1086
  148.0 52.4 %shard_map.232 = (f32[256,1024]{1,0:T(8,128)}, bf16[4,256,1024]{2,1,0:T(8,128)(2,1)}, bf16[8,256,1024]{2,1,0:T(8,128)(2,1)}) custom-call(bf16[256,1024]{1,0:T(8,128)(2,1)} %get-tuple-element.55.third, bf16[4,256,1024]{2,1,0:T(8,128)(2,1)} %get-tuple-element.56.grad, bf16[4,8,32,1024]{3,2,1,0:T(8,128)(2,1)} %get-tuple-element.57.win, bf16[128,1024]{1,0:T(8,128)(2,1)} %fout.1), custom_call_target="tpu_custom_call" | custom-call | tf_op jit(solution)/shard_map/pallas_call | solution.py:1200
  200.4 0.8 slice.104
  201.2 0.2 copy-done.5
  201.5 0.2 copy.28
  201.6 58.2 %shard_map.233 = (f32[256,1024]{1,0:T(8,128)}, bf16[32,96,1024]{2,1,0:T(8,128)(2,1)}, bf16[8,128,256]{2,1,0:T(8,128)(2,1)}, bf16[2,128,256]{2,1,0:T(8,128)(2,1)}...) custom-call(f32[256,1024]{1,0:T(8,128)} %get-tuple-element.58.g_third, bf16[2,128,1024]{2,1,0:T(8,128)(2,1)} %g_out.1, ...), custom_call_target="tpu_custom_call" | custom-call | tf_op jit(solution)/shard_map/pallas_call | solution.py:1325
  259.8 15.3 %shard_map.234 = (bf16[1024,256]{1,0:T(8,128)(2,1)}, bf16[1024,256]{1,0:T(8,128)(2,1)}, bf16[1024,256]{1,0:T(8,128)(2,1)}) custom-call(s32[1]{0:T(128)} %dynamic_slice.9.length, f32[1024,128]{1,0:T(8,128)} %broadcast_in_dim.20.bias, bf16[1024,256]{1,0:T(8,128)(2,1)} %get-tuple-element.67.q_ref, bf16[1024,256]{1,0:T(8,128)(2,1)} %get-tuple-element.68.k_ref, ...), custom_call_target="tpu_custom_call" | custom-call | tf_op jit(solution)/shard_map/pallas_call | solution.py:990
  275.1 1.9 convolution_convert_fusion.2
  277.1 0.8 convolution_convert_fusion.1
  277.9 0.2 copy-done.8
  278.1 0.8 convolution_convert_fusion
  278.9 0.1 copy-done.12
  279.0 0.3 fusion.8
  279.3 0.3 fusion.10
  279.6 0.3 copy.29
  279.9 1.3 copy-done.1
  281.2 0.3 convert_reduce_fusion
  281.5 0.7 multiply_reduce_fusion
  282.2 1.0 fusion.34
  283.2 0.7 fusion.39
  284.0 0.3 copy-done.9
  284.3 0.7 fusion.38
  285.0 2.9 fusion.33
  288.0 0.1 stack.54
  288.0 0.1 stack.57
  288.1 0.1 slice_reduce_fusion
  288.2 0.1 stack.55
  288.3 0.1 stack.56
  288.3 0.1 stack.58
  288.4 0.1 stack.59
  288.5 0.2 stack.50
  288.7 1.8 fusion.4.cols
  290.5 0.3 fusion.24
  290.8 1.0 fusion.11.text
  291.8 88.4 %shard_map.235 = (f32[2,128,1024]{2,1,0:T(8,128)}, f32[96,1024]{1,0:T(8,128)}, f32[160,1024]{1,0:T(8,128)}, f32[16,128]{1,0:T(8,128)}, bf16[2,16,1024]{2,1,0:T(8,128)(2,1)}) custom-call(bf16[8,128,1024]{2,1,0:T(8,128)(2,1)} %bitcast.117, bf16[4,8,96,1024]{3,2,1,0:T(8,128)(2,1)} %bitcast.118, bf16[4,8,176,256]{3,2,1,0:T(8,128)(2,1)} %fusion.4.cols, ...), custom_call_target="tpu_custom_call" | custom-call | tf_op jit(solution)/shard_map/pallas_call | solution.py:1452
  380.2 1.9 fusion.36
  382.1 1.3 slice_bitcast_fusion.2
  383.4 0.8 pad_maximum_fusion.1
  384.2 0.8 pad_maximum_fusion
  384.9 0.1 convert_reduce_fusion.1
  385.1 0.3 fusion.19
  385.4 0.4 multiply_reduce_fusion.1
  385.8 1.2 fusion.18
  387.0 2.0 fusion.20
  389.1 3.4 all-to-all-start
  392.5 0.6 fusion.37
  393.1 4.9 %all-to-all-done = bf16[4,32,1024]{2,1,0:T(8,128)(2,1)S(1)} async-done(((bf16[4,32,1024]{2,1,0:T(8,128)(2,1)}), bf16[4,32,1024]{2,1,0:T(8,128)(2,1)S(1)}, u32[]{:S(2)}, u32[]{:S(2)}) %all-to-all-start) | async-done | bytes 262176 | tf_op jit(solution)/shard_map/all_to_all | solution.py:1535
  398.1 0.3 copy.36
  398.4 1.1 copy.40
  399.5 0.8 copy.48
  400.3 0.6 copy.49
  (47 shorter events, 0.3 us)
Async XLA Ops:
  7.2 379.9 %reduce-scatter.2.cloned.1.call-start = ((), (), s32[]{:S(2)}) async-start(), calls=%async_computation.2 | async-start | bytes 4718592 | tf_op jit(solution)/shard_map/reduce_scatter | solution.py:1533
  200.4 1.1 copy-start.5
  259.8 15.3 %copy-start.16 = (bf16[1024,1024]{1,0:T(8,128)(2,1)S(1)}, bf16[1024,1024]{1,0:T(8,128)(2,1)}, u32[]{:S(2)}) copy-start(bf16[1024,1024]{1,0:T(8,128)(2,1)} %get-tuple-element.78) | copy-start | bytes 6291460
  275.1 1.9 copy-start.10
  277.0 1.0 copy-start.8
  278.1 0.9 copy-start.12
  279.6 1.6 copy-start.1
  279.8 2.4 copy-start.4
  279.9 2.4 copy-start.7
  283.2 1.0 copy-start.9
  285.0 3.1 copy-start.14
  288.7 1.8 copy-start.3
  380.2 4.7 %copy-start = (bf16[2,128,1024]{2,1,0:T(8,128)(2,1)S(1)}, bf16[2,128,1024]{2,1,0:T(8,128)(2,1)}, u32[]{:S(2)}) copy-start(bf16[2,128,1024]{2,1,0:T(8,128)(2,1)} %hid.3) | copy-start | bytes 1572868
  380.2 5.2 %copy-start.2 = (f32[2,128,1024]{2,1,0:T(8,128)S(1)}, f32[2,128,1024]{2,1,0:T(8,128)}, u32[]{:S(2)}) copy-start(f32[2,128,1024]{2,1,0:T(8,128)} %get-tuple-element.83) | copy-start | bytes 3145732
  382.1 3.7 copy-start.6
  385.8 6.7 %copy-start.15 = (f32[16,128]{1,0:T(8,128)S(1)}, f32[16,128]{1,0:T(8,128)}, u32[]{:S(2)}) copy-start(f32[16,128]{1,0:T(8,128)} %get-tuple-element.88) | copy-start | bytes 24580
  387.0 12.5 %copy-start.11 = (bf16[256,1024]{1,0:T(8,128)(2,1)S(1)}, bf16[256,1024]{1,0:T(8,128)(2,1)}, u32[]{:S(2)}) copy-start(bf16[256,1024]{1,0:T(8,128)(2,1)} %get-tuple-element.65) | copy-start | bytes 1572868
  387.0 13.3 %copy-start.13 = (bf16[2,16,1024]{2,1,0:T(8,128)(2,1)S(1)}, bf16[2,16,1024]{2,1,0:T(8,128)(2,1)}, u32[]{:S(2)}) copy-start(bf16[2,16,1024]{2,1,0:T(8,128)(2,1)} %get-tuple-element.133) | copy-start | bytes 196612
  389.1 8.9 %all-to-all-start = ((bf16[4,32,1024]{2,1,0:T(8,128)(2,1)}), bf16[4,32,1024]{2,1,0:T(8,128)(2,1)S(1)}, u32[]{:S(2)}, u32[]{:S(2)}) async-start(bf16[4,32,1024]{2,1,0:T(8,128)(2,1)} %bitcast.45), calls=%async_computation.1 | async-start | bytes 524288 | tf_op jit(solution)/shard_map/all_to_all | solution.py:1535
Sparse Core Ops, SparseCore 0:
  200.5 65.0 reduce-scatter.1

commit v3 on v2

--- a/solution.py
+++ b/solution.py
@@ -610,6 +610,87 @@
         first, second = (s[2], s[4]) if half == 0 else (s[5], s[3])
         own = self.parts(self.wire.here.c, half)
         return own[...].astype(F32) + first[...].astype(F32) + second[...].astype(F32)
+
+
+class ZScatter:
+    def __init__(self, wire, terms, near, far, tag):
+        self.wire, self.terms, self.near, self.far, self.tag = wire, terms, near, far, tag
+        self.open = []
+
+    def term(self, m):
+        pair = self.wire.here.pair
+        return self.terms.at[m + pair * (3 - 2 * m)]
+
+    def _start(self, go, src, dst, tag, f):
+        copy = self.wire.copy(src, dst, self.tag + tag, self.wire.here.c, f)
+        pl.when(go)(copy.start)
+        self.open.append((go, copy))
+
+    def begin(self):
+        h = self.wire.here
+        for i, m in enumerate((3, 2, 1)):
+            self._start(jnp.logical_not(h.is_gate), self.term(m), self.near.at[i], i, h.partner)
+
+    def step(self, s):
+        h, w = self.wire.here, self.wire
+        block, m, tag, to, f = (
+            (self.near.at[0], 3, 0, 0, h.far_gate),
+            (self.near.at[1], 2, 1, 1, h.far_gate),
+            (self.far.at[0], 0, 3, 0, h.partner),
+        )[s - 1]
+
+        @pl.when(h.is_gate)
+        def _():
+            w.arrived(block, self.tag + tag)
+            add_into(block, self.term(m))
+
+        self._start(h.is_gate, block, self.far.at[to], 3 + to, f)
+
+    def end(self):
+        h, w = self.wire.here, self.wire
+
+        @pl.when(h.is_gate)
+        def _():
+            w.arrived(self.near.at[2], self.tag + 2)
+            w.arrived(self.far.at[1], self.tag + 4)
+
+        @pl.when(jnp.logical_not(h.is_gate))
+        def _():
+            w.arrived(self.far.at[0], self.tag + 3)
+
+    def total(self, out):
+        h = self.wire.here
+        self.end()
+
+        @pl.when(h.is_gate)
+        def _():
+            others = self.near[2].astype(F32) + self.far[1].astype(F32)
+            out[...] = self.terms[h.z].astype(F32) + others
+
+        @pl.when(jnp.logical_not(h.is_gate))
+        def _():
+            out[...] = self.terms[h.z].astype(F32) + self.far[0].astype(F32)
+
+    def drain(self):
+        for go, copy in self.open:
+            pl.when(go)(copy.wait_send)
+
+
+class SiblingSum:
+    def __init__(self, wire, terms, inbox, sums, tag):
+        self.wire, self.terms, self.inbox, self.sums, self.tag = wire, terms, inbox, sums, tag
+
+    def begin(self):
+        h, w = self.wire.here, self.wire
+        for z in range(4):
+            w.send(self.terms(2 * z + 1 - h.core), self.inbox(z), self.tag + z, h.c, h.sib)
+
+    def end(self):
+        h, w = self.wire.here, self.wire
+        for z in range(4):
+            w.arrived(self.inbox(z), self.tag + z)
+            own, other = self.terms(2 * z + h.core), self.inbox(z)
+            self.sums(z)[...] = (own[...].astype(F32) + other[...].astype(F32)).astype(BF16)
 
 
 def add_into(into, other):
@@ -945,61 +1026,37 @@
     )(length, bias, text, hid, cols_a, cols_b, square, fin)
 
 
-def attend_back_body(
-    length, bias, q_ref, k_ref, v_ref, o_ref, lse_ref, g_ref, dq_ref, dk_ref, dv_ref, dq_t, k_t, dk, dv
-):
-    k_t[...] = k_ref[...].T
+def attend_back_rows(i, length, bias, q_ref, k_ref, v_ref, o_ref, lse_ref, g_ref, dq_ref, dq_t, k_t, dk, dv):
     lane_head = lax.broadcasted_iota(jnp.int32, (ROWS, 256), 1) // HD
-    dk[...] = jnp.zeros_like(dk)
-    dv[...] = jnp.zeros_like(dv)
-    for i in range(1024 // ROWS):
-        first, n = i * ROWS, (i + 1) * ROWS
-        q = q_ref[first:n, :] * jnp.asarray(HD**-0.5, BF16)
-        live = first + lax.broadcasted_iota(jnp.int32, (ROWS, 256), 0) < length[0]
-        g = jnp.where(live, g_ref[first:n, :], 0)
-        both = (g.astype(F32) * o_ref[first:n, :].astype(F32)).T
-        row_dots = jnp.concatenate(
-            [jnp.sum(both[HD * j : HD * j + HD], axis=0, keepdims=True) for j in range(4)], axis=0
-        )
-        lse = lse_ref[0:4, first:n]
-
-        def pick(rows, j):
-            at = lax.broadcasted_iota(jnp.int32, rows.shape, 0) == j
-            return jnp.sum(jnp.where(at, rows, 0), axis=0, keepdims=True)
-
-        def head(j, _):
-            q_head = jnp.where(lane_head == j, q, 0)
-            g_head = jnp.where(lane_head == j, g, 0)
-            scores = mask_scores(dot(k_ref[0:n, :], q_head, (1, 1)), bias, first, ROWS)
-            probs = jnp.exp(scores - pick(lse, j))
-            grads = dot(v_ref[0:n, :], g_head, (1, 1))
-            dlogits = (probs * (grads - pick(row_dots, j))).astype(BF16)
-            dv[0:n, :] += dot(probs.astype(BF16), g_head, (1, 0))
-            dk[0:n, :] += dot(dlogits, q_head, (1, 0))
-            at = pl.ds(pl.multiple_of(j * HD, HD), HD)
-            dq_t[at, :] = dot(k_t[at, 0:n], dlogits, (1, 0))
-            return 0
-
-        lax.fori_loop(0, 4, head, 0)
-        dq_ref[first:n, :] = (dq_t[...].T * (HD**-0.5)).astype(BF16)
-    dk_ref[...] = dk[...].astype(BF16)
-    dv_ref[...] = dv[...].astype(BF16)
-
-
-def attend_back(length, bias, q, k, v, o, lse, g):
-    return pl.pallas_call(
-        attend_back_body,
-        out_shape=(shape((1024, 256)),) * 3,
-        in_specs=[SMEM] + [VMEM] * 7,
-        out_specs=(VMEM,) * 3,
-        scratch_shapes=[
-            pltpu.VMEM((256, ROWS), F32),
-            pltpu.VMEM((256, 1024), BF16),
-            pltpu.VMEM((1024, 256), F32),
-            pltpu.VMEM((1024, 256), F32),
-        ],
-        compiler_params=pltpu.CompilerParams(vmem_limit_bytes=56 * 2**20),
-    )(length, bias, q, k, v, o, lse, g)
+    first, n = i * ROWS, (i + 1) * ROWS
+    q = q_ref[first:n, :] * jnp.asarray(HD**-0.5, BF16)
+    live = first + lax.broadcasted_iota(jnp.int32, (ROWS, 256), 0) < length[0]
+    g = jnp.where(live, g_ref[first:n, :], 0)
+    both = (g.astype(F32) * o_ref[first:n, :].astype(F32)).T
+    row_dots = jnp.concatenate(
+        [jnp.sum(both[HD * j : HD * j + HD], axis=0, keepdims=True) for j in range(4)], axis=0
+    )
+    lse = lse_ref[0:4, first:n]
+
+    def pick(rows, j):
+        at = lax.broadcasted_iota(jnp.int32, rows.shape, 0) == j
+        return jnp.sum(jnp.where(at, rows, 0), axis=0, keepdims=True)
+
+    def head(j, _):
+        q_head = jnp.where(lane_head == j, q, 0)
+        g_head = jnp.where(lane_head == j, g, 0)
+        scores = mask_scores(dot(k_ref[0:n, :], q_head, (1, 1)), bias, first, ROWS)
+        probs = jnp.exp(scores - pick(lse, j))
+        grads = dot(v_ref[0:n, :], g_head, (1, 1))
+        dlogits = (probs * (grads - pick(row_dots, j))).astype(BF16)
+        dv[0:n, :] += dot(probs.astype(BF16), g_head, (1, 0))
+        dk[0:n, :] += dot(dlogits, q_head, (1, 0))
+        at = pl.ds(pl.multiple_of(j * HD, HD), HD)
+        dq_t[at, :] = dot(k_t[at, 0:n], dlogits, (1, 0))
+        return 0
+
+    lax.fori_loop(0, 4, head, 0)
+    dq_ref[first:n, :] = (dq_t[...].T * (HD**-0.5)).astype(BF16)
 
 
 def square_of(square, which):
@@ -1109,8 +1166,8 @@
 
 
 def feed_body(
-    third, grad, win, fout, o_third, o_out, o_terms,
-    tokens, wout, inner, slope, g_pre, terms, slots, local, send_sem, recv_sem,
+    third, grad, win, fout, o_third, o_out, o_terms, o_sum,
+    tokens, wout, inner, slope, g_pre, terms, slots, out_w, inbox, sums, left, right, local, send_sem, recv_sem,
 ):
     h = Here()
     w = Wire(h, send_sem, recv_sem)
@@ -1169,39 +1226,57 @@
         [slots.at[i] for i in range(6)],
         16,
     )
+    sibling = SiblingSum(w, lambda f: out_w.at[f], lambda z: inbox.at[z], lambda z: sums.at[z], 22)
+    z_scatter = ZScatter(w, sums, left, right, 26)
+    tall = (1024, 1024)
+
+    def out_weight(i, _):
+        columns = pl.ds(pl.multiple_of(i * 256, 256), 256)
+        out = dot(inner[:, :, columns].reshape(1024, 256), grad[...].reshape(tall), (0, 0))
+        out_w[pl.ds(2 * i, 2)] = out.astype(BF16).reshape(2, 128, 1024)
+        return 0
+
+    def in_weight(i, _):
+        columns = pl.ds(pl.multiple_of(i * 256, 256), 256)
+        out = dot(tokens[:, :, columns].reshape(1024, 256), g_pre[...].reshape(tall), (0, 0))
+        o_terms[:, pl.ds(pl.multiple_of(32 * i, 32), 32), :] = out.astype(BF16).reshape(8, 32, 1024)
+        return 0
+
     hidden_back(h.cd)
     scatter.begin(0)
     hidden_back(h.cx)
     hidden_back(h.cy)
     scatter.begin(1)
+    lax.fori_loop(0, 4, out_weight, 0)
+    sibling.begin()
     scatter.middle()
     hidden_back(h.c)
-
-    def weight_terms(i, _):
-        columns = pl.ds(pl.multiple_of(i * 256, 256), 256)
-        tall = (1024, 1024)
-        out = dot(inner[:, :, columns].reshape(1024, 256), grad[...].reshape(tall), (0, 0))
-        o_terms[pl.ds(2 * i, 2), 0:128, :] = out.astype(BF16).reshape(2, 128, 1024)
-        out = dot(tokens[:, :, columns].reshape(1024, 256), g_pre[...].reshape(tall), (0, 0))
-        o_terms[:, pl.ds(pl.multiple_of(128 + 32 * i, 32), 32), :] = out.astype(BF16).reshape(8, 32, 1024)
-        return 0
-
-    lax.fori_loop(0, 4, weight_terms, 0)
-    for c in range(4):
-        out_terms(c)
+    sibling.end()
+    z_scatter.begin()
+    lax.fori_loop(0, 2, in_weight, 0)
+    z_scatter.step(1)
+    lax.fori_loop(2, 4, in_weight, 0)
+    out_terms(0)
+    z_scatter.step(2)
+    z_scatter.step(3)
+    out_terms(1)
+    out_terms(2)
+    out_terms(3)
     scatter.end()
     for half in range(2):
         o_third[128 * half : 128 * half + 128, :] = scatter.total(half)
+    z_scatter.total(o_sum)
     w.drain()
+    z_scatter.drain()
 
 
 def feed(third, grad, win, fout):
     full = (4, 256, 1024)
     return comm_call(
         feed_body,
-        (shape((256, 1024), F32), shape(full), shape((8, 256, 1024))),
+        (shape((256, 1024), F32), shape(full), shape((8, 128, 1024)), shape((128, 1024), F32)),
         [HBM, VMEM, VMEM, HBM],
-        (VMEM,) * 3,
+        (VMEM,) * 4,
         [
             pltpu.VMEM(full, BF16),
             pltpu.VMEM((8, 128, 1024), BF16),
@@ -1210,10 +1285,15 @@
             pltpu.VMEM(full, BF16),
             pltpu.VMEM(full, BF16),
             pltpu.VMEM((6, 128, 1024), BF16),
+            pltpu.VMEM((8, 128, 1024), BF16),
+            pltpu.VMEM((4, 128, 1024), BF16),
+            pltpu.VMEM((4, 128, 1024), BF16),
+            pltpu.VMEM((3, 128, 1024), BF16),
+            pltpu.VMEM((2, 128, 1024), BF16),
             pltpu.SemaphoreType.DMA((2,)),
         ],
+        48,
         32,
-        22,
         3,
     )(third, grad, win, fout)
 
@@ -1228,20 +1308,50 @@
 
 
 def middle_back_body(
-    g_third, g_out, after_cross, after_self, second, query_ref, crossed, att, square, tkv, text_bias, params, out_terms,
-    o_after_self, o_square, o_heads, o_text, o_norm, o_output,
-    g_crossed, g_query, g_att, g_text, slots, sums, from_sib, from_z, local, send_sem, recv_sem,
+    g_third, g_out, after_cross, after_self, second, query_ref, crossed, att, square, tkv, text_bias, params,
+    out_terms, in_terms,
+    o_after_self, o_square, o_zsquare, o_heads, o_text, o_norm, o_output, o_in,
+    g_crossed, g_query, g_att, g_text, slots, sums, from_sib, from_z,
+    i_inbox, i_sums, i_left, i_right, i_total, i_out, i_in,
+    g_square, s_inbox, s_sums, s_slots, local, send_sem, recv_sem,
 ):
     h = Here()
     w = Wire(h, send_sem, recv_sem)
-    greet(frame_others(h) + clip_others(h)[:2])
+    T_HEADS, T_TSIB, T_TZ, T_OUT, T_IN, T_IZ, T_IC, T_SQ = 0, 7, 11, 14, 20, 24, 30, 33
+    greet(frame_others(h) + clip_others(h))
     scatter = ClipScatter(
         w,
         lambda c, half: out_terms.at[c, pl.ds(128 * half, 128), :],
         [slots.at[i] for i in range(6)],
-        16,
+        T_OUT,
     )
     scatter.begin()
+    in_sibling = SiblingSum(
+        w, lambda f: in_terms.at[f], lambda z: i_inbox.at[z], lambda z: i_sums.at[z], T_IN
+    )
+    in_scatter = ZScatter(w, i_sums, i_left, i_right, T_IZ)
+    in_sibling.begin()
+
+    def square_sums(which):
+        sibling = SiblingSum(
+            w,
+            lambda f: g_square.at[which, :, f],
+            lambda z: s_inbox.at[which, z],
+            lambda z: s_sums.at[which, z],
+            T_SQ + 10 * which,
+        )
+        clip = ClipScatter(
+            w,
+            lambda c, half: s_sums.at[which, :, c, pl.ds(16 * half, 16), :],
+            [s_slots.at[which, i] for i in range(6)],
+            T_SQ + 10 * which + 4,
+        )
+        return sibling, clip
+
+    squares = [square_sums(0), square_sums(1)]
+
+    def put(ref, value):
+        ref[...] = value.astype(BF16).reshape(4, 8, 32, 1024)
 
     def columns_of(f):
         return pl.ds(pl.multiple_of(lax.rem(f, 4) * 256, 256), 256)
@@ -1251,18 +1361,19 @@
 
     def text_part(f):
         return g_text.at[lax.div(f, 4), :, :, columns_of(f)]
-
-    def put(which, value):
-        o_square[:, 32 * which : 32 * which + 32, :] = value.astype(BF16).reshape(32, 32, 1024)
 
     xhat, scale = norm_parts(after_cross[...])
     grad = g_third[...]
     o_norm[0:1, :] = jnp.sum(grad * xhat, axis=0, keepdims=True)
     o_norm[1:2, :] = jnp.sum(grad, axis=0, keepdims=True)
     g_after_cross = g_out[...].reshape(256, 1024).astype(F32) + norm_back(xhat, scale, grad, params[2:3, :])
+    o_after_self[...] = g_after_cross
     branch = g_after_cross.astype(BF16)
-    put(2, dot(crossed[...], branch, (0, 0)))
     g_crossed[...] = dot(branch, square_of(square, 2), (1, 1)).astype(BF16)
+    put(g_square.at[1], dot(crossed[...], branch, (0, 0)))
+    squares[1][0].begin()
+    in_sibling.end()
+    in_scatter.begin()
     lane_head = lax.broadcasted_iota(jnp.int32, (128, 256), 1) // HD
     for clip in range(2):
         for group in range(4):
@@ -1281,59 +1392,86 @@
             g_text[clip, 1, :, columns] = dot(probs.astype(BF16), g_stacked, (0, 0)).astype(BF16)
         if clip == 0:
             scatter.middle()
-    for z in range(4):
-        w.send(text_part(2 * z + 1 - h.core), from_sib.at[z], 8 + z, h.c, h.sib)
-    put(1, dot(second[...], g_query[...], (0, 0)))
+            in_scatter.step(1)
+    in_scatter.step(2)
+    squares[1][0].end()
+    squares[1][1].begin()
+    text_sibling = SiblingSum(
+        w, text_part, lambda z: from_sib.at[z], lambda z: sums.at[z], T_TSIB
+    )
+    text_sibling.begin()
     grad = dot(g_query[...], square_of(square, 1), (1, 1))
     xhat, scale = norm_parts(after_self[...])
     o_norm[2:3, :] = jnp.sum(grad * xhat, axis=0, keepdims=True)
     o_norm[3:4, :] = jnp.sum(grad, axis=0, keepdims=True)
-    g_after_self = g_after_cross + norm_back(xhat, scale, grad, params[1:2, :])
+    o_norm[4:8, :] = jnp.zeros((4, 1024), F32)
+    g_after_self = o_after_self[...] + norm_back(xhat, scale, grad, params[1:2, :])
     o_after_self[...] = g_after_self
     branch = g_after_self.astype(BF16)
     g_att[...] = dot(branch, square_of(square, 0), (1, 1)).astype(BF16).reshape(2, 128, 1024)
-    for d in range(1, 8):
+    for d in (4, 2, 6, 3, 5, 1, 7):
         f = h.step(d)
-        w.send(part_of(f), o_heads.at[h.f], d - 1, h.c, f)
+        w.send(part_of(f), o_heads.at[h.f], T_HEADS + d - 1, h.c, f)
     copy = pltpu.make_async_copy(part_of(h.f), o_heads.at[h.f], local.at[0])
     copy.start()
-    for z in range(4):
-        w.arrived(from_sib.at[z], 8 + z)
-        mine = text_part(2 * z + h.core)
-        sums[z] = (mine[...].astype(F32) + from_sib[z].astype(F32)).astype(BF16)
+    in_scatter.step(3)
+    put(g_square.at[0], dot(second[...], g_query[...], (0, 0)))
+    squares[0][0].begin()
+    text_sibling.end()
     for d in range(1, 4):
-        w.send(sums.at[lax.rem(h.z + d, 4)], from_z.at[d - 1], 11 + d, h.c, h.zstep(d))
-    put(0, dot(att[...].reshape(256, 1024), branch, (0, 0)))
+        w.send(sums.at[lax.rem(h.z + d, 4)], from_z.at[d - 1], T_TZ + d - 1, h.c, h.zstep(d))
+    squares[1][1].middle()
+    put(o_square, dot(att[...].reshape(256, 1024), branch, (0, 0)))
+    squares[0][0].end()
+    squares[0][1].begin()
+    in_scatter.total(i_total)
+    i_out[...] = i_total[...].astype(BF16).reshape(4, 32, 1024)
+    for i, (c, f) in enumerate(clip_others(h)):
+        w.send(i_out.at[c], i_in.at[h.c], T_IC + i, c, f)
+    i_in[h.c] = i_out[h.c]
     scatter.end()
     for half in range(2):
         rows = pl.ds(128 * half, 128)
         o_output[rows, :] = (after_cross[rows, :] + scatter.total(half)).astype(BF16)
+    squares[0][1].middle()
+    for which in (1, 0):
+        squares[which][1].end()
+        for half in range(2):
+            total = squares[which][1].total(half)
+            o_zsquare[:, 32 * which + 16 * half : 32 * which + 16 * half + 16, :] = total.astype(BF16)
     for d in range(1, 4):
-        w.arrived(from_z.at[d - 1], 11 + d)
+        w.arrived(from_z.at[d - 1], T_TZ + d - 1)
     total = sums[h.z].astype(F32)
     for d in range(3):
         total = total + from_z[d].astype(F32)
     o_text[...] = total.astype(BF16)
+    for i, (c, f) in enumerate(clip_others(h)):
+        w.arrived(i_in.at[c], T_IC + i)
+    for c in range(4):
+        o_in[:, 1024 * c : 1024 * c + 1024] = i_in[c].astype(F32)
     for d in range(1, 8):
-        w.arrived(o_heads.at[lax.rem(h.f + 8 - d, 8)], d - 1)
+        w.arrived(o_heads.at[lax.rem(h.f + 8 - d, 8)], T_HEADS + d - 1)
     copy.wait()
     w.drain()
+    in_scatter.drain()
 
 
 def middle_back(*args):
-    rows, block = (256, 1024), (2, 128, 256)
+    rows, block, quarter = (256, 1024), (2, 128, 256), (4, 128, 1024)
     return comm_call(
         middle_back_body,
         (
             shape(rows, F32),
-            shape((32, 96, 1024)),
+            shape((4, 8, 32, 1024)),
+            shape((4, 64, 1024)),
             shape((8, 128, 256)),
             shape(block),
             shape((8, 1024), F32),
             shape(rows),
+            shape((32, 4096), F32),
         ),
-        [VMEM] * 13,
-        (VMEM,) * 6,
+        [VMEM] * 14,
+        (VMEM,) * 8,
         [
             pltpu.VMEM(rows, BF16),
             pltpu.VMEM(rows, BF16),
@@ -1343,145 +1481,267 @@
             pltpu.VMEM((4,) + block, BF16),
             pltpu.VMEM((4,) + block, BF16),
             pltpu.VMEM((3,) + block, BF16),
+            pltpu.VMEM(quarter, BF16),
+            pltpu.VMEM(quarter, BF16),
+            pltpu.VMEM((3, 128, 1024), BF16),
+            pltpu.VMEM((2, 128, 1024), BF16),
+            pltpu.VMEM((128, 1024), F32),
+            pltpu.VMEM((4, 32, 1024), BF16),
+            pltpu.VMEM((4, 32, 1024), BF16),
+            pltpu.VMEM((2, 4, 8, 32, 1024), BF16),
+            pltpu.VMEM((2, 4, 4, 32, 1024), BF16),
+            pltpu.VMEM((2, 4, 4, 32, 1024), BF16),
+            pltpu.VMEM((2, 6, 4, 16, 1024), BF16),
             pltpu.SemaphoreType.DMA((1,)),
         ],
-        24,
-        24,
+        80,
+        53,
         4,
     )(*args)
 
 
 def last_body(
-    first, square, cols, text, o_first, o_square, o_cols, o_norm, o_text,
-    f_sib, f_sum, f_in, s_sib, s_sum, s_slots, s_z, s_zin, c_slots, c_sum, c_in, t_in,
-    send_sem, recv_sem,
+    length, bias, q_ref, k_ref, v_ref, o_ref, lse, g_heads, hid, first_low, w_a, w_b, text_in, g_tkv,
+    square, z_square, norms, own_hid, g_after, params,
+    o_hidden, o_square, o_qkv, o_ckv, o_norm, o_text,
+    dq_t, k_t, dk, dv, d_cols, f_terms, f_sib, f_sum, f_in, s_inbox, s_sums, s_slots, s_part,
+    z_left, z_right, y_left, y_right, a_terms, a_slots, a_sum, a_in, b_terms, b_slots, b_sum, b_in,
+    t_terms, t_in, n_row, n_terms, n_slots, n_sum, n_in, send_sem, recv_sem,
 ):
     h = Here()
     w = Wire(h, send_sem, recv_sem)
+    T_S, T_SC, T_Z, T_Y, T_B, T_T, T_A, T_F, T_N = 0, 4, 10, 16, 22, 36, 44, 86, 94
     greet(frame_others(h) + clip_others(h)[:2])
-    T_F, T_S, T_C, T_T = 0, 12, 24, 40
-    for z in range(4):
-        w.send(first.at[2 * z + 1 - h.core], f_sib.at[z], T_F + z, h.c, h.sib)
-    for z in range(4):
-        w.send(square.at[:, 2 * z + 1 - h.core], s_sib.at[:, z], T_S + z, h.c, h.sib)
-    cols_scatter = ClipScatter(
+    s_sibling = SiblingSum(
+        w, lambda f: square.at[:, f], lambda z: s_inbox.at[z], lambda z: s_sums.at[z], T_S
+    )
+    s_sibling.begin()
+    z_scatter = ZScatter(w, z_square, z_left, z_right, T_Z)
+    z_scatter.begin()
+    s_scatter = ClipScatter(
         w,
-        lambda c, half: cols.at[c, pl.ds(4 * half, 4)],
-        [c_slots.at[i] for i in range(6)],
-        T_C,
-    )
-    cols_scatter.begin()
+        lambda c, half: s_sums.at[:, c, pl.ds(16 * half, 16), :],
+        [s_slots.at[i] for i in range(6)],
+        T_SC,
+    )
+    y_scatter = ZScatter(w, s_part, y_left, y_right, T_Y)
+
+    class Columns:
+        def __init__(self, terms, slots, sums, inbox, tag):
+            self.sums, self.inbox, self.tag = sums, inbox, tag
+            self.clip = ClipScatter(
+                w, lambda c, half: terms.at[c, pl.ds(4 * half, 4)], [slots.at[i] for i in range(6)], tag
+            )
+
+        def spread(self):
+            self.clip.end()
+            for half in range(2):
+                self.sums[4 * half : 4 * half + 4] = self.clip.total(half).astype(BF16)
+            for d in (4, 2, 6, 3, 5, 1, 7):
+                f = h.step(d)
+                w.send(self.sums.at[f], self.inbox.at[h.f], self.tag + 5 + d, h.c, f)
+            self.inbox[h.f] = self.sums[h.f]
+
+        def wait(self):
+            for d in range(1, 8):
+                w.arrived(self.inbox.at[lax.rem(h.f + 8 - d, 8)], self.tag + 5 + d)
+
+    text = text_in[h.pair]
+    for j in range(2):
+        b_terms[:, :, 32 * j : 32 * j + 32, :] = (
+            dot(text, g_tkv[j], (0, 0)).astype(BF16).reshape(4, 8, 32, 256)
+        )
+    b_columns = Columns(b_terms, b_slots, b_sum, b_in, T_B)
+    b_columns.clip.begin()
+    t_terms[...] = (
+        dot(g_tkv[0], column_weight(w_b, 0), (1, 1)) + dot(g_tkv[1], column_weight(w_b, 1), (1, 1))
+    ).astype(BF16)
     for d in range(1, 8):
         f = h.step(d)
-        w.send(text.at[pl.ds(pl.multiple_of(f * 16, 16), 16), :], t_in.at[h.f], T_T + d - 1, h.c, f)
-    t_in[h.f] = text[pl.ds(pl.multiple_of(h.f * 16, 16), 16), :]
-    for z in range(4):
-        w.arrived(f_sib.at[z], T_F + z)
-        f_sum[z] = (first[2 * z + h.core].astype(F32) + f_sib[z].astype(F32)).astype(BF16)
+        w.send(
+            t_terms.at[pl.ds(pl.multiple_of(f * 16, 16), 16), :], t_in.at[h.f], T_T + d - 1, h.c, f
+        )
+    t_in[h.f] = t_terms[pl.ds(pl.multiple_of(h.f * 16, 16), 16), :]
+
+    k_t[...] = k_ref[...].T
+    dk[...] = jnp.zeros_like(dk)
+    dv[...] = jnp.zeros_like(dv)
+
+    def rows_back(i):
+        attend_back_rows(
+            i, length, bias, q_ref, k_ref, v_ref, o_ref, lse, g_heads, d_cols.at[0], dq_t, k_t, dk, dv
+        )
+
+    rows_back(0)
+    s_sibling.end()
+    s_scatter.begin()
+    z_scatter.step(1)
+    rows_back(1)
+    z_scatter.step(2)
+    z_scatter.step(3)
+    b_columns.clip.middle()
+    rows_back(2)
+    s_scatter.middle()
+    b_columns.spread()
+    rows_back(3)
+    d_cols[1] = dk[...].astype(BF16)
+    d_cols[2] = dv[...].astype(BF16)
+    a_columns = [
+        Columns(a_terms.at[j], a_slots.at[j], a_sum.at[j], a_in.at[j], T_A + 13 * j) for j in range(3)
+    ]
+    for j in range(3):
+        a_terms[j] = dot(first_low[...], d_cols[j], (0, 0)).astype(BF16).reshape(4, 8, 32, 256)
+        a_columns[j].clip.begin()
+
+    f_sibling = SiblingSum(
+        w, lambda f: f_terms.at[f], lambda z: f_sib.at[z], lambda z: f_sum.at[z], T_F
+    )
+    n_row[...] = jnp.zeros_like(n_row)
+
+    def frame_terms(i, _):
+        rows = pl.ds(pl.multiple_of(i * 256, 256), 256)
+        grad = sum(dot(d_cols[j, rows, :], column_weight(w_a, j), (1, 1)) for j in range(3))
+        f_terms[pl.ds(2 * i, 2)] = grad.astype(BF16).reshape(2, 128, 1024)
+        xhat, _ = norm_parts(hid[pl.ds(2 * i, 2)].reshape(256, 1024).astype(F32))
+        n_row[0:1, :] += jnp.sum(grad * xhat, axis=0, keepdims=True)
+        n_row[3:4, :] += jnp.sum(grad, axis=0, keepdims=True)
+        return 0
+
+    lax.fori_loop(0, 4, frame_terms, 0)
+    f_sibling.begin()
+    s_scatter.end()
+    for half in range(2):
+        s_part[:, 16 * half : 16 * half + 16, :] = s_scatter.total(half).astype(BF16)
+    y_scatter.begin()
+    a_columns[0].clip.middle()
+    f_sibling.end()
     other = 2 * (1 - h.pair)
     is_end = jnp.logical_not(h.is_gate)
-    w.send(f_sum.at[lax.div(h.partner, 2)], f_in.at[0], T_F + 4, h.c, h.partner)
     to_gate, to_far = [], []
     for j in range(2):
         to_gate.append(w.copy(f_sum.at[other + j], f_in.at[1 + j], T_F + 5 + j, h.c, h.partner))
         pl.when(is_end)(to_gate[j].start)
-    for z in range(4):
-        w.arrived(s_sib.at[:, z], T_S + z)
-
-    def add_square(i, _):
-        c, z = lax.div(i, 4), lax.rem(i, 4)
-        s_sum[c, z] = (square[c, 2 * z + h.core].astype(F32) + s_sib[c, z].astype(F32)).astype(BF16)
-        return 0
-
-    lax.fori_loop(0, 16, add_square, 0)
-    square_scatter = ClipScatter(
-        w,
-        lambda c, half: s_sum.at[c, :, pl.ds(48 * half, 48), :],
-        [s_slots.at[i] for i in range(6)],
-        T_S + 4,
-    )
-    square_scatter.begin()
+    w.send(f_sum.at[lax.div(h.partner, 2)], f_in.at[0], T_F + 4, h.c, h.partner)
+    n_row[1:2, :] = norms[2:3, :]
+    n_row[2:3, :] = norms[0:1, :]
+    n_row[4:5, :] = norms[3:4, :]
+    n_row[5:6, :] = norms[1:2, :]
+    for c in range(4):
+        for f in range(8):
+            group = 2 * c + f // 4
+            n_terms[c, f] = n_row[:, 128 * group : 128 * group + 128].astype(BF16)
+    n_columns = Columns(n_terms, n_slots, n_sum, n_in, T_N)
+    n_columns.clip.begin()
+    a_columns[1].clip.middle()
+    a_columns[0].spread()
     for j in range(2):
+
         @pl.when(h.is_gate)
         def _():
             w.arrived(f_in.at[1 + j], T_F + 5 + j)
-            f_sum[other + j] = (f_sum[other + j].astype(F32) + f_in[1 + j].astype(F32)).astype(BF16)
+            add_into(f_sum.at[other + j], f_in.at[1 + j])
 
         to_far.append(w.copy(f_sum.at[other + j], f_in.at[3], T_F + 7, h.c, h.far[j]))
         pl.when(h.is_gate)(to_far[j].start)
-    cols_scatter.middle()
-    square_scatter.middle()
-    cols_scatter.end()
-    for half in range(2):
-        c_sum[4 * half : 4 * half + 4] = cols_scatter.total(half).astype(BF16)
-    for d in range(1, 8):
-        f = h.step(d)
-        w.send(c_sum.at[f], c_in.at[h.f], T_C + 6 + d - 1, h.c, f)
-    c_in[h.f] = c_sum[h.f]
-    square_scatter.end()
-    for half in range(2):
-        s_z[:, 48 * half : 48 * half + 48, :] = square_scatter.total(half).astype(BF16)
-    for d in range(1, 4):
-        w.send(s_z.at[lax.rem(h.z + d, 4)], s_zin.at[d - 1], T_S + 10 + d - 1 if d < 3 else 47, h.c, h.zstep(d))
-    w.arrived(f_in.at[0], T_F + 4)
-    w.arrived(f_in.at[3], T_F + 7)
-    o_first[h.pair] = f_sum[h.z].astype(F32) + f_in[0].astype(F32)
-    o_first[1 - h.pair] = f_in[3].astype(F32)
+    y_scatter.step(1)
+    a_columns[2].clip.middle()
+    a_columns[1].spread()
+    n_columns.clip.middle()
+    y_scatter.step(2)
+    y_scatter.step(3)
+    a_columns[2].spread()
+    n_columns.spread()
+    z_scatter.total(o_square.at[pl.ds(32, 64), :])
+    b_columns.wait()
+    for j in range(2):
+        for q in range(4):
+            at = pl.ds(32 * j, 32)
+            o_ckv[j, :, 256 * q : 256 * q + 256] = b_in[q, at, :].astype(F32) + b_in[4 + q, at, :].astype(F32)
     for d in range(1, 8):
         w.arrived(t_in.at[lax.rem(h.f + 8 - d, 8)], T_T + d - 1)
     for p in range(2):
         o_text[p] = sum(t_in[4 * p + q].astype(F32) for q in range(4)).astype(BF16)
-    for d in range(1, 8):
-        w.arrived(c_in.at[lax.rem(h.f + 8 - d, 8)], T_C + 6 + d - 1)
-    for q in range(4):
-        o_cols[:, 256 * q : 256 * q + 256] = c_in[q, 0:160, :].astype(F32) + c_in[4 + q, 0:160, :].astype(F32)
-    o_norm[...] = sum(c_in[f, 160:176, 0:128].astype(F32) for f in range(8))
-    for d in range(1, 4):
-        w.arrived(s_zin.at[d - 1], T_S + 10 + d - 1 if d < 3 else 47)
-    o_square[...] = s_z[h.z].astype(F32) + sum(s_zin[d].astype(F32) for d in range(3))
+    w.arrived(f_in.at[0], T_F + 4)
+    w.arrived(f_in.at[3], T_F + 7)
+
+    def hidden_out(clip, total):
+        xhat, scale = norm_parts(own_hid[clip].astype(F32))
+        o_hidden[clip] = (g_after[clip] + norm_back(xhat, scale, total, params[0:1, :])).astype(BF16)
+
+    hidden_out(h.pair, f_sum[h.z].astype(F32) + f_in[0].astype(F32))
+    hidden_out(1 - h.pair, f_in[3].astype(F32))
+    y_scatter.total(o_square.at[pl.ds(0, 32), :])
+    for j in range(3):
+        a_columns[j].wait()
+        for q in range(4):
+            o_qkv[j, :, 256 * q : 256 * q + 256] = a_in[j, q].astype(F32) + a_in[j, 4 + q].astype(F32)
+    n_columns.wait()
+    o_norm[...] = sum(n_in[f].astype(F32) for f in range(8))
     w.drain()
+    z_scatter.drain()
+    y_scatter.drain()
     for j in range(2):
         pl.when(is_end)(to_gate[j].wait_send)
         pl.when(h.is_gate)(to_far[j].wait_send)
 
 
-def last_sums(first, square, cols, text):
+def last(*args):
     def buffer(*dims):
         return pltpu.VMEM(dims, BF16)
+
+    def full(*dims):
+        return pltpu.VMEM(dims, F32)
 
     return comm_call(
         last_body,
         (
-            shape((2, 128, 1024), F32),
+            shape((2, 128, 1024)),
             shape((96, 1024), F32),
-            shape((160, 1024), F32),
+            shape((3, 32, 1024), F32),
+            shape((2, 32, 1024), F32),
             shape((16, 128), F32),
             shape((2, 16, 1024)),
         ),
-        [VMEM] * 4,
-        (VMEM,) * 5,
+        [SMEM] + [VMEM] * 19,
+        (VMEM,) * 6,
         [
+            full(256, ROWS),
+            buffer(256, 1024),
+            full(1024, 256),
+            full(1024, 256),
+            buffer(3, 1024, 256),
+            buffer(8, 128, 1024),
             buffer(4, 128, 1024),
             buffer(4, 128, 1024),
             buffer(4, 128, 1024),
-            buffer(4, 4, 96, 1024),
-            buffer(4, 4, 96, 1024),
-            buffer(6, 4, 48, 1024),
-            buffer(4, 96, 1024),
-            buffer(3, 96, 1024),
-            buffer(6, 4, 176, 256),
-            buffer(8, 176, 256),
-            buffer(8, 176, 256),
+            buffer(4, 4, 32, 1024),
+            buffer(4, 4, 32, 1024),
+            buffer(6, 4, 16, 1024),
+            buffer(4, 32, 1024),
+            buffer(3, 64, 1024),
+            buffer(2, 64, 1024),
+            buffer(3, 32, 1024),
+            buffer(2, 32, 1024),
+            buffer(3, 4, 8, 32, 256),
+            buffer(3, 6, 4, 32, 256),
+            buffer(3, 8, 32, 256),
+            buffer(3, 8, 32, 256),
+            buffer(4, 8, 64, 256),
+            buffer(6, 4, 64, 256),
+            buffer(8, 64, 256),
+            buffer(8, 64, 256),
+            buffer(128, 1024),
             buffer(8, 16, 1024),
+            full(16, 1024),
+            buffer(4, 8, 16, 128),
+            buffer(6, 4, 16, 128),
+            buffer(8, 16, 128),
+            buffer(8, 16, 128),
         ],
-        64,
-        48,
+        140,
+        107,
         5,
-    )(first, square, cols, text)
-
-
-def matmul(left, right):
-    return jnp.dot(left, right, preferred_element_type=F32)
+    )(*args)
 
 
 def on_device_fast(
@@ -1519,71 +1779,36 @@
         hid_all, first_low, query, key, value, att_heads, lse, w_a, w_b, params, att, tkv, square, fin_all
     ) = front(my_len, bias, text_states, hidden_in, cols_a, cols_b, square_here, ffn_in)
     square = square.reshape(32, 96, 1024)
-    weights = [w_a[:, :, 32 * j : 32 * j + 32].reshape(1024, 256) for j in range(3)]
-    weights += [w_b[:, :, 32 * j : 32 * j + 32].reshape(1024, 256) for j in range(2)]
-    first_hat, _ = norm_parts(hid_all.reshape(1024, 1024).astype(F32))
-    my_text = lax.dynamic_slice_in_dim(text_states, pair, 1, 0)[0]
     slots = jnp.arange(128, dtype=jnp.int32)
     text_ok = (slots[None] < text_len[:, None]) & ((text_mask > 0) | (slots[None] == 0))
     text_bias = jnp.where(text_ok, 0.0, NEG).astype(F32)
     after_self, second, cross_query, crossed, after_cross, third, grad_all, ffn_w_in = middle(
         hidden_in, att, square, tkv, text_bias, params, out_grad.reshape(256, 1024), fin_all
     )
-    third_sum, out_terms, ffn_terms = feed(third, grad_all, ffn_w_in, ffn_out)
-    ffn_sum = lax.psum_scatter(ffn_terms, "frame", scatter_dimension=0, tiled=True)[0]
-    grad_ffn_out = ffn_sum[:128].astype(F32)
-    grad_ffn_in = lax.all_to_all(
-        ffn_sum[128:].reshape(4, 32, 1024), "clip", split_axis=0, concat_axis=2, tiled=True
-    )[0].astype(F32)
-    g_after_self, g_square, g_heads, g_tkv, g_norms, output = middle_back(
+    third_sum, out_terms, in_terms, grad_ffn_out = feed(third, grad_all, ffn_w_in, ffn_out)
+    g_after_self, g_square, z_square, g_heads, g_tkv, g_norms, output, grad_ffn_in = middle_back(
         third_sum, out_grad, after_cross, after_self, second, cross_query, crossed, att, square, tkv,
-        text_bias, params, out_terms,
-    )
-    output = output.reshape(2, 128, 1024)
-    g_query, g_key, g_value = attend_back(
-        my_len, bias, query, key, value, att_heads, lse, g_heads.reshape(1024, 256)
-    )
-
-    def back(grad, weight):
-        return lax.dot_general(grad, weight, (((1,), (1,)), ((), ())), preferred_element_type=F32)
-
-    def weight_term(left, grad):
-        return lax.dot_general(left, grad, (((0,), (0,)), ((), ())), preferred_element_type=F32)
-
-    g_first = back(g_query, weights[0]) + back(g_key, weights[1]) + back(g_value, weights[2])
-    gain_first = jnp.sum(g_first * first_hat, axis=0)
-    shift_first = jnp.sum(g_first, axis=0)
-    text_terms = (back(g_tkv[0], weights[3]) + back(g_tkv[1], weights[4])).astype(BF16)
-    terms = jnp.stack(
-        [weight_term(first_low, g) for g in (g_query, g_key, g_value)]
-        + [weight_term(my_text, g_tkv[i]) for i in range(2)]
-    )
-    terms = terms.astype(BF16).reshape(5, 4, 8, 32, 256).transpose(1, 2, 0, 3, 4).reshape(4, 8, 160, 256)
-    norm_terms = jnp.stack([gain_first, g_norms[2], g_norms[0], shift_first, g_norms[3], g_norms[1]])
-    norm_terms = norm_terms.astype(BF16).reshape(6, 4, 8, 32).transpose(1, 2, 0, 3)
-    norm_terms = jnp.pad(norm_terms, ((0, 0), (0, 0), (0, 10), (0, 224)))
-    cols = jnp.concatenate([terms, norm_terms], axis=2)
-    first_sum, square_sum, cols_sum, norm_sum, grad_text = last_sums(
-        g_first.astype(BF16).reshape(8, 128, 1024), g_square.reshape(4, 8, 96, 1024), cols, text_terms
-    )
-    own_hat, own_scale = norm_parts(hidden_in.astype(F32))
-    grad_hidden = (
-        g_after_self.reshape(2, 128, 1024) + norm_back(own_hat, own_scale, first_sum, params[0])
-    ).astype(BF16)
-    cols_sum = cols_sum.reshape(5, 32, 1024)
+        text_bias, params, out_terms, in_terms,
+    )
+    grad_hidden, square_sum, qkv_sum, ckv_sum, norm_sum, grad_text = last(
+        my_len, bias, query, key, value, att_heads, lse, g_heads.reshape(1024, 256), hid_all, first_low, w_a, w_b,
+        text_states, g_tkv, g_square, z_square, g_norms, hidden_in, g_after_self.reshape(2, 128, 1024), params,
+    )
+    norm_sum = lax.dynamic_slice(norm_sum, (0, 32 * (frame % 4)), (6, 32))
     return (
-        output,
+        output.reshape(2, 128, 1024),
         grad_hidden,
         grad_text,
-        jnp.stack([cols_sum[0], cols_sum[1], cols_sum[2]], axis=1),
+        jnp.moveaxis(qkv_sum, 0, 1),
         square_sum[0:32],
-        jnp.stack([square_sum[32:64], cols_sum[3], cols_sum[4]], axis=1),
+        jnp.stack([square_sum[32:64], ckv_sum[0], ckv_sum[1]], axis=1),
         square_sum[64:96],
         grad_ffn_in,
         grad_ffn_out,
-        norm_sum[0:3, 0:32],
-        norm_sum[3:6, 0:32],
-    )
+        norm_sum[0:3],
+        norm_sum[3:6],
+    )
+
 
 def solution(mesh):
     return jax.shard_map(

time: 415 us -> 349 us (0.84)
  Pallas kernels: 343 us -> 322 us
  between operations: 14.7 us -> 0.98 us
  matrix products: 9.68 us -> 0 us
  other arithmetic: 15.1 us -> 7.36 us
  waiting for transfers between devices: 4.94 us -> 0 us
    pallas_call x4 -> x3, Pallas kernels: 214 us -> 193 us  [the longest x1 74.3 us: last(): comm_call(last_body, (shape((2, 128, 1024)), shape((96, 1024), F32), shap...]
    dot_general x10 -> x0, matrix products: 9.68 us -> none  [the longest x5 5.72 us: back(): lax.dot_general(grad, weight, (((1,), (1,)), ((), ())), preferred_element...]
    all_to_all x1 -> x0, waiting for transfers between devices: 4.92 us -> none  [on_device_fast(): lax.all_to_all(ffn_sum[128:].reshape(4, 32, 1024), 'clip', split_axis=0,...]
  transfers between devices with their start and end apart: 2 -> 0, of which waited for: 1 -> 0; matrix products, arithmetic and copies ran while one was open for 6% -> 0% of each run, Pallas kernels for 40% -> 0%
where the time goes in v3:
time: 349 us; the launch traced here: 344 us
  Pallas kernels  322 us (92%)
  local copies, waits for them, and re-layouts  13.8 us (4%)
  other arithmetic  7.36 us (2%)
    pallas_call x1, Pallas kernels, front(): comm_call(front_body, (shape((8, 128, 1024)), shape((1024, 1024)), shape(...  96.4 us
    pallas_call x1, Pallas kernels, last(): comm_call(last_body, (shape((2, 128, 1024)), shape((96, 1024), F32), shap...  74.3 us
    pallas_call x1, Pallas kernels, feed(): comm_call(feed_body, (shape((256, 1024), F32), shape(full), shape((8, 128...  62.2 us
    pallas_call x1, Pallas kernels, middle_back(): comm_call(middle_back_body, (shape(rows, F32), shape((4, 8, 32, 1024)), s...  56.5 us
    pallas_call x1, Pallas kernels, middle(): comm_call(middle_body, (shape(rows, F32), shape(rows), shape(rows), shape...  32.7 us

profile of v3, /device:TPU:0, one launch (start us, length us, event | category | flops | bytes accessed | tf_op | source)
XLA Modules:
  0.0 344.2 jit_solution(6840162062914652155)
XLA Ops:
  0.7 1.2 dynamic_slice.9.length
  1.9 0.7 compare_reduce_fusion
  2.6 1.3 and_select_fusion.text_bias
  4.0 0.7 pad_maximum_fusion.3
  4.7 0.6 fusion.1
  5.3 0.3 dynamic_update_slice.6
  5.7 0.8 slice_bitcast_fusion.3
  6.6 1.6 pad_maximum_fusion.2.square
  8.1 1.6 slice.36
  9.7 1.6 pad_maximum_fusion.1.cols_a
  11.3 1.0 broadcast_in_dim.28.bias
  12.3 96.4 %shard_map.230 = (bf16[8,128,1024]{2,1,0:T(8,128)(2,1)}, bf16[1024,1024]{1,0:T(8,128)(2,1)}, bf16[1024,256]{1,0:T(8,128)(2,1)}, bf16[1024,256]{1,0:T(8,128)(2,1)...) custom-call(s32[1]{0:T(128)} %dynamic_slice.9.length, ...), custom_call_target="tpu_custom_call" | custom-call | tf_op jit(solution)/shard_map/pallas_call | solution.py:995
  108.7 32.7 %shard_map.231 = (f32[256,1024]{1,0:T(8,128)}, bf16[256,1024]{1,0:T(8,128)(2,1)}, bf16[256,1024]{1,0:T(8,128)(2,1)}, bf16[256,1024]{1,0:T(8,128)(2,1)}, f32[256,...) custom-call(bf16[2,128,1024]{2,1,0:T(8,128)(2,1)} %own_hid.1, ...), custom_call_target="tpu_custom_call" | custom-call | tf_op jit(solution)/shard_map/pallas_call | solution.py:1143
  141.4 62.2 %shard_map.232 = (f32[256,1024]{1,0:T(8,128)}, bf16[4,256,1024]{2,1,0:T(8,128)(2,1)}, bf16[8,128,1024]{2,1,0:T(8,128)(2,1)}, f32[128,1024]{1,0:T(8,128)}) custom-call(bf16[256,1024]{1,0:T(8,128)(2,1)} %get-tuple-element.56.third, bf16[4,256,1024]{2,1,0:T(8,128)(2,1)} %get-tuple-element.57.grad, bf16[4,8,32,1024]{3,2,1,0:T(8,128)(2,1)} %get-tuple-element.58.win, ...), custom_call_target="tpu_custom_call" | custom-call | tf_op jit(solution)/shard_map/pallas_call | solution.py:1275
  203.6 56.5 %shard_map.233 = (f32[256,1024]{1,0:T(8,128)}, bf16[4,8,32,1024]{3,2,1,0:T(8,128)(2,1)}, bf16[4,64,1024]{2,1,0:T(8,128)(2,1)}, bf16[8,128,256]{2,1,0:T(8,128)(2,...) custom-call(f32[256,1024]{1,0:T(8,128)} %get-tuple-element.59.g_third, ...), custom_call_target="tpu_custom_call" | custom-call | tf_op jit(solution)/shard_map/pallas_call | solution.py:1461
  260.1 74.3 %shard_map.234 = (bf16[2,128,1024]{2,1,0:T(8,128)(2,1)}, f32[96,1024]{1,0:T(8,128)}, f32[3,32,1024]{2,1,0:T(8,128)}, f32[2,32,1024]{2,1,0:T(8,128)}, f32[16,128]{1,0:T(8,128)}, /*index=5*/bf16[2,16,1024]{2,1,0:T(8,128)(2,1)}) custom-call(s32[1]{0:T(128)} %dynamic_slice.9.length, f32[1024,128]{1,0:T(8,128)} %broadcast_in_dim.28.bias, ...), custom_call_target="tpu_custom_call" | custom-call | tf_op jit(solution)/shard_map/pallas_call | solution.py:1695
  334.4 0.0 copy-start.2
  334.4 0.0 copy-start.3
  334.5 0.8 constant_dynamic-slice_fusion
  335.3 0.6 fusion.3
  335.9 0.0 copy-start.5
  335.9 0.0 copy-start.4
  335.9 1.0 slice_bitcast_fusion.1
  336.9 1.8 fusion.2
  338.7 0.0 copy-start.1
  338.7 0.8 pad_maximum_fusion
  339.5 0.0 copy-done.2
  339.5 0.0 copy-start
  339.5 0.8 copy.34
  340.3 0.0 copy-done.3
  340.3 0.8 copy.35
  341.1 0.0 copy-done.5
  341.1 0.6 copy.36
  341.7 0.0 copy-done.4
  341.7 0.7 copy.37
  342.4 0.0 copy-done.1
  342.4 0.8 copy.38
  343.2 0.0 copy-done
  343.2 0.8 copy.39
  (4 shorter events, 0.0 us)
Async XLA Ops:
  334.4 5.0 %copy-start.2 = (bf16[256,1024]{1,0:T(8,128)(2,1)S(1)}, bf16[256,1024]{1,0:T(8,128)(2,1)}, u32[]{:S(2)}) copy-start(bf16[256,1024]{1,0:T(8,128)(2,1)} %get-tuple-element.67) | copy-start | bytes 1572868
  334.4 5.8 %copy-start.3 = (bf16[2,128,1024]{2,1,0:T(8,128)(2,1)S(1)}, bf16[2,128,1024]{2,1,0:T(8,128)(2,1)}, u32[]{:S(2)}) copy-start(bf16[2,128,1024]{2,1,0:T(8,128)(2,1)} %get-tuple-element.110) | copy-start | bytes 1572868
  335.9 5.2 %copy-start.5 = (bf16[2,16,1024]{2,1,0:T(8,128)(2,1)S(1)}, bf16[2,16,1024]{2,1,0:T(8,128)(2,1)}, u32[]{:S(2)}) copy-start(bf16[2,16,1024]{2,1,0:T(8,128)(2,1)} %get-tuple-element.111) | copy-start | bytes 196612
  335.9 5.8 %copy-start.4 = (f32[3,32,1024]{2,1,0:T(8,128)S(1)}, f32[3,32,1024]{2,1,0:T(8,128)}, u32[]{:S(2)}) copy-start(f32[3,32,1024]{2,1,0:T(8,128)} %get-tuple-element.85) | copy-start | bytes 1179652
  338.7 3.8 %copy-start.1 = (f32[32,4096]{1,0:T(8,128)S(1)}, f32[32,4096]{1,0:T(8,128)}, u32[]{:S(2)}) copy-start(f32[32,4096]{1,0:T(8,128)} %get-tuple-element.116) | copy-start | bytes 1572868
  339.5 3.8 %copy-start = (f32[128,1024]{1,0:T(8,128)S(1)}, f32[128,1024]{1,0:T(8,128)}, u32[]{:S(2)}) copy-start(f32[128,1024]{1,0:T(8,128)} %get-tuple-element.117) | copy-start | bytes 1572868

commit v4 on v3

--- a/solution.py
+++ b/solution.py
@@ -574,6 +574,8 @@
         h, w = self.wire.here, self.wire
         for d in range(4):
             w.arrived(self.slot(h.zstep(d) + h.sib - h.f), self.tag + 6 + d)
+
+    def drain(self):
         for go, copy in self.open:
             pl.when(go)(copy.wait_send)
 
@@ -777,15 +779,37 @@
     o_ref[first:n, :] = jnp.where(live, out_t[...].T, 0).astype(BF16)
 
 
-def front_body(
-    length, bias, text, hid, cols_a, cols_b, square, fin,
-    o_hid, o_first, o_q, o_k, o_v, o_heads, o_lse, o_cols_a, o_cols_b, o_params, o_att, o_tkv, o_square, o_fin,
-    out_t, v_t, tkv, v_square, v_fin, local, send_sem, recv_sem,
+def square_of(square, which):
+    return square[:, :, 32 * which : 32 * which + 32, :].reshape(1024, 1024)
+
+
+def text_probs(query, keys, bias, lane_head):
+    heads = [jnp.where(lane_head == j, query, 0) for j in range(4)]
+    stacked = jnp.concatenate(heads, axis=0)
+    scores = dot(stacked, keys, (1, 1)) + bias
+    weight = jnp.exp(scores - jnp.max(scores, axis=1, keepdims=True))
+    return weight / jnp.sum(weight, axis=1, keepdims=True), stacked
+
+
+def pick_heads(stacked, lane_head):
+    return sum(jnp.where(lane_head == j, stacked[128 * j : 128 * j + 128], 0) for j in range(4))
+
+
+def forward_body(
+    length, bias, text_bias, text, hid, cols_a, cols_b, square, fin, fout, grad,
+    o_hid, o_first, o_q, o_k, o_v, o_heads, o_lse, o_w_a, o_w_b, o_params, o_att, o_tkv, o_square,
+    o_second, o_query, o_crossed, o_self, o_cross, o_out, o_in, o_third, o_sum,
+    hid_all, first, q_ref, k_ref, v_ref, heads, lse, w_a, w_b, params, att, tkv, sq,
+    second, query_ref, crossed, after_self, after_cross, out_ref, in_ref,
+    out_t, v_t, own_tkv, own_text, own_hid, fin_in, grad_all, win, wout,
+    tokens, inner, slope, g_pre, terms, slots, out_w, inbox, sums, near, far,
+    local, saved, send_sem, recv_sem,
 ):
     h = Here()
     w = Wire(h, send_sem, recv_sem)
     T_HID, T_A, T_B, T_FIN, T_AXY, T_BXY = 0, 10, 17, 24, 27, 33
     T_Z, T_SXY, T_SIB, T_ATT, T_TKV = 39, 49, 73, 85, 93
+    T_WIN, T_GRAD, T_TOK, T_WOUT, T_TERM, T_OSIB, T_OZ = 96, 106, 112, 118, 128, 134, 138
 
     def my_columns(f):
         return pl.ds(pl.multiple_of(lax.rem(f, 4) * 256, 256), 256)
@@ -793,107 +817,116 @@
     def fin_part(c):
         return fin.at[:, pl.ds(pl.multiple_of(c * 1024, 1024), 1024)]
 
-    plain = [
-        pltpu.make_async_copy(cols_a.at[:, my_columns(h.f)], o_cols_a.at[h.c, h.f], local.at[0]),
-        pltpu.make_async_copy(cols_b.at[:, my_columns(h.f)], o_cols_b.at[h.c, h.f], local.at[1]),
-        pltpu.make_async_copy(hid.at[h.pair], o_hid.at[h.f], local.at[2]),
+    own = [
+        pltpu.make_async_copy(src, dst, local.at[i])
+        for i, (src, dst) in enumerate(
+            (
+                (cols_a.at[:, my_columns(h.f)], w_a.at[h.c, h.f]),
+                (cols_b.at[:, my_columns(h.f)], w_b.at[h.c, h.f]),
+                (hid.at[h.pair], hid_all.at[h.f]),
+                (square, sq.at[h.c, h.f]),
+                (fin_part(h.c), fin_in.at[h.c]),
+                (text, own_text),
+                (hid, own_hid),
+                (grad, grad_all.at[h.c]),
+                (fout, wout.at[h.f]),
+            )
+        )
     ]
-    for copy in plain:
+    for copy in own:
         copy.start()
-    turned = [
-        LocalCopy(square, v_square, o_square.at[h.c, h.f], local.at[3]),
-        LocalCopy(fin_part(h.c), v_fin, o_fin.at[h.c], local.at[4]),
-    ]
+    saves = []
+
+    def save(src, dst):
+        copy = pltpu.make_async_copy(src, dst, saved.at[len(saves)])
+        copy.start()
+        saves.append(copy)
+
     greet(frame_others(h) + clip_others(h))
 
     for d in (2, 6, 4, 3, 5, 1, 7):
         f = h.step(d)
-        w.send(cols_a.at[:, my_columns(f)], o_cols_a.at[h.c, h.f], T_A + d - 1, h.c, f)
+        w.send(cols_a.at[:, my_columns(f)], w_a.at[h.c, h.f], T_A + d - 1, h.c, f)
+
+    def square_gather(d):
+        f = h.zstep(d)
+        return ClipGather(
+            w,
+            lambda c, half: sq.at[c, f, pl.ds(48 * half, 48), :],
+            T_SXY + 6 * d,
+            (lambda half: square.at[pl.ds(48 * half, 48), :]) if d == 0 else None,
+        )
+
+    gathers = [square_gather(d) for d in range(4)]
+    gathers[0].begin()
 
     def half_of(ref, part):
         return ref.at[pl.ds(64 * part, 64), :]
 
     for part in range(2):
-        w.send(half_of(hid.at[h.pair], part), half_of(o_hid.at[h.f], part), T_HID + 1 + part, h.c, h.partner)
         w.send(
             half_of(hid.at[1 - h.pair], part),
-            half_of(o_hid.at[h.f], part),
+            half_of(hid_all.at[h.f], part),
             T_HID + 3 + 2 * h.role + part,
             h.c,
             h.far_gate,
         )
-    w.send(hid.at[h.pair], o_hid.at[h.f], T_HID, h.c, h.sib)
-
-    def square_slot(f):
-        return o_square.at[h.c, f]
-
-    z_gather = ZGather(w, square_slot, T_Z, square)
-
-    def square_gather(d):
-        f = h.zstep(d)
-        return ClipGather(
-            w,
-            lambda c, half: o_square.at[c, f, pl.ds(48 * half, 48), :],
-            T_SXY + 6 * d,
-            (lambda half: square.at[pl.ds(48 * half, 48), :]) if d == 0 else None,
-        )
-
-    gathers = [square_gather(d) for d in range(4)]
-    gathers[0].begin()
+        w.send(half_of(hid.at[h.pair], part), half_of(hid_all.at[h.f], part), T_HID + 1 + part, h.c, h.partner)
+    w.send(hid.at[h.pair], hid_all.at[h.f], T_HID, h.c, h.sib)
     for i, (c, f) in enumerate(clip_others(h)):
-        w.send(fin_part(c), o_fin.at[h.c], T_FIN + i, c, f)
-    for copy in turned:
-        copy.turn()
-    plain[0].wait()
+        w.send(fin_part(c), fin_in.at[h.c], T_FIN + i, c, f)
+    own[0].wait()
     for d in range(1, 8):
-        w.arrived(o_cols_a.at[h.c, lax.rem(h.f + 8 - d, 8)], T_A + d - 1)
-    a_gather = ClipGather(w, lambda c, half: o_cols_a.at[c, pl.ds(4 * half, 4)], T_AXY)
+        w.arrived(w_a.at[h.c, lax.rem(h.f + 8 - d, 8)], T_A + d - 1)
+    a_gather = ClipGather(w, lambda c, half: w_a.at[c, pl.ds(4 * half, 4)], T_AXY)
     a_gather.begin()
     forwards = []
     for part in range(2):
         for j in range(2):
-            block = half_of(o_hid.at[h.far[j]], part)
+            block = half_of(hid_all.at[h.far[j]], part)
             w.arrived(block, T_HID + 3 + 2 * j + part)
             forward = w.copy(block, block, T_HID + 3 + 2 * j + part, h.c, h.partner)
             pl.when(h.is_gate)(forward.start)
             forwards.append(forward)
     for d in (2, 6, 4, 3, 5, 1, 7):
         f = h.step(d)
-        w.send(cols_b.at[:, my_columns(f)], o_cols_b.at[h.c, h.f], T_B + d - 1, h.c, f)
+        w.send(cols_b.at[:, my_columns(f)], w_b.at[h.c, h.f], T_B + d - 1, h.c, f)
     for part in range(2):
-        w.arrived(half_of(o_hid.at[h.partner], part), T_HID + 1 + part)
-    w.send(o_hid.at[h.partner], o_hid.at[h.partner], T_HID + 7, h.c, h.sib)
+        w.arrived(half_of(hid_all.at[h.partner], part), T_HID + 1 + part)
+    w.send(hid_all.at[h.partner], hid_all.at[h.partner], T_HID + 7, h.c, h.sib)
     for j in range(2):
-        w.send(o_hid.at[h.far[j]], o_hid.at[h.far[j]], T_HID + 8 + j, h.c, h.sib)
+        w.send(hid_all.at[h.far[j]], hid_all.at[h.far[j]], T_HID + 8 + j, h.c, h.sib)
     a_gather.middle()
+    own[3].wait()
+    z_gather = ZGather(w, lambda f: sq.at[h.c, f], T_Z)
     z_gather.step(1)
     z_gather.relay(0)
-    plain[1].wait()
+    gathers[0].middle()
+    own[1].wait()
     for d in range(1, 8):
-        w.arrived(o_cols_b.at[h.c, lax.rem(h.f + 8 - d, 8)], T_B + d - 1)
-    b_gather = ClipGather(w, lambda c, half: o_cols_b.at[c, pl.ds(4 * half, 4)], T_BXY)
+        w.arrived(w_b.at[h.c, lax.rem(h.f + 8 - d, 8)], T_B + d - 1)
+    b_gather = ClipGather(w, lambda c, half: w_b.at[c, pl.ds(4 * half, 4)], T_BXY)
     b_gather.begin()
-    gathers[0].middle()
     a_gather.near()
     a_gather.end()
     for g in range(8):
-        group = sum(o_cols_a[g // 2, 4 * (g % 2) + i, 96:104, 0:128].astype(F32) for i in range(4))
-        o_params[:, 128 * g : 128 * g + 128] = group
-    plain[2].wait()
-    w.arrived(o_hid.at[h.sib], T_HID)
-    w.arrived(o_hid.at[h.partner + h.sib - h.f], T_HID + 7)
+        group = sum(w_a[g // 2, 4 * (g % 2) + i, 96:104, 0:128].astype(F32) for i in range(4))
+        params[:, 128 * g : 128 * g + 128] = group
+    own[2].wait()
+    w.arrived(hid_all.at[h.sib], T_HID)
+    w.arrived(hid_all.at[h.partner + h.sib - h.f], T_HID + 7)
     for j in range(2):
-        w.arrived(o_hid.at[h.far[j] + h.sib - h.f], T_HID + 8 + j)
+        w.arrived(hid_all.at[h.far[j] + h.sib - h.f], T_HID + 8 + j)
     z_gather.step(2)
 
     def project_rows(i, _):
         at = pl.ds(pl.multiple_of(i * 256, 256), 256)
-        rows = o_hid[pl.ds(2 * i, 2)].reshape(256, 1024).astype(F32)
+        rows = hid_all[pl.ds(2 * i, 2)].reshape(256, 1024).astype(F32)
         xhat, _ = norm_parts(rows)
-        low = (xhat * o_params[0:1, :] + o_params[3:4, :]).astype(BF16)
-        o_first[at, :] = low
-        for j, out in enumerate((o_q, o_k, o_v)):
-            out[at, :] = dot(low, column_weight(o_cols_a, j), (1, 0)).astype(BF16)
+        low = (xhat * params[0:1, :] + params[3:4, :]).astype(BF16)
+        first[at, :] = low
+        for j, out in enumerate((q_ref, k_ref, v_ref)):
+            out[at, :] = dot(low, column_weight(w_a, j), (1, 0)).astype(BF16)
         return 0
 
     lax.fori_loop(0, 2, project_rows, 0)
@@ -902,37 +935,24 @@
     z_gather.relay(2)
     b_gather.middle()
     lax.fori_loop(2, 4, project_rows, 0)
-    v_t[...] = o_v[...].T
-    b_gather.near()
-    b_gather.end()
+    v_t[...] = v_ref[...].T
     z_gather.step(4)
     for d in (1, 3):
         gathers[d].begin()
         z_gather.relay(d)
 
-    def text_slot(f):
-        return o_tkv.at[lax.div(f, 4), :, :, my_columns(f)]
-
-    for j in range(2):
-        tkv[j] = dot(text[h.pair], column_weight(o_cols_b, j), (1, 0)).astype(BF16)
-    for d in range(1, 4):
-        w.send(tkv, text_slot(h.f), T_TKV + d, h.c, h.zstep(d))
-    w.send(tkv, text_slot(h.f), T_TKV, h.c, h.sib)
-    text_copy = pltpu.make_async_copy(tkv, text_slot(h.f), local.at[5])
-    text_copy.start()
-
     def att_slot(f):
-        return o_att.at[lax.div(f, 4), :, my_columns(f)]
+        return att.at[lax.div(f, 4), :, my_columns(f)]
 
     att_sends = []
 
     def attend_and_send(i):
-        attend_rows(i, length, bias, o_q, o_k, v_t, o_heads, o_lse, out_t)
+        attend_rows(i, length, bias, q_ref, k_ref, v_t, heads, lse, out_t)
         for f in (2 * i, 2 * i + 1):
-            block = o_heads.at[pl.ds(128 * f, 128), :]
+            block = heads.at[pl.ds(128 * f, 128), :]
             away = h.f != f
             copy = w.copy(block, att_slot(h.f), T_ATT + h.f, h.c, f)
-            stay = pltpu.make_async_copy(block, att_slot(h.f), local.at[6])
+            stay = pltpu.make_async_copy(block, att_slot(h.f), local.at[9])
             pl.when(away)(copy.start)
             pl.when(jnp.logical_not(away))(stay.start)
             att_sends.append((away, copy, stay))
@@ -943,178 +963,81 @@
             gathers[d].middle()
         gathers[d].near()
         for i, c in enumerate((h.cx, h.cy)):
-            w.send(o_square.at[c, f], o_square.at[c, f], T_SIB + 3 * d + i, h.c, h.sib)
+            w.send(sq.at[c, f], sq.at[c, f], T_SIB + 3 * d + i, h.c, h.sib)
 
     def square_last(d):
         f = h.zstep(d)
         gathers[d].end()
-        w.send(o_square.at[h.cd, f], o_square.at[h.cd, f], T_SIB + 3 * d + 2, h.c, h.sib)
+        w.send(sq.at[h.cd, f], sq.at[h.cd, f], T_SIB + 3 * d + 2, h.c, h.sib)
 
     attend_and_send(3)
+    def text_slot(f):
+        return tkv.at[:, :, :, my_columns(f)]
+
+    b_gather.near()
+    b_gather.end()
+    own[5].wait()
+    for clip in range(2):
+        for j in range(2):
+            own_tkv[clip, j] = dot(own_text[clip], column_weight(w_b, j), (1, 0)).astype(BF16)
+    w.send(own_tkv, text_slot(h.f), T_TKV, h.c, h.partner)
+    w.send(own_tkv, text_slot(h.f), T_TKV + 1, h.c, h.sib)
+    text_copy = pltpu.make_async_copy(own_tkv, text_slot(h.f), local.at[10])
+    text_copy.start()
     square_steps(0)
-    square_steps(2)
     square_last(0)
     attend_and_send(2)
+    square_steps(2)
+    w.arrived(text_slot(h.partner), T_TKV)
+    w.send(text_slot(h.partner), text_slot(h.partner), T_TKV + 2, h.c, h.sib)
+    attend_and_send(1)
+    square_last(2)
     square_steps(1)
-    square_last(2)
-    for d in range(1, 4):
-        f = lax.rem(h.f + 8 - 2 * d, 8)
-        w.arrived(text_slot(f), T_TKV + d)
-        w.send(text_slot(f), text_slot(f), T_TKV + 3 + d, h.c, h.sib)
-    attend_and_send(1)
+    attend_and_send(0)
+    own[4].wait()
+    for i, (c, f) in enumerate(clip_others(h)):
+        w.arrived(fin_in.at[c], T_FIN + i)
+    win_gather = ZGather(w, lambda f: win.at[:, f], T_WIN, fin_in)
+    win_copy = pltpu.make_async_copy(fin_in, win.at[:, h.f], local.at[11])
+    win_copy.start()
+    win_gather.step(1)
+    win_gather.relay(0)
     square_steps(3)
-    attend_and_send(0)
     square_last(1)
     square_last(3)
+    own[7].wait()
+    grad_gather = ClipGather(w, lambda c, half: grad_all.at[c, pl.ds(128 * half, 128), :], T_GRAD)
+    grad_gather.begin()
+    for src, dst in (
+        (hid_all, o_hid), (first, o_first), (q_ref, o_q), (k_ref, o_k), (v_ref, o_v), (heads, o_heads), (lse, o_lse),
+        (w_a, o_w_a), (w_b, o_w_b), (params, o_params),
+    ):
+        save(src, dst)
     z_gather.end()
     for d in range(4):
         f = h.zstep(d) + h.sib - h.f
         for i, c in enumerate((h.cx, h.cy, h.cd)):
-            w.arrived(o_square.at[c, f], T_SIB + 3 * d + i)
+            w.arrived(sq.at[c, f], T_SIB + 3 * d + i)
     for d in range(1, 8):
         f = lax.rem(h.f + 8 - d, 8)
         w.arrived(att_slot(f), T_ATT + f)
-    w.arrived(text_slot(h.sib), T_TKV)
-    for d in range(1, 4):
-        w.arrived(text_slot(lax.rem(h.sib + 8 - 2 * d, 8)), T_TKV + 3 + d)
-    for i, (c, f) in enumerate(clip_others(h)):
-        w.arrived(o_fin.at[c], T_FIN + i)
-    for copy in turned:
-        copy.wait()
+    for away, _, stay in att_sends:
+        pl.when(jnp.logical_not(away))(stay.wait)
+    win_gather.step(2)
+
+    own[6].wait()
+    value = own_hid[...].reshape(256, 1024).astype(F32) + dot(
+        att[...].reshape(256, 1024), square_of(sq, 0), (1, 0)
+    )
+    after_self[...] = value
+    xhat, _ = norm_parts(value)
+    second[...] = (xhat * params[1:2, :] + params[4:5, :]).astype(BF16)
+    query_ref[...] = dot(second[...], square_of(sq, 1), (1, 0)).astype(BF16)
+    win_gather.step(3)
+    grad_gather.middle()
+    w.arrived(text_slot(h.sib), T_TKV + 1)
+    w.arrived(text_slot(h.partner + h.sib - h.f), T_TKV + 2)
     text_copy.wait()
-    w.drain()
-    for copy in forwards:
-        pl.when(h.is_gate)(copy.wait_send)
-    for away, copy, stay in att_sends:
-        pl.when(away)(copy.wait_send)
-        pl.when(jnp.logical_not(away))(stay.wait)
-
-
-def front(length, bias, text, hid, cols_a, cols_b, square, fin):
-    column = (1024, 256)
-    return comm_call(
-        front_body,
-        (
-            shape((8, 128, 1024)),
-            shape((1024, 1024)),
-            shape(column),
-            shape(column),
-            shape(column),
-            shape(column),
-            shape((8, 1024), F32),
-            shape((4, 8, 112, 256)),
-            shape((4, 8, 64, 256)),
-            shape((8, 1024), F32),
-            shape((2, 128, 1024)),
-            shape((2, 2, 128, 1024)),
-            shape((4, 8, 96, 1024)),
-            shape((4, 32, 1024)),
-        ),
-        [SMEM, VMEM, VMEM] + [HBM] * 5,
-        (VMEM,) * 10 + (HBM,) * 4,
-        [
-            pltpu.VMEM((256, ROWS), F32),
-            pltpu.VMEM((256, 1024), BF16),
-            pltpu.VMEM((2, 128, 256), BF16),
-            pltpu.VMEM((96, 1024), BF16),
-            pltpu.VMEM((32, 1024), BF16),
-            pltpu.SemaphoreType.DMA((7,)),
-        ],
-        128,
-        100,
-        1,
-    )(length, bias, text, hid, cols_a, cols_b, square, fin)
-
-
-def attend_back_rows(i, length, bias, q_ref, k_ref, v_ref, o_ref, lse_ref, g_ref, dq_ref, dq_t, k_t, dk, dv):
-    lane_head = lax.broadcasted_iota(jnp.int32, (ROWS, 256), 1) // HD
-    first, n = i * ROWS, (i + 1) * ROWS
-    q = q_ref[first:n, :] * jnp.asarray(HD**-0.5, BF16)
-    live = first + lax.broadcasted_iota(jnp.int32, (ROWS, 256), 0) < length[0]
-    g = jnp.where(live, g_ref[first:n, :], 0)
-    both = (g.astype(F32) * o_ref[first:n, :].astype(F32)).T
-    row_dots = jnp.concatenate(
-        [jnp.sum(both[HD * j : HD * j + HD], axis=0, keepdims=True) for j in range(4)], axis=0
-    )
-    lse = lse_ref[0:4, first:n]
-
-    def pick(rows, j):
-        at = lax.broadcasted_iota(jnp.int32, rows.shape, 0) == j
-        return jnp.sum(jnp.where(at, rows, 0), axis=0, keepdims=True)
-
-    def head(j, _):
-        q_head = jnp.where(lane_head == j, q, 0)
-        g_head = jnp.where(lane_head == j, g, 0)
-        scores = mask_scores(dot(k_ref[0:n, :], q_head, (1, 1)), bias, first, ROWS)
-        probs = jnp.exp(scores - pick(lse, j))
-        grads = dot(v_ref[0:n, :], g_head, (1, 1))
-        dlogits = (probs * (grads - pick(row_dots, j))).astype(BF16)
-        dv[0:n, :] += dot(probs.astype(BF16), g_head, (1, 0))
-        dk[0:n, :] += dot(dlogits, q_head, (1, 0))
-        at = pl.ds(pl.multiple_of(j * HD, HD), HD)
-        dq_t[at, :] = dot(k_t[at, 0:n], dlogits, (1, 0))
-        return 0
-
-    lax.fori_loop(0, 4, head, 0)
-    dq_ref[first:n, :] = (dq_t[...].T * (HD**-0.5)).astype(BF16)
-
-
-def square_of(square, which):
-    return square[:, 32 * which : 32 * which + 32, :].reshape(1024, 1024)
-
-
-def text_probs(query, keys, bias, lane_head):
-    heads = [jnp.where(lane_head == j, query, 0) for j in range(4)]
-    stacked = jnp.concatenate(heads, axis=0)
-    scores = dot(stacked, keys, (1, 1)) + bias
-    weight = jnp.exp(scores - jnp.max(scores, axis=1, keepdims=True))
-    return weight / jnp.sum(weight, axis=1, keepdims=True), stacked
-
-
-def pick_heads(stacked, lane_head):
-    return sum(jnp.where(lane_head == j, stacked[128 * j : 128 * j + 128], 0) for j in range(4))
-
-
-def near_devices(here):
-    return [(here.c, here.sib)] + [(here.c, here.zstep(d)) for d in range(1, 4)] + clip_others(here)[:2]
-
-
-def middle_body(
-    hid, att, square, tkv, text_bias, params, grad, fin,
-    o_self, second_ref, query_ref, crossed_ref, o_cross, third_ref, o_grad, o_win,
-    v_grad, v_fin, local, send_sem, recv_sem,
-):
-    h = Here()
-    w = Wire(h, send_sem, recv_sem)
-
-    def win_slot(f):
-        return o_win.at[:, f]
-
-    own = [
-        LocalCopy(grad, v_grad, o_grad.at[h.c], local.at[0]),
-        LocalCopy(fin, v_fin, win_slot(h.f), local.at[1]),
-    ]
-    greet(near_devices(h))
-    z_gather = ZGather(w, win_slot, 0, fin)
-    grad_gather = ClipGather(
-        w,
-        lambda c, half: o_grad.at[c, pl.ds(128 * half, 128), :],
-        10,
-        lambda half: grad.at[pl.ds(128 * half, 128), :],
-    )
-    z_gather.step(1)
-    grad_gather.begin()
-    z_gather.relay(0)
-    for copy in own:
-        copy.turn()
-    att_value = att[...].reshape(256, 1024)
-    after_self = hid[...].reshape(256, 1024).astype(F32) + dot(att_value, square_of(square, 0), (1, 0))
-    o_self[...] = after_self
-    xhat, _ = norm_parts(after_self)
-    second_ref[...] = (xhat * params[1:2, :] + params[4:5, :]).astype(BF16)
-    z_gather.step(2)
-    query_ref[...] = dot(second_ref[...], square_of(square, 1), (1, 0)).astype(BF16)
-    grad_gather.middle()
     lane_head = lax.broadcasted_iota(jnp.int32, (128, 256), 1) // HD
     for clip in range(2):
         for group in range(4):
@@ -1122,74 +1045,29 @@
             query = query_ref[rows, columns] * jnp.asarray(HD**-0.5, BF16)
             probs, _ = text_probs(query, tkv[clip, 0, :, columns], text_bias[clip : clip + 1, :], lane_head)
             part = dot(probs.astype(BF16), tkv[clip, 1, :, columns], (1, 0))
-            crossed_ref[rows, columns] = pick_heads(part, lane_head).astype(BF16)
-        z_gather.step(3 + clip)
-    for d in range(1, 4):
-        z_gather.relay(d)
-    after_cross = o_self[...] + dot(crossed_ref[...], square_of(square, 2), (1, 0))
-    o_cross[...] = after_cross
-    xhat, _ = norm_parts(after_cross)
-    third_ref[...] = (xhat * params[2:3, :] + params[5:6, :]).astype(BF16)
-    grad_gather.near()
-    grad_gather.end()
-    z_gather.end()
-    for copy in own:
-        copy.wait()
-    w.drain()
-
-
-def middle(hid, att, square, tkv, text_bias, params, grad, fin):
-    rows = (256, 1024)
-    return comm_call(
-        middle_body,
-        (
-            shape(rows, F32),
-            shape(rows),
-            shape(rows),
-            shape(rows),
-            shape(rows, F32),
-            shape(rows),
-            shape((4, 256, 1024)),
-            shape((4, 8, 32, 1024)),
-        ),
-        [VMEM] * 6 + [HBM] * 2,
-        (VMEM,) * 6 + (HBM,) * 2,
-        [
-            pltpu.VMEM((256, 1024), BF16),
-            pltpu.VMEM((4, 32, 1024), BF16),
-            pltpu.SemaphoreType.DMA((2,)),
-        ],
-        20,
-        16,
-        2,
-    )(hid, att, square, tkv, text_bias, params, grad, fin)
-
-
-def feed_body(
-    third, grad, win, fout, o_third, o_out, o_terms, o_sum,
-    tokens, wout, inner, slope, g_pre, terms, slots, out_w, inbox, sums, left, right, local, send_sem, recv_sem,
-):
-    h = Here()
-    w = Wire(h, send_sem, recv_sem)
-    own = [
-        pltpu.make_async_copy(third, tokens.at[h.c], local.at[0]),
-        pltpu.make_async_copy(fout, wout.at[h.f], local.at[1]),
-    ]
-    for copy in own:
-        copy.start()
-    greet(near_devices(h))
-    gather = ClipGather(
-        w,
-        lambda c, half: tokens.at[c, pl.ds(128 * half, 128), :],
-        0,
-        lambda half: third.at[pl.ds(128 * half, 128), :],
-    )
-    gather.begin()
-    z_gather = ZGather(w, lambda f: wout.at[f], 6, fout)
-    z_gather.step(1)
-    z_gather.relay(0)
-    for copy in own:
-        copy.wait()
+            crossed[rows, columns] = pick_heads(part, lane_head).astype(BF16)
+        if clip == 0:
+            win_gather.step(4)
+            for d in range(1, 4):
+                win_gather.relay(d)
+    own[8].wait()
+    out_gather = ZGather(w, lambda f: wout.at[f], T_WOUT)
+    out_gather.step(1)
+    out_gather.relay(0)
+    value = after_self[...] + dot(crossed[...], square_of(sq, 2), (1, 0))
+    after_cross[...] = value
+    xhat, _ = norm_parts(value)
+    tokens[h.c] = (xhat * params[2:3, :] + params[5:6, :]).astype(BF16)
+
+    token_gather = ClipGather(w, lambda c, half: tokens.at[c, pl.ds(128 * half, 128), :], T_TOK)
+    token_gather.begin()
+    for src, dst in (
+        (att, o_att), (tkv, o_tkv), (sq, o_square), (second, o_second), (query_ref, o_query), (crossed, o_crossed),
+        (after_self, o_self), (after_cross, o_cross),
+    ):
+        save(src, dst)
+    win_copy.wait()
+    win_gather.end()
 
     def hidden(c):
         for part in range(2):
@@ -1200,48 +1078,47 @@
             slope[c, rows, :] = cdf + pre * jnp.exp(-0.5 * pre * pre) * 0.3989422804014327
 
     def hidden_back(c):
-        g_inner = dot(grad[c], wout[...].reshape(1024, 1024), (1, 1))
+        g_inner = dot(grad_all[c], wout[...].reshape(1024, 1024), (1, 1))
         g_pre[c] = (g_inner * slope[c]).astype(BF16)
         terms[c] = dot(g_pre[c], win[...].reshape(1024, 1024), (1, 1)).astype(BF16)
 
     def out_terms(c):
-        o_out[c] = dot(inner[c], wout[...].reshape(1024, 1024), (1, 0)).astype(BF16)
-
-    hidden(h.c)
-    z_gather.step(2)
-    gather.middle()
-    gather.near()
-    z_gather.step(3)
-    hidden(h.cx)
-    z_gather.step(4)
-    for d in range(1, 4):
-        z_gather.relay(d)
-    hidden(h.cy)
-    gather.end()
-    hidden(h.cd)
-    z_gather.end()
-    scatter = ClipScatter(
-        w,
-        lambda c, half: terms.at[c, pl.ds(128 * half, 128), :],
-        [slots.at[i] for i in range(6)],
-        16,
-    )
-    sibling = SiblingSum(w, lambda f: out_w.at[f], lambda z: inbox.at[z], lambda z: sums.at[z], 22)
-    z_scatter = ZScatter(w, sums, left, right, 26)
+        out_ref[c] = dot(inner[c], wout[...].reshape(1024, 1024), (1, 0)).astype(BF16)
+
+    sibling = SiblingSum(w, lambda f: out_w.at[f], lambda z: inbox.at[z], lambda z: sums.at[z], T_OSIB)
+    z_scatter = ZScatter(w, sums, near, far, T_OZ)
     tall = (1024, 1024)
 
     def out_weight(i, _):
         columns = pl.ds(pl.multiple_of(i * 256, 256), 256)
-        out = dot(inner[:, :, columns].reshape(1024, 256), grad[...].reshape(tall), (0, 0))
+        out = dot(inner[:, :, columns].reshape(1024, 256), grad_all[...].reshape(tall), (0, 0))
         out_w[pl.ds(2 * i, 2)] = out.astype(BF16).reshape(2, 128, 1024)
         return 0
 
     def in_weight(i, _):
         columns = pl.ds(pl.multiple_of(i * 256, 256), 256)
         out = dot(tokens[:, :, columns].reshape(1024, 256), g_pre[...].reshape(tall), (0, 0))
-        o_terms[:, pl.ds(pl.multiple_of(32 * i, 32), 32), :] = out.astype(BF16).reshape(8, 32, 1024)
+        in_ref[:, pl.ds(pl.multiple_of(32 * i, 32), 32), :] = out.astype(BF16).reshape(8, 32, 1024)
         return 0
 
+    hidden(h.c)
+    out_gather.step(2)
+    grad_gather.near()
+    grad_gather.end()
+    token_gather.middle()
+    token_gather.near()
+    out_gather.step(3)
+    hidden(h.cx)
+    hidden(h.cy)
+    out_gather.step(4)
+    for d in range(1, 4):
+        out_gather.relay(d)
+    token_gather.end()
+    hidden(h.cd)
+    out_gather.end()
+    scatter = ClipScatter(
+        w, lambda c, half: terms.at[c, pl.ds(128 * half, 128), :], [slots.at[i] for i in range(6)], T_TERM
+    )
     hidden_back(h.cd)
     scatter.begin(0)
     hidden_back(h.cx)
@@ -1256,46 +1133,120 @@
     lax.fori_loop(0, 2, in_weight, 0)
     z_scatter.step(1)
     lax.fori_loop(2, 4, in_weight, 0)
+    save(in_ref, o_in)
     out_terms(0)
     z_scatter.step(2)
     z_scatter.step(3)
     out_terms(1)
     out_terms(2)
     out_terms(3)
+    save(out_ref, o_out)
     scatter.end()
     for half in range(2):
         o_third[128 * half : 128 * half + 128, :] = scatter.total(half)
     z_scatter.total(o_sum)
     w.drain()
-    z_scatter.drain()
-
-
-def feed(third, grad, win, fout):
-    full = (4, 256, 1024)
+    for copy in forwards:
+        pl.when(h.is_gate)(copy.wait_send)
+    for away, copy, _ in att_sends:
+        pl.when(away)(copy.wait_send)
+    for one in (z_gather, win_gather, out_gather, z_scatter):
+        one.drain()
+    for copy in saves:
+        copy.wait()
+
+
+def forward(*args):
+    column, rows, full, quarter = (1024, 256), (256, 1024), (4, 256, 1024), (4, 128, 1024)
+    kept = [
+        shape((8, 128, 1024)),
+        shape((1024, 1024)),
+        shape(column),
+        shape(column),
+        shape(column),
+        shape(column),
+        shape((8, 1024), F32),
+        shape((4, 8, 112, 256)),
+        shape((4, 8, 64, 256)),
+        shape((8, 1024), F32),
+        shape((2, 128, 1024)),
+        shape((2, 2, 128, 1024)),
+        shape((4, 8, 96, 1024)),
+        shape(rows),
+        shape(rows),
+        shape(rows),
+        shape(rows, F32),
+        shape(rows, F32),
+        shape(full),
+        shape((8, 128, 1024)),
+    ]
     return comm_call(
-        feed_body,
-        (shape((256, 1024), F32), shape(full), shape((8, 128, 1024)), shape((128, 1024), F32)),
-        [HBM, VMEM, VMEM, HBM],
-        (VMEM,) * 4,
-        [
+        forward_body,
+        tuple(kept) + (shape(rows, F32), shape((128, 1024), F32)),
+        [SMEM, VMEM, VMEM] + [HBM] * 8,
+        (HBM,) * len(kept) + (VMEM,) * 2,
+        [pltpu.VMEM(one.shape, one.dtype) for one in kept]
+        + [
+            pltpu.VMEM((256, ROWS), F32),
+            pltpu.VMEM((256, 1024), BF16),
+            pltpu.VMEM((2, 2, 128, 256), BF16),
+            pltpu.VMEM((2, 128, 1024), BF16),
+            pltpu.VMEM((2, 128, 1024), BF16),
+            pltpu.VMEM((4, 32, 1024), BF16),
             pltpu.VMEM(full, BF16),
+            pltpu.VMEM((4, 8, 32, 1024), BF16),
             pltpu.VMEM((8, 128, 1024), BF16),
+            pltpu.VMEM(full, BF16),
             pltpu.VMEM(full, BF16),
             pltpu.VMEM(full, F32),
             pltpu.VMEM(full, BF16),
             pltpu.VMEM(full, BF16),
             pltpu.VMEM((6, 128, 1024), BF16),
             pltpu.VMEM((8, 128, 1024), BF16),
-            pltpu.VMEM((4, 128, 1024), BF16),
-            pltpu.VMEM((4, 128, 1024), BF16),
+            pltpu.VMEM(quarter, BF16),
+            pltpu.VMEM(quarter, BF16),
             pltpu.VMEM((3, 128, 1024), BF16),
             pltpu.VMEM((2, 128, 1024), BF16),
-            pltpu.SemaphoreType.DMA((2,)),
+            pltpu.SemaphoreType.DMA((12,)),
+            pltpu.SemaphoreType.DMA((24,)),
         ],
-        48,
-        32,
-        3,
-    )(third, grad, win, fout)
+        192,
+        144,
+        1,
+    )(*args)
+
+
+def attend_back_rows(i, length, bias, q_ref, k_ref, v_ref, o_ref, lse_ref, g_ref, dq_ref, dq_t, k_t, dk, dv):
+    lane_head = lax.broadcasted_iota(jnp.int32, (ROWS, 256), 1) // HD
+    first, n = i * ROWS, (i + 1) * ROWS
+    q = q_ref[first:n, :] * jnp.asarray(HD**-0.5, BF16)
+    live = first + lax.broadcasted_iota(jnp.int32, (ROWS, 256), 0) < length[0]
+    g = jnp.where(live, g_ref[first:n, :], 0)
+    both = (g.astype(F32) * o_ref[first:n, :].astype(F32)).T
+    row_dots = jnp.concatenate(
+        [jnp.sum(both[HD * j : HD * j + HD], axis=0, keepdims=True) for j in range(4)], axis=0
+    )
+    lse = lse_ref[0:4, first:n]
+
+    def pick(rows, j):
+        at = lax.broadcasted_iota(jnp.int32, rows.shape, 0) == j
+        return jnp.sum(jnp.where(at, rows, 0), axis=0, keepdims=True)
+
+    def head(j, _):
+        q_head = jnp.where(lane_head == j, q, 0)
+        g_head = jnp.where(lane_head == j, g, 0)
+        scores = mask_scores(dot(k_ref[0:n, :], q_head, (1, 1)), bias, first, ROWS)
+        probs = jnp.exp(scores - pick(lse, j))
+        grads = dot(v_ref[0:n, :], g_head, (1, 1))
+        dlogits = (probs * (grads - pick(row_dots, j))).astype(BF16)
+        dv[0:n, :] += dot(probs.astype(BF16), g_head, (1, 0))
+        dk[0:n, :] += dot(dlogits, q_head, (1, 0))
+        at = pl.ds(pl.multiple_of(j * HD, HD), HD)
+        dq_t[at, :] = dot(k_t[at, 0:n], dlogits, (1, 0))
+        return 0
+
+    lax.fori_loop(0, 4, head, 0)
+    dq_ref[first:n, :] = (dq_t[...].T * (HD**-0.5)).astype(BF16)
 
 
 def norm_back(xhat, scale, grad, gain):
@@ -1775,17 +1726,16 @@
     my_mask = lax.dynamic_slice_in_dim(frame_mask, pair, 1, 0)[0]
     bias = jnp.where((columns < my_len) & (my_mask > 0), 0.0, NEG).astype(F32)
     bias = jnp.broadcast_to(bias[:, None], (1024, 128))
-    (
-        hid_all, first_low, query, key, value, att_heads, lse, w_a, w_b, params, att, tkv, square, fin_all
-    ) = front(my_len, bias, text_states, hidden_in, cols_a, cols_b, square_here, ffn_in)
-    square = square.reshape(32, 96, 1024)
     slots = jnp.arange(128, dtype=jnp.int32)
     text_ok = (slots[None] < text_len[:, None]) & ((text_mask > 0) | (slots[None] == 0))
     text_bias = jnp.where(text_ok, 0.0, NEG).astype(F32)
-    after_self, second, cross_query, crossed, after_cross, third, grad_all, ffn_w_in = middle(
-        hidden_in, att, square, tkv, text_bias, params, out_grad.reshape(256, 1024), fin_all
-    )
-    third_sum, out_terms, in_terms, grad_ffn_out = feed(third, grad_all, ffn_w_in, ffn_out)
+    (
+        hid_all, first_low, query, key, value, att_heads, lse, w_a, w_b, params, att, tkv, square,
+        second, cross_query, crossed, after_self, after_cross, out_terms, in_terms, third_sum, grad_ffn_out,
+    ) = forward(
+        my_len, bias, text_bias, text_states, hidden_in, cols_a, cols_b, square_here, ffn_in, ffn_out,
+        out_grad.reshape(256, 1024),
+    )
     g_after_self, g_square, z_square, g_heads, g_tkv, g_norms, output, grad_ffn_in = middle_back(
         third_sum, out_grad, after_cross, after_self, second, cross_query, crossed, att, square, tkv,
         text_bias, params, out_terms, in_terms,

time: 349 us -> 322 us (0.923)
  Pallas kernels: 322 us -> 295 us
    pallas_call x3 -> x1, Pallas kernels: 191 us -> 164 us  [forward(): comm_call(forward_body, tuple(kept) + (shape(rows, F32), shape((128, 1024...]
where the time goes in v4:
time: 322 us; the launch traced here: 318 us
  Pallas kernels  295 us (92%)
  local copies, waits for them, and re-layouts  13.8 us (4%)
  other arithmetic  7.36 us (2%)
    pallas_call x1, Pallas kernels, forward(): comm_call(forward_body, tuple(kept) + (shape(rows, F32), shape((128, 1024...  164 us
    pallas_call x1, Pallas kernels, last(): comm_call(last_body, (shape((2, 128, 1024)), shape((96, 1024), F32), shap...  74.7 us
    pallas_call x1, Pallas kernels, middle_back(): comm_call(middle_back_body, (shape(rows, F32), shape((4, 8, 32, 1024)), s...  56.4 us

profile of v4, /device:TPU:0, one launch (start us, length us, event | category | flops | bytes accessed | tf_op | source)
XLA Modules:
  0.0 317.6 jit_solution(14364383846477134069)
XLA Ops:
  0.7 1.2 dynamic_slice.9.length
  1.9 0.7 compare_reduce_fusion
  2.6 1.3 and_select_fusion.text_bias
  4.0 0.7 pad_maximum_fusion.3
  4.7 0.6 fusion.1
  5.3 0.3 dynamic_update_slice.6
  5.7 0.8 slice_bitcast_fusion.3
  6.6 1.6 pad_maximum_fusion.2.square
  8.1 1.6 slice.36
  9.7 1.6 pad_maximum_fusion.1.cols_a
  11.3 1.0 broadcast_in_dim.28.bias
  12.3 164.4 %shard_map.230 = (bf16[8,128,1024]{2,1,0:T(8,128)(2,1)}, bf16[1024,1024]{1,0:T(8,128)(2,1)}, bf16[1024,256]{1,0:T(8,128)(2,1)}, bf16[1024,256]{1,0:T(8,128)(2,1)...) custom-call(s32[1]{0:T(128)} %dynamic_slice.9.length, ...), custom_call_target="tpu_custom_call" | custom-call | tf_op jit(solution)/shard_map/pallas_call | solution.py:1183
  176.7 56.4 %shard_map.231 = (f32[256,1024]{1,0:T(8,128)}, bf16[4,8,32,1024]{3,2,1,0:T(8,128)(2,1)}, bf16[4,64,1024]{2,1,0:T(8,128)(2,1)}, bf16[8,128,256]{2,1,0:T(8,128)(2,...) custom-call(f32[256,1024]{1,0:T(8,128)} %get-tuple-element.47.g_third, ...), custom_call_target="tpu_custom_call" | custom-call | tf_op jit(solution)/shard_map/pallas_call | solution.py:1412
  233.1 74.7 %shard_map.232 = (bf16[2,128,1024]{2,1,0:T(8,128)(2,1)}, f32[96,1024]{1,0:T(8,128)}, f32[3,32,1024]{2,1,0:T(8,128)}, f32[2,32,1024]{2,1,0:T(8,128)}, f32[16,128]{1,0:T(8,128)}, /*index=5*/bf16[2,16,1024]{2,1,0:T(8,128)(2,1)}) custom-call(s32[1]{0:T(128)} %dynamic_slice.9.length, f32[1024,128]{1,0:T(8,128)} %broadcast_in_dim.28.bias, ...), custom_call_target="tpu_custom_call" | custom-call | tf_op jit(solution)/shard_map/pallas_call | solution.py:1646
  307.8 0.0 copy-start.2
  307.8 0.0 copy-start.3
  307.8 0.8 constant_dynamic-slice_fusion
  308.6 0.6 fusion.3
  309.2 0.0 copy-start.5
  309.2 0.0 copy-start.4
  309.2 1.0 slice_bitcast_fusion.1
  310.3 1.8 fusion.2
  312.0 0.0 copy-start.1
  312.0 0.8 pad_maximum_fusion
  312.8 0.0 copy-done.2
  312.8 0.0 copy-start
  312.8 0.8 copy.34
  313.6 0.0 copy-done.3
  313.6 0.8 copy.35
  314.4 0.0 copy-done.5
  314.4 0.6 copy.36
  315.0 0.0 copy-done.4
  315.0 0.7 copy.37
  315.8 0.0 copy-done.1
  315.8 0.8 copy.38
  316.6 0.0 copy-done
  316.6 0.8 copy.39
  (4 shorter events, 0.0 us)
Async XLA Ops:
  307.8 5.0 %copy-start.2 = (bf16[256,1024]{1,0:T(8,128)(2,1)S(1)}, bf16[256,1024]{1,0:T(8,128)(2,1)}, u32[]{:S(2)}) copy-start(bf16[256,1024]{1,0:T(8,128)(2,1)} %get-tuple-element.59) | copy-start | bytes 1572868
  307.8 5.8 %copy-start.3 = (bf16[2,128,1024]{2,1,0:T(8,128)(2,1)S(1)}, bf16[2,128,1024]{2,1,0:T(8,128)(2,1)}, u32[]{:S(2)}) copy-start(bf16[2,128,1024]{2,1,0:T(8,128)(2,1)} %get-tuple-element.102) | copy-start | bytes 1572868
  309.2 5.2 %copy-start.5 = (bf16[2,16,1024]{2,1,0:T(8,128)(2,1)S(1)}, bf16[2,16,1024]{2,1,0:T(8,128)(2,1)}, u32[]{:S(2)}) copy-start(bf16[2,16,1024]{2,1,0:T(8,128)(2,1)} %get-tuple-element.103) | copy-start | bytes 196612
  309.2 5.8 %copy-start.4 = (f32[3,32,1024]{2,1,0:T(8,128)S(1)}, f32[3,32,1024]{2,1,0:T(8,128)}, u32[]{:S(2)}) copy-start(f32[3,32,1024]{2,1,0:T(8,128)} %get-tuple-element.77) | copy-start | bytes 1179652
  312.0 3.8 %copy-start.1 = (f32[32,4096]{1,0:T(8,128)S(1)}, f32[32,4096]{1,0:T(8,128)}, u32[]{:S(2)}) copy-start(f32[32,4096]{1,0:T(8,128)} %get-tuple-element.108) | copy-start | bytes 1572868
  312.8 3.8 %copy-start = (f32[128,1024]{1,0:T(8,128)S(1)}, f32[128,1024]{1,0:T(8,128)}, u32[]{:S(2)}) copy-start(f32[128,1024]{1,0:T(8,128)} %get-tuple-element.109) | copy-start | bytes 1572868

commit v5 on v4

--- a/solution.py
+++ b/solution.py
@@ -667,11 +667,11 @@
         @pl.when(h.is_gate)
         def _():
             others = self.near[2].astype(F32) + self.far[1].astype(F32)
-            out[...] = self.terms[h.z].astype(F32) + others
+            out[...] = (self.terms[h.z].astype(F32) + others).astype(out.dtype)
 
         @pl.when(jnp.logical_not(h.is_gate))
         def _():
-            out[...] = self.terms[h.z].astype(F32) + self.far[0].astype(F32)
+            out[...] = (self.terms[h.z].astype(F32) + self.far[0].astype(F32)).astype(out.dtype)
 
     def drain(self):
         for go, copy in self.open:
@@ -1062,10 +1062,12 @@
     token_gather = ClipGather(w, lambda c, half: tokens.at[c, pl.ds(128 * half, 128), :], T_TOK)
     token_gather.begin()
     for src, dst in (
-        (att, o_att), (tkv, o_tkv), (sq, o_square), (second, o_second), (query_ref, o_query), (crossed, o_crossed),
+        (att, o_att), (tkv, o_tkv), (second, o_second), (query_ref, o_query), (crossed, o_crossed),
         (after_self, o_self), (after_cross, o_cross),
     ):
         save(src, dst)
+    for which in range(3):
+        save(sq.at[:, :, pl.ds(32 * which, 32), :], o_square.at[which])
     win_copy.wait()
     win_gather.end()
 
@@ -1180,12 +1182,14 @@
         shape(full),
         shape((8, 128, 1024)),
     ]
+    scratch = [pltpu.VMEM(one.shape, one.dtype) for one in kept]
+    kept[12] = shape((3, 4, 8, 32, 1024))
     return comm_call(
         forward_body,
         tuple(kept) + (shape(rows, F32), shape((128, 1024), F32)),
         [SMEM, VMEM, VMEM] + [HBM] * 8,
         (HBM,) * len(kept) + (VMEM,) * 2,
-        [pltpu.VMEM(one.shape, one.dtype) for one in kept]
+        scratch
         + [
             pltpu.VMEM((256, ROWS), F32),
             pltpu.VMEM((256, 1024), BF16),
@@ -1258,51 +1262,90 @@
     )
 
 
-def middle_back_body(
-    g_third, g_out, after_cross, after_self, second, query_ref, crossed, att, square, tkv, text_bias, params,
-    out_terms, in_terms,
-    o_after_self, o_square, o_zsquare, o_heads, o_text, o_norm, o_output, o_in,
-    g_crossed, g_query, g_att, g_text, slots, sums, from_sib, from_z,
-    i_inbox, i_sums, i_left, i_right, i_total, i_out, i_in,
-    g_square, s_inbox, s_sums, s_slots, local, send_sem, recv_sem,
+def backward_body(
+    length, bias, text_bias, norms_in,
+    h_third, h_out, h_cross, h_self, h_second, h_query, h_crossed, h_att, h_square, h_tkv, h_out_terms, h_in_terms,
+    h_q, h_k, h_v, h_o, h_lse, h_hid, h_first, h_wa, h_wb, h_text, h_own,
+    o_output, o_in, o_hidden, o_square, o_qkv, o_ckv, o_norm, o_text,
+    v_third, v_out, after_cross, query_ref, crossed, att, mats, tkv, out_terms,
+    q_ref, k_ref, v_ref, o_ref, lse, w_a, w_b, text_in,
+    g_crossed, g_att, g_after, slots, t_inbox, t_near, t_far, t_total,
+    i_inbox, i_near, i_far, i_out, i_in,
+    g_square, s_inbox, s_slots, s_part, y_part, z_near, z_far, y_near, y_far,
+    g_heads, dq_t, k_t, dk, dv, d_cols, f_inbox, f_in,
+    a_terms, a_slots, a_sum, a_in, b_terms, b_slots, b_sum, b_in,
+    t_terms, tt_in, n_row, n_terms, n_slots, n_sum, n_in,
+    loaded, local, send_sem, recv_sem,
 ):
     h = Here()
     w = Wire(h, send_sem, recv_sem)
-    T_HEADS, T_TSIB, T_TZ, T_OUT, T_IN, T_IZ, T_IC, T_SQ = 0, 7, 11, 14, 20, 24, 30, 33
+    tag = [0]
+
+    def tags(n):
+        tag[0] += n
+        return tag[0] - n
+
+    loads = []
+
+    def load(src, dst):
+        copy = pltpu.make_async_copy(src, dst, loaded.at[len(loads)])
+        copy.start()
+        loads.append(copy)
+        return copy
+
+    l_terms = load(h_out_terms, out_terms)
+    own_terms = [mats.at[0, z, pl.ds(0, 4)] for z in range(4)]
+    l_own = [load(h_in_terms.at[2 * z + h.core], own_terms[z]) for z in range(4)]
+    l_third, l_cross = load(h_third, v_third), load(h_cross, after_cross)
+    l_out, l_m2 = load(h_out, v_out), load(h_square.at[2], mats.at[2])
+    l_middle = [load(*pair) for pair in ((h_crossed, crossed), (h_query, query_ref), (h_tkv, tkv))]
+    l_m1 = load(h_square.at[1], mats.at[1])
+    l_att = load(h_att, att)
+    l_heads = [
+        load(*pair)
+        for pair in (
+            (h_q, q_ref), (h_k, k_ref), (h_v, v_ref), (h_o, o_ref), (h_lse, lse), (h_wb, w_b), (h_text, text_in),
+            (h_wa, w_a),
+        )
+    ]
     greet(frame_others(h) + clip_others(h))
-    scatter = ClipScatter(
+
+    def matrix(which):
+        return mats[which].reshape(1024, 1024)
+
+    out_scatter = ClipScatter(
         w,
         lambda c, half: out_terms.at[c, pl.ds(128 * half, 128), :],
         [slots.at[i] for i in range(6)],
-        T_OUT,
-    )
-    scatter.begin()
-    in_sibling = SiblingSum(
-        w, lambda f: in_terms.at[f], lambda z: i_inbox.at[z], lambda z: i_sums.at[z], T_IN
-    )
-    in_scatter = ZScatter(w, i_sums, i_left, i_right, T_IZ)
-    in_sibling.begin()
+        tags(6),
+    )
+    in_tag = tags(4)
+    for z in range(4):
+        w.send(h_in_terms.at[2 * z + 1 - h.core], i_inbox.at[z], in_tag + z, h.c, h.sib)
+    in_scatter = ZScatter(w, i_inbox, i_near, i_far, tags(5))
+    l_terms.wait()
+    out_scatter.begin()
 
     def square_sums(which):
         sibling = SiblingSum(
             w,
             lambda f: g_square.at[which, :, f],
             lambda z: s_inbox.at[which, z],
-            lambda z: s_sums.at[which, z],
-            T_SQ + 10 * which,
+            lambda z: s_inbox.at[which, z],
+            tags(4),
         )
         clip = ClipScatter(
             w,
-            lambda c, half: s_sums.at[which, :, c, pl.ds(16 * half, 16), :],
+            lambda c, half: s_inbox.at[which, :, c, pl.ds(16 * half, 16), :],
             [s_slots.at[which, i] for i in range(6)],
-            T_SQ + 10 * which + 4,
+            tags(6),
         )
         return sibling, clip
 
-    squares = [square_sums(0), square_sums(1)]
-
-    def put(ref, value):
-        ref[...] = value.astype(BF16).reshape(4, 8, 32, 1024)
+    squares = [square_sums(which) for which in range(3)]
+
+    def put(which, value):
+        g_square[which] = value.astype(BF16).reshape(4, 8, 32, 1024)
 
     def columns_of(f):
         return pl.ds(pl.multiple_of(lax.rem(f, 4) * 256, 256), 256)
@@ -1313,18 +1356,35 @@
     def text_part(f):
         return g_text.at[lax.div(f, 4), :, :, columns_of(f)]
 
+    for copy in (l_third, l_cross, l_out):
+        copy.wait()
     xhat, scale = norm_parts(after_cross[...])
-    grad = g_third[...]
-    o_norm[0:1, :] = jnp.sum(grad * xhat, axis=0, keepdims=True)
-    o_norm[1:2, :] = jnp.sum(grad, axis=0, keepdims=True)
-    g_after_cross = g_out[...].reshape(256, 1024).astype(F32) + norm_back(xhat, scale, grad, params[2:3, :])
-    o_after_self[...] = g_after_cross
+    grad = v_third[...]
+    gain_third = jnp.sum(grad * xhat, axis=0, keepdims=True)
+    shift_third = jnp.sum(grad, axis=0, keepdims=True)
+    n_row[...] = jnp.zeros_like(n_row)
+    n_row[2:3, :] = gain_third
+    n_row[5:6, :] = shift_third
+    g_after_cross = v_out[...].reshape(256, 1024).astype(F32) + norm_back(xhat, scale, grad, norms_in[2:3, :])
+    g_after[...] = g_after_cross
+    after_self, own_hid = v_third, v_out
+    l_self, l_own_hid = load(h_self, after_self), load(h_own, own_hid)
     branch = g_after_cross.astype(BF16)
-    g_crossed[...] = dot(branch, square_of(square, 2), (1, 1)).astype(BF16)
-    put(g_square.at[1], dot(crossed[...], branch, (0, 0)))
-    squares[1][0].begin()
-    in_sibling.end()
+    l_m2.wait()
+    g_crossed[...] = dot(branch, matrix(2), (1, 1)).astype(BF16)
+    l_first = load(h_first, mats.at[2])
+    for copy in l_middle + l_own:
+        copy.wait()
+    put(2, dot(crossed[...], branch, (0, 0)))
+    squares[2][0].begin()
+    second = crossed
+    l_second = load(h_second, second)
+    for z in range(4):
+        w.arrived(i_inbox.at[z], in_tag + z)
+        add_into(i_inbox.at[z], own_terms[z])
     in_scatter.begin()
+    l_m0 = load(h_square.at[0], mats.at[0])
+    g_query, g_text = query_ref, tkv
     lane_head = lax.broadcasted_iota(jnp.int32, (128, 256), 1) // HD
     for clip in range(2):
         for group in range(4):
@@ -1342,146 +1402,97 @@
             g_text[clip, 0, :, columns] = dot(g_logits, stacked, (0, 0)).astype(BF16)
             g_text[clip, 1, :, columns] = dot(probs.astype(BF16), g_stacked, (0, 0)).astype(BF16)
         if clip == 0:
-            scatter.middle()
+            out_scatter.middle()
             in_scatter.step(1)
+            squares[2][0].end()
+            squares[2][1].begin()
+    text_sibling = SiblingSum(w, text_part, lambda z: t_inbox.at[z], lambda z: t_inbox.at[z], tags(4))
+    text_sibling.begin()
+    l_m1.wait()
+    grad = dot(g_query[...], matrix(1), (1, 1))
+    l_hid = load(h_hid, mats.at[1])
+    l_self.wait()
+    xhat, scale = norm_parts(after_self[...])
+    n_row[1:2, :] = jnp.sum(grad * xhat, axis=0, keepdims=True)
+    n_row[4:5, :] = jnp.sum(grad, axis=0, keepdims=True)
+    g_after_self = g_after[...] + norm_back(xhat, scale, grad, norms_in[1:2, :])
+    g_after[...] = g_after_self
+    branch = g_after_self.astype(BF16)
+    l_m0.wait()
+    g_att[...] = dot(branch, matrix(0), (1, 1)).astype(BF16).reshape(2, 128, 1024)
+    heads_tag = tags(7)
+    for d in (4, 2, 6, 3, 5, 1, 7):
+        f = h.step(d)
+        w.send(part_of(f), g_heads.at[h.f], heads_tag + d - 1, h.c, f)
+    own_part = pltpu.make_async_copy(part_of(h.f), g_heads.at[h.f], local.at[0])
+    own_part.start()
     in_scatter.step(2)
+    in_scatter.step(3)
+    l_second.wait()
+    l_att.wait()
+    put(1, dot(second[...], g_query[...], (0, 0)))
+    squares[1][0].begin()
+    put(0, dot(att[...].reshape(256, 1024), branch, (0, 0)))
+    squares[0][0].begin()
+    text_sibling.end()
+    text_scatter = ZScatter(w, t_inbox, t_near, t_far, tags(5))
+    text_scatter.begin()
+    squares[2][1].middle()
     squares[1][0].end()
     squares[1][1].begin()
-    text_sibling = SiblingSum(
-        w, text_part, lambda z: from_sib.at[z], lambda z: sums.at[z], T_TSIB
-    )
-    text_sibling.begin()
-    grad = dot(g_query[...], square_of(square, 1), (1, 1))
-    xhat, scale = norm_parts(after_self[...])
-    o_norm[2:3, :] = jnp.sum(grad * xhat, axis=0, keepdims=True)
-    o_norm[3:4, :] = jnp.sum(grad, axis=0, keepdims=True)
-    o_norm[4:8, :] = jnp.zeros((4, 1024), F32)
-    g_after_self = o_after_self[...] + norm_back(xhat, scale, grad, params[1:2, :])
-    o_after_self[...] = g_after_self
-    branch = g_after_self.astype(BF16)
-    g_att[...] = dot(branch, square_of(square, 0), (1, 1)).astype(BF16).reshape(2, 128, 1024)
-    for d in (4, 2, 6, 3, 5, 1, 7):
-        f = h.step(d)
-        w.send(part_of(f), o_heads.at[h.f], T_HEADS + d - 1, h.c, f)
-    copy = pltpu.make_async_copy(part_of(h.f), o_heads.at[h.f], local.at[0])
-    copy.start()
-    in_scatter.step(3)
-    put(g_square.at[0], dot(second[...], g_query[...], (0, 0)))
-    squares[0][0].begin()
-    text_sibling.end()
-    for d in range(1, 4):
-        w.send(sums.at[lax.rem(h.z + d, 4)], from_z.at[d - 1], T_TZ + d - 1, h.c, h.zstep(d))
-    squares[1][1].middle()
-    put(o_square, dot(att[...].reshape(256, 1024), branch, (0, 0)))
+    out_scatter.end()
+    for half in range(2):
+        rows = pl.ds(128 * half, 128)
+        o_output[rows, :] = (after_cross[rows, :] + out_scatter.total(half)).astype(BF16)
     squares[0][0].end()
     squares[0][1].begin()
-    in_scatter.total(i_total)
-    i_out[...] = i_total[...].astype(BF16).reshape(4, 32, 1024)
+    in_scatter.total(i_out)
+    i_tag = tags(3)
     for i, (c, f) in enumerate(clip_others(h)):
-        w.send(i_out.at[c], i_in.at[h.c], T_IC + i, c, f)
+        w.send(i_out.at[c], i_in.at[h.c], i_tag + i, c, f)
     i_in[h.c] = i_out[h.c]
-    scatter.end()
-    for half in range(2):
-        rows = pl.ds(128 * half, 128)
-        o_output[rows, :] = (after_cross[rows, :] + scatter.total(half)).astype(BF16)
-    squares[0][1].middle()
-    for which in (1, 0):
+    squares[1][1].middle()
+
+    def square_part(which, out, row):
         squares[which][1].end()
         for half in range(2):
             total = squares[which][1].total(half)
-            o_zsquare[:, 32 * which + 16 * half : 32 * which + 16 * half + 16, :] = total.astype(BF16)
-    for d in range(1, 4):
-        w.arrived(from_z.at[d - 1], T_TZ + d - 1)
-    total = sums[h.z].astype(F32)
-    for d in range(3):
-        total = total + from_z[d].astype(F32)
-    o_text[...] = total.astype(BF16)
-    for i, (c, f) in enumerate(clip_others(h)):
-        w.arrived(i_in.at[c], T_IC + i)
-    for c in range(4):
-        o_in[:, 1024 * c : 1024 * c + 1024] = i_in[c].astype(F32)
+            out[:, row + 16 * half : row + 16 * half + 16, :] = total.astype(BF16)
+
+    text_scatter.step(1)
+    for copy in l_heads:
+        copy.wait()
+    k_t[...] = k_ref[...].T
+    dk[...] = jnp.zeros_like(dk)
+    dv[...] = jnp.zeros_like(dv)
     for d in range(1, 8):
-        w.arrived(o_heads.at[lax.rem(h.f + 8 - d, 8)], T_HEADS + d - 1)
-    copy.wait()
-    w.drain()
-    in_scatter.drain()
-
-
-def middle_back(*args):
-    rows, block, quarter = (256, 1024), (2, 128, 256), (4, 128, 1024)
-    return comm_call(
-        middle_back_body,
-        (
-            shape(rows, F32),
-            shape((4, 8, 32, 1024)),
-            shape((4, 64, 1024)),
-            shape((8, 128, 256)),
-            shape(block),
-            shape((8, 1024), F32),
-            shape(rows),
-            shape((32, 4096), F32),
-        ),
-        [VMEM] * 14,
-        (VMEM,) * 8,
-        [
-            pltpu.VMEM(rows, BF16),
-            pltpu.VMEM(rows, BF16),
-            pltpu.VMEM((2, 128, 1024), BF16),
-            pltpu.VMEM((2, 2, 128, 1024), BF16),
-            pltpu.VMEM((6, 128, 1024), BF16),
-            pltpu.VMEM((4,) + block, BF16),
-            pltpu.VMEM((4,) + block, BF16),
-            pltpu.VMEM((3,) + block, BF16),
-            pltpu.VMEM(quarter, BF16),
-            pltpu.VMEM(quarter, BF16),
-            pltpu.VMEM((3, 128, 1024), BF16),
-            pltpu.VMEM((2, 128, 1024), BF16),
-            pltpu.VMEM((128, 1024), F32),
-            pltpu.VMEM((4, 32, 1024), BF16),
-            pltpu.VMEM((4, 32, 1024), BF16),
-            pltpu.VMEM((2, 4, 8, 32, 1024), BF16),
-            pltpu.VMEM((2, 4, 4, 32, 1024), BF16),
-            pltpu.VMEM((2, 4, 4, 32, 1024), BF16),
-            pltpu.VMEM((2, 6, 4, 16, 1024), BF16),
-            pltpu.SemaphoreType.DMA((1,)),
-        ],
-        80,
-        53,
-        4,
-    )(*args)
-
-
-def last_body(
-    length, bias, q_ref, k_ref, v_ref, o_ref, lse, g_heads, hid, first_low, w_a, w_b, text_in, g_tkv,
-    square, z_square, norms, own_hid, g_after, params,
-    o_hidden, o_square, o_qkv, o_ckv, o_norm, o_text,
-    dq_t, k_t, dk, dv, d_cols, f_terms, f_sib, f_sum, f_in, s_inbox, s_sums, s_slots, s_part,
-    z_left, z_right, y_left, y_right, a_terms, a_slots, a_sum, a_in, b_terms, b_slots, b_sum, b_in,
-    t_terms, t_in, n_row, n_terms, n_slots, n_sum, n_in, send_sem, recv_sem,
-):
-    h = Here()
-    w = Wire(h, send_sem, recv_sem)
-    T_S, T_SC, T_Z, T_Y, T_B, T_T, T_A, T_F, T_N = 0, 4, 10, 16, 22, 36, 44, 86, 94
-    greet(frame_others(h) + clip_others(h)[:2])
-    s_sibling = SiblingSum(
-        w, lambda f: square.at[:, f], lambda z: s_inbox.at[z], lambda z: s_sums.at[z], T_S
-    )
-    s_sibling.begin()
-    z_scatter = ZScatter(w, z_square, z_left, z_right, T_Z)
+        w.arrived(g_heads.at[lax.rem(h.f + 8 - d, 8)], heads_tag + d - 1)
+    own_part.wait()
+    g_rows = g_heads[...].reshape(1024, 256)
+
+    def rows_back(i):
+        attend_back_rows(
+            i, length, bias, q_ref, k_ref, v_ref, o_ref, lse, g_rows, d_cols.at[0], dq_t, k_t, dk, dv
+        )
+
+    text_scatter.step(2)
+    text_scatter.step(3)
+    squares[0][1].middle()
+    rows_back(0)
+    square_part(2, s_part, 32)
+    square_part(1, s_part, 0)
+    z_scatter = ZScatter(w, s_part, z_near, z_far, tags(5))
     z_scatter.begin()
-    s_scatter = ClipScatter(
-        w,
-        lambda c, half: s_sums.at[:, c, pl.ds(16 * half, 16), :],
-        [s_slots.at[i] for i in range(6)],
-        T_SC,
-    )
-    y_scatter = ZScatter(w, s_part, y_left, y_right, T_Y)
+    rows_back(1)
 
     class Columns:
-        def __init__(self, terms, slots, sums, inbox, tag):
-            self.sums, self.inbox, self.tag = sums, inbox, tag
+        def __init__(self, terms, slots, sums, inbox):
+            self.sums, self.inbox, self.tag = sums, inbox, tags(13)
             self.clip = ClipScatter(
-                w, lambda c, half: terms.at[c, pl.ds(4 * half, 4)], [slots.at[i] for i in range(6)], tag
+                w,
+                lambda c, half: terms.at[c, pl.ds(4 * half, 4)],
+                [slots.at[i] for i in range(6)],
+                self.tag,
             )
 
         def spread(self):
@@ -1497,91 +1508,80 @@
             for d in range(1, 8):
                 w.arrived(self.inbox.at[lax.rem(h.f + 8 - d, 8)], self.tag + 5 + d)
 
+    text_scatter.total(t_total)
+    g_tkv = [t_total[j].astype(BF16) for j in range(2)]
     text = text_in[h.pair]
     for j in range(2):
         b_terms[:, :, 32 * j : 32 * j + 32, :] = (
             dot(text, g_tkv[j], (0, 0)).astype(BF16).reshape(4, 8, 32, 256)
         )
-    b_columns = Columns(b_terms, b_slots, b_sum, b_in, T_B)
+    b_columns = Columns(b_terms, b_slots, b_sum, b_in)
     b_columns.clip.begin()
     t_terms[...] = (
         dot(g_tkv[0], column_weight(w_b, 0), (1, 1)) + dot(g_tkv[1], column_weight(w_b, 1), (1, 1))
     ).astype(BF16)
+    tt_tag = tags(7)
     for d in range(1, 8):
         f = h.step(d)
         w.send(
-            t_terms.at[pl.ds(pl.multiple_of(f * 16, 16), 16), :], t_in.at[h.f], T_T + d - 1, h.c, f
+            t_terms.at[pl.ds(pl.multiple_of(f * 16, 16), 16), :], tt_in.at[h.f], tt_tag + d - 1, h.c, f
         )
-    t_in[h.f] = t_terms[pl.ds(pl.multiple_of(h.f * 16, 16), 16), :]
-
-    k_t[...] = k_ref[...].T
-    dk[...] = jnp.zeros_like(dk)
-    dv[...] = jnp.zeros_like(dv)
-
-    def rows_back(i):
-        attend_back_rows(
-            i, length, bias, q_ref, k_ref, v_ref, o_ref, lse, g_heads, d_cols.at[0], dq_t, k_t, dk, dv
-        )
-
-    rows_back(0)
-    s_sibling.end()
-    s_scatter.begin()
+    tt_in[h.f] = t_terms[pl.ds(pl.multiple_of(h.f * 16, 16), 16), :]
     z_scatter.step(1)
-    rows_back(1)
+    rows_back(2)
+    square_part(0, y_part, 0)
+    y_scatter = ZScatter(w, y_part, y_near, y_far, tags(5))
+    y_scatter.begin()
     z_scatter.step(2)
     z_scatter.step(3)
     b_columns.clip.middle()
-    rows_back(2)
-    s_scatter.middle()
-    b_columns.spread()
     rows_back(3)
     d_cols[1] = dk[...].astype(BF16)
     d_cols[2] = dv[...].astype(BF16)
-    a_columns = [
-        Columns(a_terms.at[j], a_slots.at[j], a_sum.at[j], a_in.at[j], T_A + 13 * j) for j in range(3)
-    ]
+    l_first.wait()
+    a_columns = [Columns(a_terms.at[j], a_slots.at[j], a_sum.at[j], a_in.at[j]) for j in range(3)]
     for j in range(3):
-        a_terms[j] = dot(first_low[...], d_cols[j], (0, 0)).astype(BF16).reshape(4, 8, 32, 256)
+        a_terms[j] = dot(mats[2].reshape(1024, 1024), d_cols[j], (0, 0)).astype(BF16).reshape(4, 8, 32, 256)
         a_columns[j].clip.begin()
-
+    y_scatter.step(1)
+
+    f_terms = mats.at[0]
     f_sibling = SiblingSum(
-        w, lambda f: f_terms.at[f], lambda z: f_sib.at[z], lambda z: f_sum.at[z], T_F
-    )
-    n_row[...] = jnp.zeros_like(n_row)
+        w,
+        lambda f: f_terms.at[lax.div(f, 2), pl.ds(pl.multiple_of(lax.rem(f, 2) * 4, 4), 4)],
+        lambda z: f_inbox.at[z],
+        lambda z: f_inbox.at[z],
+        tags(4),
+    )
+    l_hid.wait()
 
     def frame_terms(i, _):
         rows = pl.ds(pl.multiple_of(i * 256, 256), 256)
         grad = sum(dot(d_cols[j, rows, :], column_weight(w_a, j), (1, 1)) for j in range(3))
-        f_terms[pl.ds(2 * i, 2)] = grad.astype(BF16).reshape(2, 128, 1024)
-        xhat, _ = norm_parts(hid[pl.ds(2 * i, 2)].reshape(256, 1024).astype(F32))
+        f_terms[i] = grad.astype(BF16).reshape(8, 32, 1024)
+        xhat, _ = norm_parts(mats[1, i].reshape(256, 1024).astype(F32))
         n_row[0:1, :] += jnp.sum(grad * xhat, axis=0, keepdims=True)
         n_row[3:4, :] += jnp.sum(grad, axis=0, keepdims=True)
         return 0
 
     lax.fori_loop(0, 4, frame_terms, 0)
     f_sibling.begin()
-    s_scatter.end()
-    for half in range(2):
-        s_part[:, 16 * half : 16 * half + 16, :] = s_scatter.total(half).astype(BF16)
-    y_scatter.begin()
+    y_scatter.step(2)
     a_columns[0].clip.middle()
     f_sibling.end()
+    f_tag = tags(4)
     other = 2 * (1 - h.pair)
     is_end = jnp.logical_not(h.is_gate)
     to_gate, to_far = [], []
     for j in range(2):
-        to_gate.append(w.copy(f_sum.at[other + j], f_in.at[1 + j], T_F + 5 + j, h.c, h.partner))
+        to_gate.append(w.copy(f_inbox.at[other + j], f_in.at[1 + j], f_tag + 1 + j, h.c, h.partner))
         pl.when(is_end)(to_gate[j].start)
-    w.send(f_sum.at[lax.div(h.partner, 2)], f_in.at[0], T_F + 4, h.c, h.partner)
-    n_row[1:2, :] = norms[2:3, :]
-    n_row[2:3, :] = norms[0:1, :]
-    n_row[4:5, :] = norms[3:4, :]
-    n_row[5:6, :] = norms[1:2, :]
+    w.send(f_inbox.at[lax.div(h.partner, 2)], f_in.at[0], f_tag, h.c, h.partner)
     for c in range(4):
         for f in range(8):
             group = 2 * c + f // 4
             n_terms[c, f] = n_row[:, 128 * group : 128 * group + 128].astype(BF16)
-    n_columns = Columns(n_terms, n_slots, n_sum, n_in, T_N)
+    n_columns = Columns(n_terms, n_slots, n_sum, n_in)
     n_columns.clip.begin()
     a_columns[1].clip.middle()
     a_columns[0].spread()
@@ -1589,54 +1589,59 @@
 
         @pl.when(h.is_gate)
         def _():
-            w.arrived(f_in.at[1 + j], T_F + 5 + j)
-            add_into(f_sum.at[other + j], f_in.at[1 + j])
-
-        to_far.append(w.copy(f_sum.at[other + j], f_in.at[3], T_F + 7, h.c, h.far[j]))
+            w.arrived(f_in.at[1 + j], f_tag + 1 + j)
+            add_into(f_inbox.at[other + j], f_in.at[1 + j])
+
+        to_far.append(w.copy(f_inbox.at[other + j], f_in.at[3], f_tag + 3, h.c, h.far[j]))
         pl.when(h.is_gate)(to_far[j].start)
-    y_scatter.step(1)
     a_columns[2].clip.middle()
     a_columns[1].spread()
     n_columns.clip.middle()
-    y_scatter.step(2)
     y_scatter.step(3)
     a_columns[2].spread()
     n_columns.spread()
+    b_columns.spread()
     z_scatter.total(o_square.at[pl.ds(32, 64), :])
+    for i, (c, f) in enumerate(clip_others(h)):
+        w.arrived(i_in.at[c], i_tag + i)
+    for c in range(4):
+        o_in[:, 1024 * c : 1024 * c + 1024] = i_in[c].astype(F32)
+    for d in range(1, 8):
+        w.arrived(tt_in.at[lax.rem(h.f + 8 - d, 8)], tt_tag + d - 1)
+    for p in range(2):
+        o_text[p] = sum(tt_in[4 * p + q].astype(F32) for q in range(4)).astype(BF16)
+    y_scatter.total(o_square.at[pl.ds(0, 32), :])
+    w.arrived(f_in.at[0], f_tag)
+    w.arrived(f_in.at[3], f_tag + 3)
+
+    def hidden_out(clip, total):
+        xhat, scale = norm_parts(own_hid[clip].astype(F32))
+        rows = pl.ds(pl.multiple_of(clip * 128, 128), 128)
+        o_hidden[clip] = (g_after[rows, :] + norm_back(xhat, scale, total, norms_in[0:1, :])).astype(BF16)
+
+    l_own_hid.wait()
+    hidden_out(h.pair, (f_inbox[h.z].astype(F32) + f_in[0].astype(F32)).reshape(128, 1024))
+    hidden_out(1 - h.pair, f_in[3].astype(F32).reshape(128, 1024))
+    for j in range(3):
+        a_columns[j].wait()
+        for q in range(4):
+            o_qkv[j, :, 256 * q : 256 * q + 256] = a_in[j, q].astype(F32) + a_in[j, 4 + q].astype(F32)
     b_columns.wait()
     for j in range(2):
         for q in range(4):
             at = pl.ds(32 * j, 32)
             o_ckv[j, :, 256 * q : 256 * q + 256] = b_in[q, at, :].astype(F32) + b_in[4 + q, at, :].astype(F32)
-    for d in range(1, 8):
-        w.arrived(t_in.at[lax.rem(h.f + 8 - d, 8)], T_T + d - 1)
-    for p in range(2):
-        o_text[p] = sum(t_in[4 * p + q].astype(F32) for q in range(4)).astype(BF16)
-    w.arrived(f_in.at[0], T_F + 4)
-    w.arrived(f_in.at[3], T_F + 7)
-
-    def hidden_out(clip, total):
-        xhat, scale = norm_parts(own_hid[clip].astype(F32))
-        o_hidden[clip] = (g_after[clip] + norm_back(xhat, scale, total, params[0:1, :])).astype(BF16)
-
-    hidden_out(h.pair, f_sum[h.z].astype(F32) + f_in[0].astype(F32))
-    hidden_out(1 - h.pair, f_in[3].astype(F32))
-    y_scatter.total(o_square.at[pl.ds(0, 32), :])
-    for j in range(3):
-        a_columns[j].wait()
-        for q in range(4):
-            o_qkv[j, :, 256 * q : 256 * q + 256] = a_in[j, q].astype(F32) + a_in[j, 4 + q].astype(F32)
     n_columns.wait()
     o_norm[...] = sum(n_in[f].astype(F32) for f in range(8))
     w.drain()
-    z_scatter.drain()
-    y_scatter.drain()
+    for one in (in_scatter, text_scatter, z_scatter, y_scatter):
+        one.drain()
     for j in range(2):
         pl.when(is_end)(to_gate[j].wait_send)
         pl.when(h.is_gate)(to_far[j].wait_send)
 
 
-def last(*args):
+def backward(*args):
     def buffer(*dims):
         return pltpu.VMEM(dims, BF16)
 
@@ -1644,8 +1649,10 @@
         return pltpu.VMEM(dims, F32)
 
     return comm_call(
-        last_body,
+        backward_body,
         (
+            shape((256, 1024)),
+            shape((32, 4096), F32),
             shape((2, 128, 1024)),
             shape((96, 1024), F32),
             shape((3, 32, 1024), F32),
@@ -1653,45 +1660,33 @@
             shape((16, 128), F32),
             shape((2, 16, 1024)),
         ),
-        [SMEM] + [VMEM] * 19,
-        (VMEM,) * 6,
+        [SMEM] + [VMEM] * 3 + [HBM] * 23,
+        (VMEM,) * 8,
         [
-            full(256, ROWS),
-            buffer(256, 1024),
-            full(1024, 256),
-            full(1024, 256),
-            buffer(3, 1024, 256),
-            buffer(8, 128, 1024),
-            buffer(4, 128, 1024),
-            buffer(4, 128, 1024),
-            buffer(4, 128, 1024),
-            buffer(4, 4, 32, 1024),
-            buffer(4, 4, 32, 1024),
-            buffer(6, 4, 16, 1024),
-            buffer(4, 32, 1024),
-            buffer(3, 64, 1024),
-            buffer(2, 64, 1024),
-            buffer(3, 32, 1024),
-            buffer(2, 32, 1024),
-            buffer(3, 4, 8, 32, 256),
-            buffer(3, 6, 4, 32, 256),
-            buffer(3, 8, 32, 256),
-            buffer(3, 8, 32, 256),
-            buffer(4, 8, 64, 256),
-            buffer(6, 4, 64, 256),
-            buffer(8, 64, 256),
-            buffer(8, 64, 256),
-            buffer(128, 1024),
-            buffer(8, 16, 1024),
-            full(16, 1024),
-            buffer(4, 8, 16, 128),
-            buffer(6, 4, 16, 128),
-            buffer(8, 16, 128),
-            buffer(8, 16, 128),
+            full(256, 1024), buffer(2, 128, 1024), full(256, 1024), buffer(256, 1024), buffer(256, 1024),
+            buffer(2, 128, 1024), buffer(3, 4, 8, 32, 1024), buffer(2, 2, 128, 1024), buffer(4, 256, 1024),
+            buffer(1024, 256), buffer(1024, 256), buffer(1024, 256), buffer(1024, 256), full(8, 1024),
+            buffer(4, 8, 112, 256), buffer(4, 8, 64, 256), buffer(2, 128, 1024),
+            buffer(256, 1024), buffer(2, 128, 1024), full(256, 1024),
+            buffer(6, 128, 1024), buffer(4, 2, 128, 256), buffer(3, 2, 128, 256), buffer(2, 2, 128, 256),
+            full(2, 128, 256),
+            buffer(4, 4, 32, 1024), buffer(3, 4, 32, 1024), buffer(2, 4, 32, 1024),
+            buffer(4, 32, 1024), buffer(4, 32, 1024),
+            buffer(3, 4, 8, 32, 1024), buffer(3, 4, 4, 32, 1024), buffer(3, 6, 4, 16, 1024),
+            buffer(4, 64, 1024), buffer(4, 32, 1024), buffer(3, 64, 1024), buffer(2, 64, 1024),
+            buffer(3, 32, 1024), buffer(2, 32, 1024),
+            buffer(8, 128, 256), full(256, ROWS), buffer(256, 1024), full(1024, 256), full(1024, 256),
+            buffer(3, 1024, 256), buffer(4, 4, 32, 1024), buffer(4, 4, 32, 1024),
+            buffer(3, 4, 8, 32, 256), buffer(3, 6, 4, 32, 256), buffer(3, 8, 32, 256), buffer(3, 8, 32, 256),
+            buffer(4, 8, 64, 256), buffer(6, 4, 64, 256), buffer(8, 64, 256), buffer(8, 64, 256),
+            buffer(128, 1024), buffer(8, 16, 1024), full(16, 1024), buffer(4, 8, 16, 128), buffer(6, 4, 16, 128),
+            buffer(8, 16, 128), buffer(8, 16, 128),
+            pltpu.SemaphoreType.DMA((32,)),
+            pltpu.SemaphoreType.DMA((1,)),
         ],
-        140,
-        107,
-        5,
+        208,
+        160,
+        2,
     )(*args)
 
 
@@ -1736,13 +1731,11 @@
         my_len, bias, text_bias, text_states, hidden_in, cols_a, cols_b, square_here, ffn_in, ffn_out,
         out_grad.reshape(256, 1024),
     )
-    g_after_self, g_square, z_square, g_heads, g_tkv, g_norms, output, grad_ffn_in = middle_back(
+    output, grad_ffn_in, grad_hidden, square_sum, qkv_sum, ckv_sum, norm_sum, grad_text = backward(
+        my_len, bias, text_bias, params,
         third_sum, out_grad, after_cross, after_self, second, cross_query, crossed, att, square, tkv,
-        text_bias, params, out_terms, in_terms,
-    )
-    grad_hidden, square_sum, qkv_sum, ckv_sum, norm_sum, grad_text = last(
-        my_len, bias, query, key, value, att_heads, lse, g_heads.reshape(1024, 256), hid_all, first_low, w_a, w_b,
-        text_states, g_tkv, g_square, z_square, g_norms, hidden_in, g_after_self.reshape(2, 128, 1024), params,
+        out_terms, in_terms.reshape(8, 4, 32, 1024), query, key, value, att_heads, lse, hid_all.reshape(4, 8, 32, 1024),
+        first_low.reshape(4, 8, 32, 1024), w_a, w_b, text_states, hidden_in,
     )
     norm_sum = lax.dynamic_slice(norm_sum, (0, 32 * (frame % 4)), (6, 32))
     return (

time: 322 us -> 299 us (0.929)
  Pallas kernels: 295 us -> 272 us
    pallas_call x2 -> x1, Pallas kernels: 131 us -> 107 us  [backward(): comm_call(backward_body, (shape((256, 1024)), shape((32, 4096), F32), sha...]
where the time goes in v5:
time: 299 us; the launch traced here: 294 us
  Pallas kernels  272 us (91%)
  local copies, waits for them, and re-layouts  13.8 us (5%)
  other arithmetic  7.36 us (2%)
    pallas_call x1, Pallas kernels, forward(): comm_call(forward_body, tuple(kept) + (shape(rows, F32), shape((128, 1024...  164 us
    pallas_call x1, Pallas kernels, backward(): comm_call(backward_body, (shape((256, 1024)), shape((32, 4096), F32), sha...  107 us

profile of v5, /device:TPU:0, one launch (start us, length us, event | category | flops | bytes accessed | tf_op | source)
XLA Modules:
  0.0 293.9 jit_solution(12108606823989142673)
XLA Ops:
  0.7 1.2 dynamic_slice.9.length
  1.9 0.7 compare_reduce_fusion
  2.6 1.3 and_select_fusion.text_bias
  4.0 0.7 pad_maximum_fusion.3
  4.7 0.6 fusion.1
  5.3 0.3 dynamic_update_slice.6
  5.7 0.8 slice_bitcast_fusion.3
  6.6 1.6 pad_maximum_fusion.2.square
  8.1 1.6 slice.36
  9.7 1.6 pad_maximum_fusion.1.cols_a
  11.3 1.0 broadcast_in_dim.28.bias
  12.3 164.3 %shard_map.230 = (bf16[8,128,1024]{2,1,0:T(8,128)(2,1)}, bf16[1024,1024]{1,0:T(8,128)(2,1)}, bf16[1024,256]{1,0:T(8,128)(2,1)}, bf16[1024,256]{1,0:T(8,128)(2,1)...) custom-call(s32[1]{0:T(128)} %dynamic_slice.9.length, ...), custom_call_target="tpu_custom_call" | custom-call | tf_op jit(solution)/shard_map/pallas_call | solution.py:1187
  176.7 107.4 %shard_map.231 = (bf16[256,1024]{1,0:T(8,128)(2,1)}, f32[32,4096]{1,0:T(8,128)}, bf16[2,128,1024]{2,1,0:T(8,128)(2,1)}, f32[96,1024]{1,0:T(8,128)}, f32[3,32,102...) custom-call(s32[1]{0:T(128)} %dynamic_slice.9.length, ...), custom_call_target="tpu_custom_call" | custom-call | tf_op jit(solution)/shard_map/pallas_call | solution.py:1651
  284.1 0.0 copy-start.3
  284.1 0.0 copy-start.2
  284.1 0.8 constant_dynamic-slice_fusion
  285.0 0.6 fusion.3
  285.5 0.0 copy-start.5
  285.5 0.0 copy-start.4
  285.6 1.0 slice_bitcast_fusion.1
  286.6 1.8 fusion.2
  288.4 0.0 copy-start.1
  288.4 0.8 pad_maximum_fusion
  289.1 0.0 copy-done.3
  289.1 0.0 copy-start
  289.1 0.8 copy.34
  289.9 0.0 copy-done.2
  289.9 0.8 copy.35
  290.7 0.0 copy-done.5
  290.7 0.6 copy.36
  291.4 0.0 copy-done.4
  291.4 0.7 copy.37
  292.1 0.0 copy-done.1
  292.1 0.8 copy.38
  292.9 0.0 copy-done
  292.9 0.8 copy.39
  (4 shorter events, 0.0 us)
Async XLA Ops:
  284.1 5.0 %copy-start.3 = (bf16[256,1024]{1,0:T(8,128)(2,1)S(1)}, bf16[256,1024]{1,0:T(8,128)(2,1)}, u32[]{:S(2)}) copy-start(bf16[256,1024]{1,0:T(8,128)(2,1)} %get-tuple-element.62) | copy-start | bytes 1572868
  284.1 5.8 %copy-start.2 = (bf16[2,128,1024]{2,1,0:T(8,128)(2,1)S(1)}, bf16[2,128,1024]{2,1,0:T(8,128)(2,1)}, u32[]{:S(2)}) copy-start(bf16[2,128,1024]{2,1,0:T(8,128)(2,1)} %get-tuple-element.90) | copy-start | bytes 1572868
  285.5 5.2 %copy-start.5 = (bf16[2,16,1024]{2,1,0:T(8,128)(2,1)S(1)}, bf16[2,16,1024]{2,1,0:T(8,128)(2,1)}, u32[]{:S(2)}) copy-start(bf16[2,16,1024]{2,1,0:T(8,128)(2,1)} %get-tuple-element.91) | copy-start | bytes 196612
  285.5 5.8 %copy-start.4 = (f32[3,32,1024]{2,1,0:T(8,128)S(1)}, f32[3,32,1024]{2,1,0:T(8,128)}, u32[]{:S(2)}) copy-start(f32[3,32,1024]{2,1,0:T(8,128)} %get-tuple-element.65) | copy-start | bytes 1179652
  288.4 3.8 %copy-start.1 = (f32[32,4096]{1,0:T(8,128)S(1)}, f32[32,4096]{1,0:T(8,128)}, u32[]{:S(2)}) copy-start(f32[32,4096]{1,0:T(8,128)} %get-tuple-element.96) | copy-start | bytes 1572868
  289.1 3.8 %copy-start = (f32[128,1024]{1,0:T(8,128)S(1)}, f32[128,1024]{1,0:T(8,128)}, u32[]{:S(2)}) copy-start(f32[128,1024]{1,0:T(8,128)} %get-tuple-element.97) | copy-start | bytes 1572868

commit v6 on v5

--- a/solution.py
+++ b/solution.py
@@ -580,6 +580,63 @@
             pl.when(go)(copy.wait_send)
 
 
+class MatrixGather:
+    def __init__(self, wire, block, rows, tag):
+        h = wire.here
+        self.wire, self.block, self.tag = wire, block, tag
+        self.z = ZGather(wire, lambda f: block(h.c, f), tag)
+        toward = 2 - 4 * h.pair
+        at_end = jnp.logical_not(h.is_gate)
+        self.order = [
+            h.f,
+            h.f + toward,
+            jnp.where(at_end, h.f + 2 * toward, h.f - toward),
+            jnp.where(at_end, h.f + 3 * toward, h.f + 2 * toward),
+        ]
+        self.clip = [
+            ClipGather(
+                wire,
+                lambda c, half, f=f: block(c, f).at[pl.ds(rows // 2 * half, rows // 2), :],
+                tag + 10 + 6 * d,
+            )
+            for d, f in enumerate(self.order)
+        ]
+
+    def step(self, s):
+        self.z.step(s)
+        self.clip[s - 1].begin()
+        self.z.relay(s - 1) if s == 1 else None
+        if s == 4:
+            for d in range(1, 4):
+                self.z.relay(d)
+
+    def _relay(self, d, i, c):
+        h, w = self.wire.here, self.wire
+        block = self.block(c, self.order[d])
+        w.send(block, block, self.tag + 34 + 3 * d + i, h.c, h.sib)
+
+    def middle(self, d):
+        self.clip[d].middle()
+
+    def near(self, d):
+        h = self.wire.here
+        self.clip[d].near()
+        self._relay(d, 0, h.cx)
+        self._relay(d, 1, h.cy)
+
+    def last(self, d):
+        self.clip[d].end()
+        self._relay(d, 2, self.wire.here.cd)
+
+    def end(self):
+        h, w = self.wire.here, self.wire
+        self.z.end()
+        for d in range(4):
+            f = self.order[d] + h.sib - h.f
+            for i, c in enumerate((h.cx, h.cy, h.cd)):
+                w.arrived(self.block(c, f), self.tag + 34 + 3 * d + i)
+
+
 class ClipScatter:
     def __init__(self, wire, parts, slots, tag):
         self.wire, self.parts, self.slots, self.tag = wire, parts, slots, tag
@@ -738,6 +795,22 @@
     return lax.dot_general(left, right, ((contract[:1], contract[1:]), ((), ())), preferred_element_type=F32)
 
 
+def fill_key_bias(bias, clip_len, frame_mask, clip):
+    column = lax.broadcasted_iota(jnp.int32, (1, 1024), 1)
+    valid = (column < clip_len[clip]) & (frame_mask[pl.ds(clip, 1), :] > 0)
+    row = jnp.where(valid, 0.0, NEG).astype(F32)
+    bias[...] = jnp.broadcast_to(row, (128, 1024)).T
+
+
+def text_bias_rows(text_len, text_mask):
+    slot = lax.broadcasted_iota(jnp.int32, (1, 128), 1)
+    rows = []
+    for clip in range(2):
+        valid = (slot < text_len[clip]) & ((text_mask[clip : clip + 1, :] > 0) | (slot == 0))
+        rows.append(jnp.where(valid, 0.0, NEG).astype(F32))
+    return rows
+
+
 def mask_scores(scores, bias_ref, first, rows):
     low = scores[first:] + bias_ref[first : first + rows, 0:1]
     key = lax.broadcasted_iota(jnp.int32, (rows, rows), 0)
@@ -775,7 +848,7 @@
         return 0
 
     lax.fori_loop(0, 4, head, 0)
-    live = first + lax.broadcasted_iota(jnp.int32, (ROWS, 256), 0) < length[0]
+    live = first + lax.broadcasted_iota(jnp.int32, (ROWS, 256), 0) < length
     o_ref[first:n, :] = jnp.where(live, out_t[...].T, 0).astype(BF16)
 
 
@@ -796,20 +869,28 @@
 
 
 def forward_body(
-    length, bias, text_bias, text, hid, cols_a, cols_b, square, fin, fout, grad,
+    clip_len, text_len, frame_mask, text_mask, gain, shift, self_qkv, cross_qkv, self_out, cross_out,
+    text, hid, fin, fout, grad,
     o_hid, o_first, o_q, o_k, o_v, o_heads, o_lse, o_w_a, o_w_b, o_params, o_att, o_tkv, o_square,
     o_second, o_query, o_crossed, o_self, o_cross, o_out, o_in, o_third, o_sum,
-    hid_all, first, q_ref, k_ref, v_ref, heads, lse, w_a, w_b, params, att, tkv, sq,
+    hid_all, first, q_ref, k_ref, v_ref, heads, lse, w_a, w_b, params, att, tkv, sq_self, sq_cross,
     second, query_ref, crossed, after_self, after_cross, out_ref, in_ref,
     out_t, v_t, own_tkv, own_text, own_hid, fin_in, grad_all, win, wout,
     tokens, inner, slope, g_pre, terms, slots, out_w, inbox, sums, near, far,
-    local, saved, send_sem, recv_sem,
+    bias, cols_a, cols_b, square, placed, local, saved, send_sem, recv_sem,
 ):
     h = Here()
     w = Wire(h, send_sem, recv_sem)
-    T_HID, T_A, T_B, T_FIN, T_AXY, T_BXY = 0, 10, 17, 24, 27, 33
-    T_Z, T_SXY, T_SIB, T_ATT, T_TKV = 39, 49, 73, 85, 93
-    T_WIN, T_GRAD, T_TOK, T_WOUT, T_TERM, T_OSIB, T_OZ = 96, 106, 112, 118, 128, 134, 138
+    length = clip_len[h.pair]
+    tag = [0]
+
+    def tags(n):
+        tag[0] += n
+        return tag[0] - n
+
+    T_HID, T_A, T_B, T_FIN, T_AXY, T_BXY = tags(10), tags(7), tags(7), tags(3), tags(6), tags(6)
+    T_SELF, T_CROSS, T_ATT, T_TKV, T_WIN, T_GRAD = tags(46), tags(46), tags(8), tags(3), tags(10), tags(6)
+    T_TOK, T_WOUT, T_TERM, T_OSIB, T_OZ = tags(6), tags(10), tags(6), tags(4), tags(5)
 
     def my_columns(f):
         return pl.ds(pl.multiple_of(lax.rem(f, 4) * 256, 256), 256)
@@ -817,6 +898,21 @@
     def fin_part(c):
         return fin.at[:, pl.ds(pl.multiple_of(c * 1024, 1024), 1024)]
 
+    spread = lax.broadcasted_iota(jnp.int32, (32, 128), 0) + 32 * lax.rem(h.f, 4)
+    spread = jnp.where(spread == lax.broadcasted_iota(jnp.int32, (32, 128), 1), 1.0, 0.0).astype(BF16)
+    placed[...] = jnp.zeros_like(placed)
+    placed[0:3, :] = dot(gain[...], spread, (1, 0))
+    placed[3:6, :] = dot(shift[...], spread, (1, 0))
+    for q in range(8):
+        group = placed[...] if q % 2 == 0 else jnp.zeros((16, 128), F32)
+        cols_a[96:112, 128 * q : 128 * q + 128] = group.astype(BF16)
+    for j in range(3):
+        cols_a[32 * j : 32 * j + 32, :] = self_qkv[j]
+    for j in range(2):
+        cols_b[32 * j : 32 * j + 32, :] = cross_qkv[1 + j]
+    square[0:32, :] = self_out[...]
+    square[32:64, :] = cross_qkv[0]
+    square[64:96, :] = cross_out[...]
     own = [
         pltpu.make_async_copy(src, dst, local.at[i])
         for i, (src, dst) in enumerate(
@@ -824,12 +920,13 @@
                 (cols_a.at[:, my_columns(h.f)], w_a.at[h.c, h.f]),
                 (cols_b.at[:, my_columns(h.f)], w_b.at[h.c, h.f]),
                 (hid.at[h.pair], hid_all.at[h.f]),
-                (square, sq.at[h.c, h.f]),
+                (square.at[pl.ds(0, 32)], sq_self.at[h.c, h.f]),
                 (fin_part(h.c), fin_in.at[h.c]),
                 (text, own_text),
                 (hid, own_hid),
                 (grad, grad_all.at[h.c]),
                 (fout, wout.at[h.f]),
+                (square.at[pl.ds(32, 64)], sq_cross.at[h.c, h.f]),
             )
         )
     ]
@@ -844,25 +941,24 @@
 
     greet(frame_others(h) + clip_others(h))
 
+    own[0].wait()
     for d in (2, 6, 4, 3, 5, 1, 7):
         f = h.step(d)
         w.send(cols_a.at[:, my_columns(f)], w_a.at[h.c, h.f], T_A + d - 1, h.c, f)
-
-    def square_gather(d):
-        f = h.zstep(d)
-        return ClipGather(
-            w,
-            lambda c, half: sq.at[c, f, pl.ds(48 * half, 48), :],
-            T_SXY + 6 * d,
-            (lambda half: square.at[pl.ds(48 * half, 48), :]) if d == 0 else None,
-        )
-
-    gathers = [square_gather(d) for d in range(4)]
-    gathers[0].begin()
+    own[7].wait()
+    grad_gather = ClipGather(w, lambda c, half: grad_all.at[c, pl.ds(128 * half, 128), :], T_GRAD)
+    grad_gather.begin()
+    for i, (c, f) in enumerate(clip_others(h)):
+        w.send(fin_part(c), fin_in.at[h.c], T_FIN + i, c, f)
+    w.send(hid.at[h.pair], hid_all.at[h.f], T_HID, h.c, h.sib)
 
     def half_of(ref, part):
         return ref.at[pl.ds(64 * part, 64), :]
 
+    for d in range(1, 8):
+        w.arrived(w_a.at[h.c, lax.rem(h.f + 8 - d, 8)], T_A + d - 1)
+    a_gather = ClipGather(w, lambda c, half: w_a.at[c, pl.ds(4 * half, 4)], T_AXY)
+    a_gather.begin()
     for part in range(2):
         w.send(
             half_of(hid.at[1 - h.pair], part),
@@ -872,14 +968,9 @@
             h.far_gate,
         )
         w.send(half_of(hid.at[h.pair], part), half_of(hid_all.at[h.f], part), T_HID + 1 + part, h.c, h.partner)
-    w.send(hid.at[h.pair], hid_all.at[h.f], T_HID, h.c, h.sib)
-    for i, (c, f) in enumerate(clip_others(h)):
-        w.send(fin_part(c), fin_in.at[h.c], T_FIN + i, c, f)
-    own[0].wait()
-    for d in range(1, 8):
-        w.arrived(w_a.at[h.c, lax.rem(h.f + 8 - d, 8)], T_A + d - 1)
-    a_gather = ClipGather(w, lambda c, half: w_a.at[c, pl.ds(4 * half, 4)], T_AXY)
-    a_gather.begin()
+    own[3].wait()
+    self_gather = MatrixGather(w, lambda c, f: sq_self.at[c, f], 32, T_SELF)
+    self_gather.step(1)
     forwards = []
     for part in range(2):
         for j in range(2):
@@ -888,27 +979,37 @@
             forward = w.copy(block, block, T_HID + 3 + 2 * j + part, h.c, h.partner)
             pl.when(h.is_gate)(forward.start)
             forwards.append(forward)
-    for d in (2, 6, 4, 3, 5, 1, 7):
-        f = h.step(d)
-        w.send(cols_b.at[:, my_columns(f)], w_b.at[h.c, h.f], T_B + d - 1, h.c, f)
+    self_gather.step(2)
+    a_gather.middle()
     for part in range(2):
         w.arrived(half_of(hid_all.at[h.partner], part), T_HID + 1 + part)
     w.send(hid_all.at[h.partner], hid_all.at[h.partner], T_HID + 7, h.c, h.sib)
     for j in range(2):
         w.send(hid_all.at[h.far[j]], hid_all.at[h.far[j]], T_HID + 8 + j, h.c, h.sib)
-    a_gather.middle()
-    own[3].wait()
-    z_gather = ZGather(w, lambda f: sq.at[h.c, f], T_Z)
-    z_gather.step(1)
-    z_gather.relay(0)
-    gathers[0].middle()
+    self_gather.step(3)
     own[1].wait()
-    for d in range(1, 8):
-        w.arrived(w_b.at[h.c, lax.rem(h.f + 8 - d, 8)], T_B + d - 1)
-    b_gather = ClipGather(w, lambda c, half: w_b.at[c, pl.ds(4 * half, 4)], T_BXY)
-    b_gather.begin()
+    for d in (2, 6, 4, 3, 5, 1, 7):
+        f = h.step(d)
+        w.send(cols_b.at[:, my_columns(f)], w_b.at[h.c, h.f], T_B + d - 1, h.c, f)
+    fill_key_bias(bias, clip_len, frame_mask, h.pair)
+    text_bias = text_bias_rows(text_len, text_mask)
+    self_gather.middle(0)
+    self_gather.step(4)
+    self_gather.middle(1)
+    own[9].wait()
+    cross_gather = MatrixGather(w, lambda c, f: sq_cross.at[c, f], 64, T_CROSS)
     a_gather.near()
     a_gather.end()
+    grad_gather.middle()
+    cross_gather.step(1)
+    own[4].wait()
+    for i, (c, f) in enumerate(clip_others(h)):
+        w.arrived(fin_in.at[c], T_FIN + i)
+    win_gather = ZGather(w, lambda f: win.at[:, f], T_WIN, fin_in)
+    win_copy = pltpu.make_async_copy(fin_in, win.at[:, h.f], local.at[11])
+    win_copy.start()
+    win_gather.step(1)
+    win_gather.relay(0)
     for g in range(8):
         group = sum(w_a[g // 2, 4 * (g % 2) + i, 96:104, 0:128].astype(F32) for i in range(4))
         params[:, 128 * g : 128 * g + 128] = group
@@ -917,7 +1018,6 @@
     w.arrived(hid_all.at[h.partner + h.sib - h.f], T_HID + 7)
     for j in range(2):
         w.arrived(hid_all.at[h.far[j] + h.sib - h.f], T_HID + 8 + j)
-    z_gather.step(2)
 
     def project_rows(i, _):
         at = pl.ds(pl.multiple_of(i * 256, 256), 256)
@@ -930,16 +1030,18 @@
         return 0
 
     lax.fori_loop(0, 2, project_rows, 0)
-    z_gather.step(3)
-    gathers[2].begin()
-    z_gather.relay(2)
-    b_gather.middle()
+    self_gather.middle(2)
+    for d in range(1, 8):
+        w.arrived(w_b.at[h.c, lax.rem(h.f + 8 - d, 8)], T_B + d - 1)
+    b_gather = ClipGather(w, lambda c, half: w_b.at[c, pl.ds(4 * half, 4)], T_BXY)
+    b_gather.begin()
+    cross_gather.step(2)
     lax.fori_loop(2, 4, project_rows, 0)
     v_t[...] = v_ref[...].T
-    z_gather.step(4)
-    for d in (1, 3):
-        gathers[d].begin()
-        z_gather.relay(d)
+    win_gather.step(2)
+    self_gather.middle(3)
+    cross_gather.step(3)
+    b_gather.middle()
 
     def att_slot(f):
         return att.at[lax.div(f, 4), :, my_columns(f)]
@@ -952,23 +1054,10 @@
             block = heads.at[pl.ds(128 * f, 128), :]
             away = h.f != f
             copy = w.copy(block, att_slot(h.f), T_ATT + h.f, h.c, f)
-            stay = pltpu.make_async_copy(block, att_slot(h.f), local.at[9])
+            stay = pltpu.make_async_copy(block, att_slot(h.f), local.at[12])
             pl.when(away)(copy.start)
             pl.when(jnp.logical_not(away))(stay.start)
             att_sends.append((away, copy, stay))
-
-    def square_steps(d):
-        f = h.zstep(d)
-        if d > 0:
-            gathers[d].middle()
-        gathers[d].near()
-        for i, c in enumerate((h.cx, h.cy)):
-            w.send(sq.at[c, f], sq.at[c, f], T_SIB + 3 * d + i, h.c, h.sib)
-
-    def square_last(d):
-        f = h.zstep(d)
-        gathers[d].end()
-        w.send(sq.at[h.cd, f], sq.at[h.cd, f], T_SIB + 3 * d + 2, h.c, h.sib)
 
     attend_and_send(3)
     def text_slot(f):
@@ -984,57 +1073,47 @@
     w.send(own_tkv, text_slot(h.f), T_TKV + 1, h.c, h.sib)
     text_copy = pltpu.make_async_copy(own_tkv, text_slot(h.f), local.at[10])
     text_copy.start()
-    square_steps(0)
-    square_last(0)
+    cross_gather.step(4)
+    win_gather.step(3)
+    cross_gather.middle(0)
     attend_and_send(2)
-    square_steps(2)
+    for d in range(4):
+        self_gather.near(d)
+        self_gather.last(d)
+    cross_gather.middle(1)
     w.arrived(text_slot(h.partner), T_TKV)
     w.send(text_slot(h.partner), text_slot(h.partner), T_TKV + 2, h.c, h.sib)
     attend_and_send(1)
-    square_last(2)
-    square_steps(1)
+    win_gather.step(4)
+    for d in range(1, 4):
+        win_gather.relay(d)
+    cross_gather.middle(2)
     attend_and_send(0)
-    own[4].wait()
-    for i, (c, f) in enumerate(clip_others(h)):
-        w.arrived(fin_in.at[c], T_FIN + i)
-    win_gather = ZGather(w, lambda f: win.at[:, f], T_WIN, fin_in)
-    win_copy = pltpu.make_async_copy(fin_in, win.at[:, h.f], local.at[11])
-    win_copy.start()
-    win_gather.step(1)
-    win_gather.relay(0)
-    square_steps(3)
-    square_last(1)
-    square_last(3)
-    own[7].wait()
-    grad_gather = ClipGather(w, lambda c, half: grad_all.at[c, pl.ds(128 * half, 128), :], T_GRAD)
-    grad_gather.begin()
+    cross_gather.middle(3)
     for src, dst in (
         (hid_all, o_hid), (first, o_first), (q_ref, o_q), (k_ref, o_k), (v_ref, o_v), (heads, o_heads), (lse, o_lse),
         (w_a, o_w_a), (w_b, o_w_b), (params, o_params),
     ):
         save(src, dst)
-    z_gather.end()
-    for d in range(4):
-        f = h.zstep(d) + h.sib - h.f
-        for i, c in enumerate((h.cx, h.cy, h.cd)):
-            w.arrived(sq.at[c, f], T_SIB + 3 * d + i)
+    self_gather.end()
     for d in range(1, 8):
         f = lax.rem(h.f + 8 - d, 8)
         w.arrived(att_slot(f), T_ATT + f)
     for away, _, stay in att_sends:
         pl.when(jnp.logical_not(away))(stay.wait)
-    win_gather.step(2)
 
     own[6].wait()
     value = own_hid[...].reshape(256, 1024).astype(F32) + dot(
-        att[...].reshape(256, 1024), square_of(sq, 0), (1, 0)
+        att[...].reshape(256, 1024), square_of(sq_self, 0), (1, 0)
     )
     after_self[...] = value
     xhat, _ = norm_parts(value)
     second[...] = (xhat * params[1:2, :] + params[4:5, :]).astype(BF16)
-    query_ref[...] = dot(second[...], square_of(sq, 1), (1, 0)).astype(BF16)
-    win_gather.step(3)
-    grad_gather.middle()
+    for d in range(4):
+        cross_gather.near(d)
+        cross_gather.last(d)
+    cross_gather.end()
+    query_ref[...] = dot(second[...], square_of(sq_cross, 0), (1, 0)).astype(BF16)
     w.arrived(text_slot(h.sib), T_TKV + 1)
     w.arrived(text_slot(h.partner + h.sib - h.f), T_TKV + 2)
     text_copy.wait()
@@ -1043,18 +1122,14 @@
         for group in range(4):
             rows, columns = pl.ds(128 * clip, 128), pl.ds(256 * group, 256)
             query = query_ref[rows, columns] * jnp.asarray(HD**-0.5, BF16)
-            probs, _ = text_probs(query, tkv[clip, 0, :, columns], text_bias[clip : clip + 1, :], lane_head)
+            probs, _ = text_probs(query, tkv[clip, 0, :, columns], text_bias[clip], lane_head)
             part = dot(probs.astype(BF16), tkv[clip, 1, :, columns], (1, 0))
             crossed[rows, columns] = pick_heads(part, lane_head).astype(BF16)
-        if clip == 0:
-            win_gather.step(4)
-            for d in range(1, 4):
-                win_gather.relay(d)
     own[8].wait()
     out_gather = ZGather(w, lambda f: wout.at[f], T_WOUT)
     out_gather.step(1)
     out_gather.relay(0)
-    value = after_self[...] + dot(crossed[...], square_of(sq, 2), (1, 0))
+    value = after_self[...] + dot(crossed[...], square_of(sq_cross, 1), (1, 0))
     after_cross[...] = value
     xhat, _ = norm_parts(value)
     tokens[h.c] = (xhat * params[2:3, :] + params[5:6, :]).astype(BF16)
@@ -1066,8 +1141,9 @@
         (after_self, o_self), (after_cross, o_cross),
     ):
         save(src, dst)
-    for which in range(3):
-        save(sq.at[:, :, pl.ds(32 * which, 32), :], o_square.at[which])
+    save(sq_self, o_square.at[0])
+    for which in range(2):
+        save(sq_cross.at[:, :, pl.ds(32 * which, 32), :], o_square.at[1 + which])
     win_copy.wait()
     win_gather.end()
 
@@ -1117,23 +1193,23 @@
         out_gather.relay(d)
     token_gather.end()
     hidden(h.cd)
+    lax.fori_loop(0, 4, out_weight, 0)
+    sibling.begin()
     out_gather.end()
     scatter = ClipScatter(
         w, lambda c, half: terms.at[c, pl.ds(128 * half, 128), :], [slots.at[i] for i in range(6)], T_TERM
     )
     hidden_back(h.cd)
     scatter.begin(0)
+    sibling.end()
+    z_scatter.begin()
     hidden_back(h.cx)
     hidden_back(h.cy)
     scatter.begin(1)
-    lax.fori_loop(0, 4, out_weight, 0)
-    sibling.begin()
+    hidden_back(h.c)
     scatter.middle()
-    hidden_back(h.c)
-    sibling.end()
-    z_scatter.begin()
+    z_scatter.step(1)
     lax.fori_loop(0, 2, in_weight, 0)
-    z_scatter.step(1)
     lax.fori_loop(2, 4, in_weight, 0)
     save(in_ref, o_in)
     out_terms(0)
@@ -1152,7 +1228,7 @@
         pl.when(h.is_gate)(copy.wait_send)
     for away, copy, _ in att_sends:
         pl.when(away)(copy.wait_send)
-    for one in (z_gather, win_gather, out_gather, z_scatter):
+    for one in (self_gather.z, cross_gather.z, win_gather, out_gather, z_scatter):
         one.drain()
     for copy in saves:
         copy.wait()
@@ -1183,11 +1259,12 @@
         shape((8, 128, 1024)),
     ]
     scratch = [pltpu.VMEM(one.shape, one.dtype) for one in kept]
+    scratch[12:13] = [pltpu.VMEM((4, 8, rows, 1024), BF16) for rows in (32, 64)]
     kept[12] = shape((3, 4, 8, 32, 1024))
     return comm_call(
         forward_body,
         tuple(kept) + (shape(rows, F32), shape((128, 1024), F32)),
-        [SMEM, VMEM, VMEM] + [HBM] * 8,
+        [SMEM] * 2 + [VMEM] * 8 + [HBM] * 5,
         (HBM,) * len(kept) + (VMEM,) * 2,
         scratch
         + [
@@ -1211,11 +1288,16 @@
             pltpu.VMEM(quarter, BF16),
             pltpu.VMEM((3, 128, 1024), BF16),
             pltpu.VMEM((2, 128, 1024), BF16),
-            pltpu.SemaphoreType.DMA((12,)),
+            pltpu.VMEM((1024, 128), F32),
+            pltpu.VMEM((112, 1024), BF16),
+            pltpu.VMEM((64, 1024), BF16),
+            pltpu.VMEM((96, 1024), BF16),
+            pltpu.VMEM((16, 128), F32),
+            pltpu.SemaphoreType.DMA((13,)),
             pltpu.SemaphoreType.DMA((24,)),
         ],
+        216,
         192,
-        144,
         1,
     )(*args)
 
@@ -1224,7 +1306,7 @@
     lane_head = lax.broadcasted_iota(jnp.int32, (ROWS, 256), 1) // HD
     first, n = i * ROWS, (i + 1) * ROWS
     q = q_ref[first:n, :] * jnp.asarray(HD**-0.5, BF16)
-    live = first + lax.broadcasted_iota(jnp.int32, (ROWS, 256), 0) < length[0]
+    live = first + lax.broadcasted_iota(jnp.int32, (ROWS, 256), 0) < length
     g = jnp.where(live, g_ref[first:n, :], 0)
     both = (g.astype(F32) * o_ref[first:n, :].astype(F32)).T
     row_dots = jnp.concatenate(
@@ -1263,7 +1345,7 @@
 
 
 def backward_body(
-    length, bias, text_bias, norms_in,
+    clip_len, text_len, frame_mask, text_mask, norms_in,
     h_third, h_out, h_cross, h_self, h_second, h_query, h_crossed, h_att, h_square, h_tkv, h_out_terms, h_in_terms,
     h_q, h_k, h_v, h_o, h_lse, h_hid, h_first, h_wa, h_wb, h_text, h_own,
     o_output, o_in, o_hidden, o_square, o_qkv, o_ckv, o_norm, o_text,
@@ -1275,10 +1357,11 @@
     g_heads, dq_t, k_t, dk, dv, d_cols, f_inbox, f_in,
     a_terms, a_slots, a_sum, a_in, b_terms, b_slots, b_sum, b_in,
     t_terms, tt_in, n_row, n_terms, n_slots, n_sum, n_in,
-    loaded, local, send_sem, recv_sem,
+    bias, loaded, local, send_sem, recv_sem,
 ):
     h = Here()
     w = Wire(h, send_sem, recv_sem)
+    length = clip_len[h.pair]
     tag = [0]
 
     def tags(n):
@@ -1356,6 +1439,8 @@
     def text_part(f):
         return g_text.at[lax.div(f, 4), :, :, columns_of(f)]
 
+    fill_key_bias(bias, clip_len, frame_mask, h.pair)
+    text_bias = text_bias_rows(text_len, text_mask)
     for copy in (l_third, l_cross, l_out):
         copy.wait()
     xhat, scale = norm_parts(after_cross[...])
@@ -1391,7 +1476,7 @@
             rows, columns = pl.ds(128 * clip, 128), pl.ds(256 * group, 256)
             keys, values = tkv[clip, 0, :, columns], tkv[clip, 1, :, columns]
             query = query_ref[rows, columns] * jnp.asarray(HD**-0.5, BF16)
-            probs, stacked = text_probs(query, keys, text_bias[clip : clip + 1, :], lane_head)
+            probs, stacked = text_probs(query, keys, text_bias[clip], lane_head)
             grads = g_crossed[rows, columns]
             g_stacked = jnp.concatenate([jnp.where(lane_head == j, grads, 0) for j in range(4)], axis=0)
             g_probs = dot(g_stacked, values, (1, 1))
@@ -1660,7 +1745,7 @@
             shape((16, 128), F32),
             shape((2, 16, 1024)),
         ),
-        [SMEM] + [VMEM] * 3 + [HBM] * 23,
+        [SMEM] * 2 + [VMEM] * 3 + [HBM] * 23,
         (VMEM,) * 8,
         [
             full(256, 1024), buffer(2, 128, 1024), full(256, 1024), buffer(256, 1024), buffer(256, 1024),
@@ -1680,13 +1765,54 @@
             buffer(3, 4, 8, 32, 256), buffer(3, 6, 4, 32, 256), buffer(3, 8, 32, 256), buffer(3, 8, 32, 256),
             buffer(4, 8, 64, 256), buffer(6, 4, 64, 256), buffer(8, 64, 256), buffer(8, 64, 256),
             buffer(128, 1024), buffer(8, 16, 1024), full(16, 1024), buffer(4, 8, 16, 128), buffer(6, 4, 16, 128),
-            buffer(8, 16, 128), buffer(8, 16, 128),
+            buffer(8, 16, 128), buffer(8, 16, 128), full(1024, 128),
             pltpu.SemaphoreType.DMA((32,)),
             pltpu.SemaphoreType.DMA((1,)),
         ],
         208,
         160,
         2,
+    )(*args)
+
+
+def finish_body(*refs):
+    ins, outs = refs[:8], refs[8:]
+    output, hidden, text, qkv, square, ckv, fin, norm = ins
+    o_output, o_hidden, o_text, o_qkv, o_self_out, o_cross, o_cross_out, o_fin, o_gain, o_shift = outs
+    o_output[...] = output[...].reshape(2, 128, 1024)
+    o_hidden[...] = hidden[...]
+    o_text[...] = text[...]
+    o_fin[...] = fin[...]
+    o_qkv[...] = qkv[...]
+    o_self_out[...] = square[0:32, :]
+    o_cross[0] = square[32:64, :]
+    o_cross[1:3] = ckv[...]
+    o_cross_out[...] = square[64:96, :]
+    place = lax.rem(lax.axis_index("frame"), 4)
+    for row, out in ((0, o_gain), (3, o_shift)):
+        out[...] = sum(
+            jnp.where(place == i, norm[row : row + 3, 32 * i : 32 * i + 32], 0) for i in range(4)
+        )
+
+
+def finish(*args):
+    return pl.pallas_call(
+        finish_body,
+        out_shape=(
+            shape((2, 128, 1024)),
+            shape((2, 128, 1024)),
+            shape((2, 16, 1024)),
+            shape((3, 32, 1024), F32),
+            shape((32, 1024), F32),
+            shape((3, 32, 1024), F32),
+            shape((32, 1024), F32),
+            shape((32, 4096), F32),
+            shape((3, 32), F32),
+            shape((3, 32), F32),
+        ),
+        in_specs=[VMEM] * 8,
+        out_specs=(VMEM,) * 10,
+        compiler_params=pltpu.CompilerParams(vmem_limit_bytes=60 * 2**20),
     )(*args)
 
 
@@ -1707,49 +1833,33 @@
     text_len,
     text_mask,
 ):
-    frame = lax.axis_index("frame")
-    pair = frame // 4
-    norms = jnp.concatenate([ln_gain, ln_bias], axis=0)
-    placed = lax.dynamic_update_slice(jnp.zeros((16, 256), BF16), norms, (0, 32 * (frame % 4)))
-    cols_a = jnp.concatenate(
-        [jnp.moveaxis(self_qkv, 1, 0).reshape(96, 1024), jnp.tile(placed, (1, 4))], axis=0
-    )
-    cols_b = jnp.moveaxis(cross_qkv, 1, 0)[1:].reshape(64, 1024)
-    square_here = jnp.concatenate([self_out, cross_qkv[:, 0], cross_out], axis=0)
-    columns = jnp.arange(1024, dtype=jnp.int32)
-    my_len = lax.dynamic_slice_in_dim(clip_len, pair, 1, 0)
-    my_mask = lax.dynamic_slice_in_dim(frame_mask, pair, 1, 0)[0]
-    bias = jnp.where((columns < my_len) & (my_mask > 0), 0.0, NEG).astype(F32)
-    bias = jnp.broadcast_to(bias[:, None], (1024, 128))
-    slots = jnp.arange(128, dtype=jnp.int32)
-    text_ok = (slots[None] < text_len[:, None]) & ((text_mask > 0) | (slots[None] == 0))
-    text_bias = jnp.where(text_ok, 0.0, NEG).astype(F32)
     (
         hid_all, first_low, query, key, value, att_heads, lse, w_a, w_b, params, att, tkv, square,
         second, cross_query, crossed, after_self, after_cross, out_terms, in_terms, third_sum, grad_ffn_out,
     ) = forward(
-        my_len, bias, text_bias, text_states, hidden_in, cols_a, cols_b, square_here, ffn_in, ffn_out,
-        out_grad.reshape(256, 1024),
+        clip_len, text_len, frame_mask, text_mask, ln_gain, ln_bias, jnp.moveaxis(self_qkv, 1, 0),
+        jnp.moveaxis(cross_qkv, 1, 0), self_out, cross_out, text_states, hidden_in, ffn_in, ffn_out, out_grad.reshape(256, 1024),
     )
     output, grad_ffn_in, grad_hidden, square_sum, qkv_sum, ckv_sum, norm_sum, grad_text = backward(
-        my_len, bias, text_bias, params,
+        clip_len, text_len, frame_mask, text_mask, params,
         third_sum, out_grad, after_cross, after_self, second, cross_query, crossed, att, square, tkv,
-        out_terms, in_terms.reshape(8, 4, 32, 1024), query, key, value, att_heads, lse, hid_all.reshape(4, 8, 32, 1024),
-        first_low.reshape(4, 8, 32, 1024), w_a, w_b, text_states, hidden_in,
-    )
-    norm_sum = lax.dynamic_slice(norm_sum, (0, 32 * (frame % 4)), (6, 32))
+        out_terms, in_terms.reshape(8, 4, 32, 1024), query, key, value, att_heads, lse,
+        hid_all.reshape(4, 8, 32, 1024), first_low.reshape(4, 8, 32, 1024), w_a, w_b, text_states, hidden_in,
+    )
+    results = finish(output, grad_hidden, grad_text, qkv_sum, square_sum, ckv_sum, grad_ffn_in, norm_sum)
+    output, grad_hidden, grad_text, qkv, g_self_out, cross, g_cross_out, grad_ffn_in, gains, shifts = results
     return (
-        output.reshape(2, 128, 1024),
+        output,
         grad_hidden,
         grad_text,
-        jnp.moveaxis(qkv_sum, 0, 1),
-        square_sum[0:32],
-        jnp.stack([square_sum[32:64], ckv_sum[0], ckv_sum[1]], axis=1),
-        square_sum[64:96],
+        jnp.moveaxis(qkv, 0, 1),
+        g_self_out,
+        jnp.moveaxis(cross, 0, 1),
+        g_cross_out,
         grad_ffn_in,
         grad_ffn_out,
-        norm_sum[0:3],
-        norm_sum[3:6],
+        gains,
+        shifts,
     )
 
 

time: 299 us -> 273 us (0.913)
  local copies, waits for them, and re-layouts: 13.8 us -> 0.8 us
  other arithmetic: 7.36 us -> 0 us
  Pallas kernels: 272 us -> 267 us
    pallas_call x1, Pallas kernels: 164 us -> 157 us  [forward(): comm_call(forward_body, tuple(kept) + (shape(rows, F32), shape((128, 1024...]
    slice x3 -> x0, local copies, waits for them, and re-layouts: 3.91 us -> none  [the longest x1 1.76 us: on_device_fast(): square_sum[64:96]]
    concatenate x3 -> x0, other arithmetic: 3.89 us -> none  [the longest x1 1.63 us: on_device_fast(): jnp.concatenate([jnp.moveaxis(self_qkv, 1, 0).reshape(96, 1024), jnp.tile...]
    unnamed x19 -> x3, local copies, waits for them, and re-layouts: 4.58 us -> 0.8 us
    pallas_call x0 -> x1, Pallas kernels: none -> 3.3 us  [finish(): pl.pallas_call(finish_body, out_shape=(shape((2, 128, 1024)), shape((2, 1...]
where the time goes in v6:
time: 273 us; the launch traced here: 268 us
  Pallas kernels  267 us (98%)
    pallas_call x1, Pallas kernels, forward(): comm_call(forward_body, tuple(kept) + (shape(rows, F32), shape((128, 1024...  157 us
    pallas_call x1, Pallas kernels, backward(): comm_call(backward_body, (shape((256, 1024)), shape((32, 4096), F32), sha...  106 us

profile of v6, /device:TPU:0, one launch (start us, length us, event | category | flops | bytes accessed | tf_op | source)
XLA Modules:
  0.0 268.4 jit_solution(2418431670850838196)
XLA Ops:
  0.6 157.3 %shard_map.230 = (bf16[8,128,1024]{2,1,0:T(8,128)(2,1)}, bf16[1024,1024]{1,0:T(8,128)(2,1)}, bf16[1024,256]{1,0:T(8,128)(2,1)}, bf16[1024,256]{1,0:T(8,128)(2,1)...) custom-call(s32[2]{0:T(128)} %clip_len.3, ...), custom_call_target="tpu_custom_call" | custom-call | tf_op jit(solution)/shard_map/pallas_call | solution.py:1264
  158.0 106.1 %shard_map.231 = (bf16[256,1024]{1,0:T(8,128)(2,1)}, f32[32,4096]{1,0:T(8,128)}, bf16[2,128,1024]{2,1,0:T(8,128)(2,1)}, f32[96,1024]{1,0:T(8,128)}, f32[3,32,102...) custom-call(s32[2]{0:T(128)} %clip_len.3, s32[2]{0:T(128)} %text_len.3, ...), custom_call_target="tpu_custom_call" | custom-call | tf_op jit(solution)/shard_map/pallas_call | solution.py:1736
  264.1 0.0 copy-start
  264.1 3.3 %shard_map.232 = (bf16[2,128,1024]{2,1,0:T(8,128)(2,1)}, bf16[2,128,1024]{2,1,0:T(8,128)(2,1)}, bf16[2,16,1024]{2,1,0:T(8,128)(2,1)}, f32[3,32,1024]{2,1,0:T(8,1...) custom-call(bf16[256,1024]{1,0:T(8,128)(2,1)} %get-tuple-element.72., ...), custom_call_target="tpu_custom_call" | custom-call | tf_op jit(solution)/shard_map/pallas_call | solution.py:1799
  267.4 0.0 copy-done
  267.4 0.8 copy.27
Async XLA Ops:
  264.1 3.3 %copy-start = (f32[128,1024]{1,0:T(8,128)S(1)}, f32[128,1024]{1,0:T(8,128)}, u32[]{:S(2)}) copy-start(f32[128,1024]{1,0:T(8,128)} %get-tuple-element.110) | copy-start | bytes 1572868
